TPU v7x, 512 devices: a whole 4x8x8 slice. The times are simulated.
512 devices in a mesh: dp: 32 (over z, x), expert: 16 (over y, core).
Axes of the slice: x: 4, y: 8, z: 8, core: 2. Of those that a mesh axis runs over, the one named last changes fastest.
Arguments:
- tokens: bfloat16 [65536, 1024], P(('dp', 'expert')), may hold values from -6 to 6
- route_ids: int32 [65536, 8], P(('dp', 'expert')), may hold values from 0 to 127, as said below
- route_weights: float32 [65536, 8], P(('dp', 'expert')), may hold values from 0.05 to 1
- upstream: bfloat16 [65536, 1024], P(('dp', 'expert')), may hold values from -6 to 6
- w_gate: bfloat16 [16, 1024, 384], P('expert', 'dp'), may hold values from -0.1875 to 0.1875
- w_up: bfloat16 [16, 1024, 384], P('expert', 'dp'), may hold values from -0.1875 to 0.1875
- w_down: bfloat16 [16, 384, 1024], P('expert', 'dp'), may hold values from -0.3125 to 0.3125
Outputs:
- mixed: bfloat16 [65536, 1024], P(('dp', 'expert'))
- grad_tokens: bfloat16 [65536, 1024], P(('dp', 'expert'))
- grad_route: float32 [65536, 8], P(('dp', 'expert'))
- grad_gate: bfloat16 [16, 1024, 384], P('expert', 'dp')
- grad_up: bfloat16 [16, 1024, 384], P('expert', 'dp')
- grad_down: bfloat16 [16, 384, 1024], P('expert', 'dp')
Inputs may be any that keep to these rules, and one draw needn't show every extreme that they name: `route_ids`: the k-th id of every row lies in [k * 16, (k + 1) * 16). Among the rows of one device no id is named by more than 16 rows, and in each band of ids some id is named by exactly 16 of them.
All inputs are finite; a program needn't handle non-finite values.
Results may differ from a plain program's by a relative error of at most 0.023.
Values may be sent and summed in bfloat16 or wider, within the bound.
No kernel may reach another device: no remote copies, remote signals or barrier semaphores. Data moves between devices by JAX's collectives and lax.ppermute only.
A program may use at most 64 MiB of HBM per device.

v0:
```python
import jax
import jax.numpy as jnp
from jax import lax
from jax.sharding import PartitionSpec as P

TOP = 8
SLOT_CAP = 16


def expert_forward(rows, gate_mat, up_mat, down_mat):
    pre_gate = jnp.dot(rows, gate_mat, preferred_element_type=jnp.float32)
    pre_up = jnp.dot(rows, up_mat, preferred_element_type=jnp.float32)
    hidden = (jax.nn.silu(pre_gate) * pre_up).astype(jnp.bfloat16)
    outputs = jnp.dot(hidden, down_mat, preferred_element_type=jnp.float32).astype(jnp.bfloat16)
    return (outputs, pre_gate, pre_up, hidden)


def expert_backward(scaled, pre_gate, pre_up, gate_mat, up_mat, down_mat):
    grad_hidden = jnp.dot(scaled, down_mat.T, preferred_element_type=jnp.float32)
    sigma = jax.nn.sigmoid(pre_gate)
    grad_gate_pre = (grad_hidden * pre_up * sigma * (1.0 + pre_gate * (1.0 - sigma))).astype(
        jnp.bfloat16
    )
    grad_up_pre = (grad_hidden * jax.nn.silu(pre_gate)).astype(jnp.bfloat16)
    row_grads = (
        jnp.dot(grad_gate_pre, gate_mat.T, preferred_element_type=jnp.float32)
        + jnp.dot(grad_up_pre, up_mat.T, preferred_element_type=jnp.float32)
    ).astype(jnp.bfloat16)
    return (row_grads, grad_gate_pre, grad_up_pre)


def on_device(tokens, route_ids, route_weights, upstream, w_gate, w_up, w_down):
    flight = lax.axis_size("expert")
    width = tokens.shape[1]
    capacity = SLOT_CAP
    experts_axis = jnp.arange(flight, dtype=jnp.int32)
    live_route = route_ids < flight
    hits = route_ids[:, :, None] == experts_axis[None, None, :]
    named = jnp.any(hits, axis=1).astype(jnp.int32)
    slot_rank = jnp.cumsum(named, axis=0) - 1
    placed = (slot_rank.T[:, None, :] == jnp.arange(capacity, dtype=jnp.int32)[None, :, None]) & (
        named.T[:, None, :] > 0
    )
    weight_of = jnp.sum(jnp.where(hits, route_weights[:, :, None], 0.0), axis=1)
    picker = placed.astype(jnp.bfloat16)
    rows_sent = jnp.einsum(
        "jst,td->jsd", picker, tokens, preferred_element_type=jnp.float32
    ).astype(jnp.bfloat16)
    upstream_sent = jnp.einsum(
        "jst,td->jsd", picker, upstream, preferred_element_type=jnp.float32
    ).astype(jnp.bfloat16)
    weight_sent = jnp.sum(jnp.where(placed, weight_of.T[:, None, :], 0.0), axis=2)
    scaled_sent = (weight_sent[:, :, None] * upstream_sent.astype(jnp.float32)).astype(jnp.bfloat16)
    rows_recv, scaled_recv = (
        lax.all_to_all(rows_sent, "expert", split_axis=0, concat_axis=0, tiled=True),
        lax.all_to_all(scaled_sent, "expert", split_axis=0, concat_axis=0, tiled=True),
    )
    expert_rows = rows_recv.reshape(flight * capacity, width)
    scaled_rows = scaled_recv.reshape(flight * capacity, width)
    gate_full, up_full, down_full = (
        lax.all_gather(w_gate, "dp", axis=1, tiled=True),
        lax.all_gather(w_up, "dp", axis=1, tiled=True),
        lax.all_gather(w_down, "dp", axis=1, tiled=True),
    )
    gate_mat, up_mat, down_mat = (gate_full[0], up_full[0], down_full[0])
    outputs, pre_gate, pre_up, hidden = expert_forward(expert_rows, gate_mat, up_mat, down_mat)
    outputs_owned = outputs.reshape(flight, capacity, width)
    row_grads, grad_gate_pre, grad_up_pre = expert_backward(
        scaled_rows, pre_gate, pre_up, gate_mat, up_mat, down_mat
    )
    grads_owned = row_grads.reshape(flight, capacity, width)
    outputs_home, grads_home = (
        lax.all_to_all(outputs_owned, "expert", split_axis=0, concat_axis=0, tiled=True),
        lax.all_to_all(grads_owned, "expert", split_axis=0, concat_axis=0, tiled=True),
    )
    part_gate = jnp.einsum(
        "rd,rf->df", expert_rows, grad_gate_pre, preferred_element_type=jnp.float32
    )
    part_up = jnp.einsum("rd,rf->df", expert_rows, grad_up_pre, preferred_element_type=jnp.float32)
    part_down = jnp.einsum("rf,rd->fd", hidden, scaled_rows, preferred_element_type=jnp.float32)
    share_gate, share_up, share_down = (
        lax.psum_scatter(
            part_gate[None].astype(jnp.bfloat16), "dp", scatter_dimension=1, tiled=True
        ).astype(jnp.float32),
        lax.psum_scatter(
            part_up[None].astype(jnp.bfloat16), "dp", scatter_dimension=1, tiled=True
        ).astype(jnp.float32),
        lax.psum_scatter(
            part_down[None].astype(jnp.bfloat16), "dp", scatter_dimension=1, tiled=True
        ).astype(jnp.float32),
    )
    flat_out = outputs_home.reshape(flight * capacity, width)
    flat_grads = grads_home.reshape(flight * capacity, width)
    clipped = jnp.clip(route_ids, 0, flight - 1)
    slot = jnp.take_along_axis(slot_rank, clipped, axis=1)
    upstream_wide = upstream.astype(jnp.float32)
    mixed = jnp.zeros((tokens.shape[0], width), jnp.float32)
    grad_sum = jnp.zeros((tokens.shape[0], width), jnp.float32)
    route_columns = []
    for column in range(TOP):
        alive = live_route[:, column]
        index = jnp.where(alive, clipped[:, column] * capacity + slot[:, column], 0)
        picked = jnp.take(flat_out, index, axis=0).astype(jnp.float32)
        gate_weight = jnp.where(alive, route_weights[:, column], 0.0)
        mixed = mixed + gate_weight[:, None] * picked
        route_columns.append(jnp.where(alive, jnp.sum(upstream_wide * picked, axis=1), 0.0))
        grad_rows = jnp.take(flat_grads, index, axis=0).astype(jnp.float32)
        grad_sum = grad_sum + jnp.where(alive[:, None], grad_rows, 0.0)
    grad_route = jnp.stack(route_columns, axis=1)
    return (
        mixed.astype(jnp.bfloat16),
        grad_sum.astype(jnp.bfloat16),
        grad_route,
        share_gate.astype(jnp.bfloat16),
        share_up.astype(jnp.bfloat16),
        share_down.astype(jnp.bfloat16),
    )


def solution(mesh):
    return jax.shard_map(
        on_device,
        mesh=mesh,
        in_specs=(
            P(("dp", "expert"), None),
            P(("dp", "expert"), None),
            P(("dp", "expert"), None),
            P(("dp", "expert"), None),
            P("expert", "dp", None),
            P("expert", "dp", None),
            P("expert", "dp", None),
        ),
        out_specs=(
            P(("dp", "expert"), None),
            P(("dp", "expert"), None),
            P(("dp", "expert"), None),
            P("expert", "dp", None),
            P("expert", "dp", None),
            P("expert", "dp", None),
        ),
        check_vma=False,
    )
```

profile of v0, /device:TPU:7, one launch (start us, length us, event | category | flops | bytes accessed | tf_op | source)
XLA Modules:
  0.0 650.5 jit_solution(17828731346154300516)
XLA Ops:
  9.4 7.8 %all-to-all-start = ((bf16[16,16,1024]{2,1,0:T(8,128)(2,1)}), bf16[16,16,1024]{2,1,0:T(8,128)(2,1)S(1)}, u32[]{:S(2)}, u32[]{:S(2)}) async-start(bf16[16,16,1024]{2,1,0:T(8,128)(2,1)} %convolution_convert_fusion.5), calls=%async_computation | async-start | bytes 1048576 | tf_op jit(solution)/shard_map/all_to_all | solution.py:55
  17.4 44.8 %all_gather.10 = bf16[1,1024,384]{2,1,0:T(8,128)(2,1)S(1)} all-gather(bf16[1,32,384]{2,1,0:T(8,128)(2,1)S(1)} %copy-done.17), channel_id=1, replica_groups=mesh['dp'=32,'expert'=16] {'dp'}, dimensions={1}, use_global_device_ids=true | all-gather | bytes 811008 | tf_op jit(solution)/shard_map/all_gather | solution.py:62
  62.4 7.1 %gather_fusion = s32[1024]{0:T(1024)S(1)} fusion(s32[128,16]{1,0:T(8,128)S(1)} %get-tuple-element.72, s32[1024]{0:T(1024)S(1)} %reshape.221), kind=kCustom, calls=%fused_computation.16 | custom fusion | bytes 16384 | tf_op jit(solution)/shard_map/jit(take_along_axis)/gather | solution.py:95
  71.7 35.1 %all_gather.9 = bf16[1,1024,384]{2,1,0:T(8,128)(2,1)S(1)} all-gather(bf16[1,32,384]{2,1,0:T(8,128)(2,1)S(1)} %copy-done.18), channel_id=1, replica_groups=mesh['dp'=32,'expert'=16] {'dp'}, dimensions={1}, use_global_device_ids=true | all-gather | bytes 811008 | tf_op jit(solution)/shard_map/all_gather | solution.py:61
  106.8 42.7 %all_gather.11 = bf16[1,384,1024]{2,0,1:T(2,128)(2,1)} all-gather(bf16[1,12,1024]{2,0,1:T(2,128)(2,1)S(1)} %copy.130), channel_id=1, replica_groups=mesh['dp'=32,'expert'=16] {'dp'}, dimensions={1}, use_global_device_ids=true | all-gather | bytes 811008 | tf_op jit(solution)/shard_map/all_gather | solution.py:63
  151.2 41.4 %all-to-all-start.2 = ((bf16[16,16,1024]{2,1,0:T(8,128)(2,1)}), bf16[16,16,1024]{2,1,0:T(8,128)(2,1)S(1)}, u32[]{:S(2)}, u32[]{:S(2)}) async-start(bf16[16,16,1024]{2,1,0:T(8,128)(2,1)} %fusion.7), calls=%async_computation.2 | async-start | bytes 1048576 | tf_op jit(solution)/shard_map/all_to_all | solution.py:56
  196.3 13.7 %all-to-all-done.2 = bf16[16,16,1024]{2,1,0:T(8,128)(2,1)S(1)} async-done(((bf16[16,16,1024]{2,1,0:T(8,128)(2,1)}), bf16[16,16,1024]{2,1,0:T(8,128)(2,1)S(1)}, u32[]{:S(2)}, u32[]{:S(2)}) %all-to-all-start.2) | async-done | bytes 524320 | tf_op jit(solution)/shard_map/all_to_all | solution.py:56
  210.0 2.8 multiply_convert_fusion
  226.9 1.9 select_reduce_fusion.9
  228.8 2.7 convolution_convert_fusion.3
  231.6 3.5 all-to-all-start.1
  235.2 2.3 fusion.2
  240.2 11.5 %all-to-all-done.1 = bf16[16,16,1024]{2,1,0:T(8,128)(2,1)S(1)} async-done(((bf16[16,16,1024]{2,1,0:T(8,128)(2,1)}), bf16[16,16,1024]{2,1,0:T(8,128)(2,1)S(1)}, u32[]{:S(2)}, u32[]{:S(2)}) %all-to-all-start.1) | async-done | bytes 524320 | tf_op jit(solution)/shard_map/all_to_all | solution.py:73
  251.7 3.5 all-to-all-start.3
  255.6 61.9 %fusion = bf16[16,1024]{1,0:T(8,128)(2,1)S(1)} fusion(bf16[1,384,1024]{2,1,0:T(8,128)(2,1)S(1)} %fusion.3), kind=kCustom, calls=%all-reduce-scatter | all-reduce-scatter fusion | flops 524289 | bytes 821248
  317.6 2.7 collective-permute-start
  320.3 1.9 collective-permute-start.1
  322.2 4.7 collective-permute-start.7
  326.9 5.8 collective-permute-start.2
  332.7 1.6 collective-permute-start.3
  334.4 4.3 collective-permute-start.4
  338.7 2.2 collective-permute-start.5
  340.9 3.3 collective-permute-start.6
  356.4 1.7 gather_fusion.12
  359.0 1.7 gather_fusion.13
  361.7 1.7 gather_fusion.14
  364.4 1.7 gather_fusion.15
  367.1 1.8 gather_fusion.16
  382.5 2.2 fusion.25
  384.8 2.3 add_convert_fusion
  387.1 33.7 %reduce-scatter.6.cloned.1.call-done = bf16[1,32,384]{2,1,0:T(8,128)(2,1)} async-done(((bf16[1,1024,384]{2,1,0:T(8,128)(2,1)}), bf16[1,32,384]{2,1,0:T(8,128)(2,1)}) %reduce-scatter.6.cloned.1.call-update) | async-done | bytes 24592 | tf_op jit(solution)/shard_map/reduce_scatter | solution.py:82
  420.7 222.9 %reduce-scatter.8.cloned.1.call-done = bf16[1,32,384]{2,1,0:T(8,128)(2,1)} async-done(((bf16[1,1024,384]{2,1,0:T(8,128)(2,1)}), bf16[1,32,384]{2,1,0:T(8,128)(2,1)}) %reduce-scatter.8.cloned.1.call-update) | async-done | bytes 24592 | tf_op jit(solution)/shard_map/reduce_scatter | solution.py:85
  (176 shorter events, 56.2 us)
Async XLA Ops:
  9.4 141.8 %all-to-all-start = ((bf16[16,16,1024]{2,1,0:T(8,128)(2,1)}), bf16[16,16,1024]{2,1,0:T(8,128)(2,1)S(1)}, u32[]{:S(2)}, u32[]{:S(2)}) async-start(bf16[16,16,1024]{2,1,0:T(8,128)(2,1)} %convolution_convert_fusion.5), calls=%async_computation | async-start | bytes 1048576 | tf_op jit(solution)/shard_map/all_to_all | solution.py:55
  70.5 79.0 %copy-start.32 = (pred[128]{0:T(512)(128)(4,1)}, pred[128]{0:T(512)(128)(4,1)S(1)}, u32[]{:S(2)}) copy-start(pred[128]{0:T(512)(128)(4,1)S(1)} %get-tuple-element.35) | copy-start | bytes 388
  70.5 79.0 %copy-start.37 = (pred[128]{0:T(512)(128)(4,1)}, pred[128]{0:T(512)(128)(4,1)S(1)}, u32[]{:S(2)}) copy-start(pred[128]{0:T(512)(128)(4,1)S(1)} %get-tuple-element.42) | copy-start | bytes 388
  70.5 122.2 %copy-start.35 = (pred[128]{0:T(512)(128)(4,1)}, pred[128]{0:T(512)(128)(4,1)S(1)}, u32[]{:S(2)}) copy-start(pred[128]{0:T(512)(128)(4,1)S(1)} %get-tuple-element.40) | copy-start | bytes 388
  70.5 122.2 %copy-start.36 = (pred[128]{0:T(512)(128)(4,1)}, pred[128]{0:T(512)(128)(4,1)S(1)}, u32[]{:S(2)}) copy-start(pred[128]{0:T(512)(128)(4,1)S(1)} %get-tuple-element.41) | copy-start | bytes 388
  70.7 79.4 %copy-start.1 = (bf16[128,1024]{1,0:T(8,128)(2,1)S(1)}, bf16[128,1024]{1,0:T(8,128)(2,1)}, u32[]{:S(2)}) copy-start(bf16[128,1024]{1,0:T(8,128)(2,1)} %param.12) | copy-start | bytes 786436
  151.2 58.8 %all-to-all-start.2 = ((bf16[16,16,1024]{2,1,0:T(8,128)(2,1)}), bf16[16,16,1024]{2,1,0:T(8,128)(2,1)S(1)}, u32[]{:S(2)}, u32[]{:S(2)}) async-start(bf16[16,16,1024]{2,1,0:T(8,128)(2,1)} %fusion.7), calls=%async_computation.2 | async-start | bytes 1048576 | tf_op jit(solution)/shard_map/all_to_all | solution.py:56
  192.6 228.1 %reduce-scatter.6.cloned.1.call-start = ((), (), s32[]{:S(2)}) async-start(), calls=%async_computation.6 | async-start | bytes 811008 | tf_op jit(solution)/shard_map/reduce_scatter | solution.py:82
  212.7 16.1 %copy-start.12 = (bf16[256,384]{1,0:T(8,128)(2,1)}, bf16[256,384]{1,0:T(8,128)(2,1)S(1)}, u32[]{:S(2)}) copy-start(bf16[256,384]{1,0:T(8,128)(2,1)S(1)} %get-tuple-element.69) | copy-start | bytes 589828
  212.7 18.8 %copy-start.14 = (bf16[256,384]{1,0:T(8,128)(2,1)}, bf16[256,384]{1,0:T(8,128)(2,1)S(1)}, u32[]{:S(2)}) copy-start(bf16[256,384]{1,0:T(8,128)(2,1)S(1)} %get-tuple-element.68) | copy-start | bytes 589828
  231.6 20.2 %all-to-all-start.1 = ((bf16[16,16,1024]{2,1,0:T(8,128)(2,1)}), bf16[16,16,1024]{2,1,0:T(8,128)(2,1)S(1)}, u32[]{:S(2)}, u32[]{:S(2)}) async-start(bf16[16,16,1024]{2,1,0:T(8,128)(2,1)} %bitcast.94), calls=%async_computation.1 | async-start | bytes 1048576 | tf_op jit(solution)/shard_map/all_to_all | solution.py:73
  235.0 408.6 %reduce-scatter.8.cloned.1.call-start = ((), (), s32[]{:S(2)}) async-start(), calls=%async_computation.7 | async-start | bytes 811008 | tf_op jit(solution)/shard_map/reduce_scatter | solution.py:85
  235.2 133.8 %copy-start.30 = (pred[128]{0:T(512)(128)(4,1)}, pred[128]{0:T(512)(128)(4,1)S(1)}, u32[]{:S(2)}) copy-start(pred[128]{0:T(512)(128)(4,1)S(1)} %get-tuple-element.63) | copy-start | bytes 388
  235.2 133.8 %copy-start.31 = (pred[128]{0:T(512)(128)(4,1)}, pred[128]{0:T(512)(128)(4,1)S(1)}, u32[]{:S(2)}) copy-start(pred[128]{0:T(512)(128)(4,1)S(1)} %get-tuple-element.98) | copy-start | bytes 388
  239.0 16.3 %copy-start.13 = (bf16[256,384]{1,0:T(8,128)(2,1)S(1)}, bf16[256,384]{1,0:T(8,128)(2,1)}, u32[]{:S(2)}) copy-start(bf16[256,384]{1,0:T(8,128)(2,1)} %copy-done.12) | copy-start | bytes 589828
  251.7 98.0 %all-to-all-start.3 = ((bf16[16,16,1024]{2,1,0:T(8,128)(2,1)}), bf16[16,16,1024]{2,1,0:T(8,128)(2,1)S(1)}, u32[]{:S(2)}, u32[]{:S(2)}) async-start(bf16[16,16,1024]{2,1,0:T(8,128)(2,1)} %bitcast.12), calls=%async_computation.3 | async-start | bytes 1048576 | tf_op jit(solution)/shard_map/all_to_all | solution.py:74
  317.6 21.1 %collective-permute-start = (bf16[16,1024]{1,0:T(8,128)(2,1)S(1)}, bf16[16,1024]{1,0:T(8,128)(2,1)S(1)}, u32[]{:S(2)}, u32[]{:S(2)}) collective-permute-start(bf16[16,1024]{1,0:T(8,128)(2,1)S(1)} %fusion), channel_id=1, source_target_pairs={{0,16},{16,32},{32,48},{48,64},{64,80},{80,96},{96,112},{112,128},... | collective-permute-start | bytes 98312
  320.3 20.6 %collective-permute-start.1 = (bf16[16,1024]{1,0:T(8,128)(2,1)S(1)}, bf16[16,1024]{1,0:T(8,128)(2,1)S(1)}, u32[]{:S(2)}, u32[]{:S(2)}) collective-permute-start(bf16[16,1024]{1,0:T(8,128)(2,1)S(1)} %fusion), channel_id=1, source_target_pairs={{0,32},{16,48},{32,64},{48,80},{64,96},{80,112},{96,128},{112,144}... | collective-permute-start | bytes 98312
  322.2 12.1 %collective-permute-start.7 = (bf16[12,1024]{1,0:T(8,128)(2,1)S(1)}, bf16[12,1024]{1,0:T(8,128)(2,1)S(1)}, u32[]{:S(2)}, u32[]{:S(2)}) collective-permute-start(bf16[12,1024]{1,0:T(8,128)(2,1)S(1)} %slice.186), channel_id=1, source_target_pairs={{0,128},{16,144},{32,160},{48,176},{64,192},{80,208},{96,224},{112... | collective-permute-start | bytes 73736
  326.9 19.3 %collective-permute-start.2 = (bf16[16,1024]{1,0:T(8,128)(2,1)S(1)}, bf16[16,1024]{1,0:T(8,128)(2,1)S(1)}, u32[]{:S(2)}, u32[]{:S(2)}) collective-permute-start(bf16[16,1024]{1,0:T(8,128)(2,1)S(1)} %fusion), channel_id=1, source_target_pairs={{0,48},{16,64},{32,80},{48,96},{64,112},{80,128},{96,144},{112,160... | collective-permute-start | bytes 98312
  332.7 13.5 %collective-permute-start.3 = (bf16[16,1024]{1,0:T(8,128)(2,1)S(1)}, bf16[16,1024]{1,0:T(8,128)(2,1)S(1)}, u32[]{:S(2)}, u32[]{:S(2)}) collective-permute-start(bf16[16,1024]{1,0:T(8,128)(2,1)S(1)} %fusion), channel_id=1, source_target_pairs={{0,64},{16,80},{32,96},{48,112},{64,128},{80,144},{96,160},{112,17... | collective-permute-start | bytes 98312
  334.4 11.9 %collective-permute-start.4 = (bf16[16,1024]{1,0:T(8,128)(2,1)S(1)}, bf16[16,1024]{1,0:T(8,128)(2,1)S(1)}, u32[]{:S(2)}, u32[]{:S(2)}) collective-permute-start(bf16[16,1024]{1,0:T(8,128)(2,1)S(1)} %fusion), channel_id=1, source_target_pairs={{0,80},{16,96},{32,112},{48,128},{64,144},{80,160},{96,176},{112,1... | collective-permute-start | bytes 98312
  338.7 7.6 %collective-permute-start.5 = (bf16[16,1024]{1,0:T(8,128)(2,1)S(1)}, bf16[16,1024]{1,0:T(8,128)(2,1)S(1)}, u32[]{:S(2)}, u32[]{:S(2)}) collective-permute-start(bf16[16,1024]{1,0:T(8,128)(2,1)S(1)} %fusion), channel_id=1, source_target_pairs={{0,96},{16,112},{32,128},{48,144},{64,160},{80,176},{96,192},{112,... | collective-permute-start | bytes 98312
  340.9 5.3 collective-permute-start.6
  371.6 13.0 %copy-start.3 = (bf16[128,1024]{1,0:T(8,128)(2,1)S(1)}, bf16[128,1024]{1,0:T(8,128)(2,1)}, u32[]{:S(2)}) copy-start(bf16[128,1024]{1,0:T(8,128)(2,1)} %gather_fusion.9) | copy-start | bytes 786436
  371.6 13.0 %copy-start.4 = (bf16[128,1024]{1,0:T(8,128)(2,1)S(1)}, bf16[128,1024]{1,0:T(8,128)(2,1)}, u32[]{:S(2)}) copy-start(bf16[128,1024]{1,0:T(8,128)(2,1)} %gather_fusion.10) | copy-start | bytes 786436
  371.6 13.0 %copy-start.5 = (bf16[128,1024]{1,0:T(8,128)(2,1)S(1)}, bf16[128,1024]{1,0:T(8,128)(2,1)}, u32[]{:S(2)}) copy-start(bf16[128,1024]{1,0:T(8,128)(2,1)} %gather_fusion.11) | copy-start | bytes 786436
  371.6 13.0 %copy-start.6 = (bf16[128,1024]{1,0:T(8,128)(2,1)S(1)}, bf16[128,1024]{1,0:T(8,128)(2,1)}, u32[]{:S(2)}) copy-start(bf16[128,1024]{1,0:T(8,128)(2,1)} %gather_fusion.12) | copy-start | bytes 786436
  371.7 13.0 %copy-start.21 = (pred[128]{0:T(512)(128)(4,1)S(1)}, pred[128]{0:T(512)(128)(4,1)}, u32[]{:S(2)}) copy-start(pred[128]{0:T(512)(128)(4,1)} %get-tuple-element.51) | copy-start | bytes 388
  371.7 13.0 %copy-start.23 = (pred[128]{0:T(512)(128)(4,1)S(1)}, pred[128]{0:T(512)(128)(4,1)}, u32[]{:S(2)}) copy-start(pred[128]{0:T(512)(128)(4,1)} %get-tuple-element.92) | copy-start | bytes 388
  371.7 13.0 %copy-start.25 = (pred[128]{0:T(512)(128)(4,1)S(1)}, pred[128]{0:T(512)(128)(4,1)}, u32[]{:S(2)}) copy-start(pred[128]{0:T(512)(128)(4,1)} %get-tuple-element.55) | copy-start | bytes 388
  371.7 13.0 %copy-start.27 = (pred[128]{0:T(512)(128)(4,1)S(1)}, pred[128]{0:T(512)(128)(4,1)}, u32[]{:S(2)}) copy-start(pred[128]{0:T(512)(128)(4,1)} %get-tuple-element.94) | copy-start | bytes 388
  (23 other events, 97.3 us)
Sparse Core Ops, SparseCore 0:
  214.3 206.4 reduce-scatter.5
  425.7 217.9 reduce-scatter.7
where the time goes:
time: 658 us; the launch traced here: 651 us
  waiting for transfers between devices  282 us (43%)
  blocking collectives  185 us (28%)
  starting transfers between devices  82.8 us (13%)
  local copies, waits for them, and re-layouts  51.4 us (8%)
  other arithmetic  17.6 us (3%)
  matrix products  16.8 us (3%)
  between operations  15.5 us (2%)
    reduce_scatter x1, waiting for transfers between devices, on_device(): lax.psum_scatter(part_up[None].astype(jnp.bfloat16), 'dp', scatter_dimens...  223 us
    unnamed x1, blocking collectives  61.9 us
    all_gather x1, blocking collectives, on_device(): lax.all_gather(w_up, 'dp', axis=1, tiled=True)  44.8 us
    all_gather x1, blocking collectives, on_device(): lax.all_gather(w_down, 'dp', axis=1, tiled=True)  42.7 us
    all_to_all x1, starting transfers between devices, on_device(): lax.all_to_all(scaled_sent, 'expert', split_axis=0, concat_axis=0, tiled=...  41.4 us
    all_gather x1, blocking collectives, on_device(): lax.all_gather(w_gate, 'dp', axis=1, tiled=True)  35.1 us
    reduce_scatter x1, waiting for transfers between devices, on_device(): lax.psum_scatter(part_gate[None].astype(jnp.bfloat16), 'dp', scatter_dime...  33.7 us
    unnamed x8, starting transfers between devices  26.6 us
  transfers between devices with their start and end apart: 14, of which 4 were waited for; matrix products, arithmetic and copies ran while one was open for 22% of the time, Pallas kernels for 0%

commit v1 on v0

v1 whole, which is shorter than its diff:
```python
import functools

import jax
import jax.numpy as jnp
from jax import lax
from jax.experimental import pallas as pl
from jax.experimental.pallas import tpu as pltpu
from jax.sharding import PartitionSpec as P

FLIGHT = 16
CAP = 16
NZ = 8
NX = 4
TOK = 128
D = 1024
FF = 384
ROWS = FLIGHT * CAP
FD = FF // (NZ * NX)
SH = D // (NZ * NX)
PW = 2 * FF + D // 2
BF = jnp.bfloat16
F32 = jnp.float32
MIB = 1 << 20


def dot(a, b, dims):
    return lax.dot_general(a, b, (dims, ((), ())), preferred_element_type=F32)


def nn(a, b):
    return dot(a, b, ((1,), (0,)))


def tn(a, b):
    return dot(a, b, ((0,), (0,)))


def nt(a, b):
    return dot(a, b, ((1,), (1,)))


def route_rows(ids_t, weights_t):
    live = ids_t < FLIGHT
    expert = jnp.sum(jnp.where(live, ids_t, 0), axis=0, keepdims=True)
    weight = jnp.sum(jnp.where(live, weights_t, 0.0), axis=0, keepdims=True)
    alive = jnp.max(live.astype(jnp.int32), axis=0, keepdims=True) > 0
    return live, expert, weight, alive


def place(ids_t, weights_t):
    live, expert, weight, alive = route_rows(ids_t, weights_t)
    named = (lax.broadcasted_iota(jnp.int32, (FLIGHT, TOK), 0) == expert) & alive
    before = lax.broadcasted_iota(jnp.int32, (TOK, TOK), 0) < lax.broadcasted_iota(
        jnp.int32, (TOK, TOK), 1
    )
    rank = nn(named.astype(F32).astype(BF), before.astype(F32).astype(BF))
    slot = jnp.sum(jnp.where(named, rank, 0.0), axis=0, keepdims=True).astype(jnp.int32)
    row = jnp.where(alive, expert * CAP + slot, -1)
    mask = lax.broadcasted_iota(jnp.int32, (ROWS, TOK), 0) == row
    return live, weight, mask


def column_of(row):
    eye = lax.broadcasted_iota(jnp.int32, (TOK, TOK), 0) == lax.broadcasted_iota(
        jnp.int32, (TOK, TOK), 1
    )
    return jnp.sum(jnp.where(eye, row, 0.0), axis=1, keepdims=True)


def row_of(column):
    eye = lax.broadcasted_iota(jnp.int32, (TOK, TOK), 0) == lax.broadcasted_iota(
        jnp.int32, (TOK, TOK), 1
    )
    return jnp.sum(jnp.where(eye, column, 0.0), axis=0, keepdims=True)


def pack_kernel(gate_ref, up_ref, down_ref, out_ref):
    out_ref[:, :FF] = gate_ref[...]
    out_ref[:, FF : 2 * FF] = up_ref[...]
    down = jnp.concatenate(
        [down_ref[...].astype(F32), jnp.zeros((16 - FD, D), F32)], axis=0
    ).astype(BF)
    out_ref[:16, 2 * FF :] = down[:, : D // 2]
    out_ref[16:, 2 * FF :] = down[:, D // 2 :]


def dispatch_kernel(ids_ref, weights_ref, tokens_ref, upstream_ref, out_ref):
    live, weight, mask = place(ids_ref[...], weights_ref[...])
    picker = mask.astype(F32).astype(BF)
    out_ref[:, :D] = nn(picker, tokens_ref[...]).astype(BF)
    row_weight = jnp.sum(jnp.where(mask, weight, 0.0), axis=1, keepdims=True)
    out_ref[:, D:] = (row_weight * nn(picker, upstream_ref[...])).astype(BF)


def expert_kernel(
    recv_ref,
    b0_ref,
    b1_ref,
    b2_ref,
    b3_ref,
    sent_ref,
    q0_ref,
    q1_ref,
    q2_ref,
    q3_ref,
    full,
    grads,
):
    place_dp = lax.axis_index("dp")
    z, x = place_dp // NX, place_dp % NX
    for k, block in enumerate((b0_ref, b1_ref, b2_ref, b3_ref)):
        x_from = lax.rem(x + (NX - k), NX)
        for d in range(NZ):
            z_from = lax.rem(z + (NZ - d), NZ)
            start = pl.multiple_of((z_from * NX + x_from) * SH, SH)
            full[pl.ds(start, SH), :] = block[d * SH : (d + 1) * SH, :]
    gate, up = full[:, :FF], full[:, FF : 2 * FF]
    column = lax.broadcasted_iota(jnp.int32, (FF, 16 * NZ * NX), 1)
    of_row = (column // 16) * FD + column % 16
    unpad = ((lax.broadcasted_iota(jnp.int32, (FF, 16 * NZ * NX), 0) == of_row) & (column % 16 < FD)).astype(F32).astype(BF)
    packed = full[:, 2 * FF :].reshape(NZ * NX, 2, 16, D // 2)
    left = nn(unpad, packed[:, 0].reshape(16 * NZ * NX, D // 2)).astype(BF)
    right = nn(unpad, packed[:, 1].reshape(16 * NZ * NX, D // 2)).astype(BF)
    down = jnp.concatenate([left, right], axis=1)
    rows, scaled = recv_ref[:, :D], recv_ref[:, D:]
    pre_gate = nn(rows, gate)
    pre_up = nn(rows, up)
    grad_hidden = nt(scaled, down)
    sigma = jax.nn.sigmoid(pre_gate)
    silu = pre_gate * sigma
    hidden = (silu * pre_up).astype(BF)
    sent_ref[:, :D] = nn(hidden, down).astype(BF)
    grad_gate_pre = (grad_hidden * pre_up * sigma * (1.0 + pre_gate * (1.0 - sigma))).astype(BF)
    grad_up_pre = (grad_hidden * silu).astype(BF)
    sent_ref[:, D:] = (nt(grad_gate_pre, gate) + nt(grad_up_pre, up)).astype(BF)
    grads[:, :FF] = tn(rows, grad_gate_pre).astype(BF)
    grads[:, FF : 2 * FF] = tn(rows, grad_up_pre).astype(BF)
    hidden_padded = nn(hidden, unpad).astype(BF)
    part_down = tn(hidden_padded, scaled).astype(BF)
    halves = jnp.stack(
        [
            part_down[:, : D // 2].reshape(NZ * NX, 16, D // 2),
            part_down[:, D // 2 :].reshape(NZ * NX, 16, D // 2),
        ],
        axis=1,
    )
    grads[:, 2 * FF :] = halves.reshape(D, D // 2)
    for k, quarter in enumerate((q0_ref, q1_ref, q2_ref, q3_ref)):
        x_to = lax.rem(x + k, NX)
        for i in range(NZ):
            start = pl.multiple_of((i * NX + x_to) * SH, SH)
            quarter[i * SH : (i + 1) * SH, :] = grads[pl.ds(start, SH), :]


def sum_x_kernel(a_ref, b_ref, c_ref, d_ref, *out_refs):
    z = lax.axis_index("dp") // NX
    for d, out in enumerate(out_refs):
        start = pl.multiple_of(lax.rem(z + d, NZ) * SH, SH)
        here = pl.ds(start, SH)
        total = a_ref[here, :].astype(F32) + b_ref[here, :].astype(F32)
        total = total + c_ref[here, :].astype(F32) + d_ref[here, :].astype(F32)
        out[...] = total.astype(BF)


def sum_z_kernel(*refs):
    parts, (gate_ref, up_ref, down_ref) = refs[:NZ], refs[NZ:]
    total = parts[0][...].astype(F32)
    for part in parts[1:]:
        total = total + part[...].astype(F32)
    gate_ref[...] = total[:, :FF].astype(BF)
    up_ref[...] = total[:, FF : 2 * FF].astype(BF)
    down_ref[:, : D // 2] = total[:FD, 2 * FF :].astype(BF)
    down_ref[:, D // 2 :] = total[16 : 16 + FD, 2 * FF :].astype(BF)


def combine_kernel(ids_ref, weights_ref, upstream_ref, home_ref, mixed_ref, tokens_ref, route_ref):
    live, weight, mask = place(ids_ref[...], weights_ref[...])
    picker = mask.astype(F32).astype(BF)
    tokens_ref[...] = tn(picker, home_ref[:, D:]).astype(BF)
    picked = tn(picker, home_ref[:, :D])
    mixed_ref[...] = (column_of(weight) * picked).astype(BF)
    inner = jnp.sum(upstream_ref[...].astype(F32) * picked, axis=1, keepdims=True)
    route_ref[...] = jnp.where(live, row_of(inner), 0.0)


def call(kernel, outs, scratch=(), vmem=None, flops=0, moved=1 * MIB):
    shapes = [jax.ShapeDtypeStruct(s, t) for s, t in outs]
    single = len(shapes) == 1
    return pl.pallas_call(
        kernel,
        out_shape=shapes[0] if single else shapes,
        scratch_shapes=list(scratch),
        compiler_params=pltpu.CompilerParams(vmem_limit_bytes=vmem or 16 * MIB),
        cost_estimate=pl.CostEstimate(flops=flops, bytes_accessed=moved, transcendentals=0),
    )


def shift_z(v, d):
    pairs = [(z * NX + x, ((z + d) % NZ) * NX + x) for z in range(NZ) for x in range(NX)]
    return lax.ppermute(v, "dp", pairs)


def shift_x(v, k):
    pairs = [(z * NX + x, z * NX + (x + k) % NX) for z in range(NZ) for x in range(NX)]
    return lax.ppermute(v, "dp", pairs)


def exchange(v):
    v = v.reshape(FLIGHT, CAP, 2 * D)
    return lax.all_to_all(v, "expert", split_axis=0, concat_axis=0, tiled=True).reshape(ROWS, 2 * D)


def on_device(tokens, route_ids, route_weights, upstream, w_gate, w_up, w_down):
    ids_t, weights_t = route_ids.T, route_weights.T
    shard = call(pack_kernel, [((SH, PW), BF)])(w_gate[0], w_up[0], w_down[0])
    block = jnp.concatenate([shard] + [shift_z(shard, d) for d in range(1, NZ)], axis=0)
    sent = call(dispatch_kernel, [((ROWS, 2 * D), BF)], flops=4 * ROWS * TOK * D)(
        ids_t, weights_t, tokens, upstream
    )
    recv = exchange(sent)
    blocks = [block] + [shift_x(block, k) for k in range(1, NX)]
    quarter = ((NZ * SH, PW), BF)
    back, *quarters = call(
        expert_kernel,
        [((ROWS, 2 * D), BF)] + [quarter] * NX,
        scratch=[pltpu.VMEM((D, PW), BF), pltpu.VMEM((D, PW), BF)],
        vmem=40 * MIB,
        flops=18 * ROWS * D * FF,
        moved=8 * MIB,
    )(recv, *blocks)
    home = exchange(back)
    arrived = [quarters[0]] + [shift_x(quarters[k], k) for k in range(1, NX)]
    slices = call(sum_x_kernel, [((SH, PW), BF)] * NZ, moved=4 * MIB)(*arrived)
    parts = [slices[0]] + [shift_z(slices[d], d) for d in range(1, NZ)]
    grad_gate, grad_up, grad_down = call(
        sum_z_kernel, [((SH, FF), BF), ((SH, FF), BF), ((FD, D), BF)]
    )(*parts)
    mixed, grad_tokens, grad_route = call(
        combine_kernel,
        [((TOK, D), BF), ((TOK, D), BF), ((8, TOK), F32)],
        flops=4 * ROWS * TOK * D,
        moved=2 * MIB,
    )(ids_t, weights_t, upstream, home)
    return (mixed, grad_tokens, grad_route.T, grad_gate[None], grad_up[None], grad_down[None])


def solution(mesh):
    rows, held = P(("dp", "expert"), None), P("expert", "dp", None)
    return jax.shard_map(
        on_device,
        mesh=mesh,
        in_specs=(rows, rows, rows, rows, held, held, held),
        out_specs=(rows, rows, rows, held, held, held),
        check_vma=False,
    )
```

time: 658 us -> 188 us (0.29)
  waiting for transfers between devices: 282 us -> 77.1 us
  blocking collectives: 185 us -> 0 us
  local copies, waits for them, and re-layouts: 51.4 us -> 12 us
  other arithmetic: 17.6 us -> 0 us
  matrix products: 16.8 us -> 0 us
  between operations: 15.5 us -> 0.99 us
  Pallas kernels: 0 us -> 8.61 us
    reduce_scatter x2 -> x0, waiting for transfers between devices: 257 us -> none  [the longest x1 223 us: on_device(): lax.psum_scatter(part_up[None].astype(jnp.bfloat16), 'dp', scatter_dimens...]
    all_gather x3 -> x0, blocking collectives: 123 us -> none  [the longest x1 44.8 us: on_device(): lax.all_gather(w_up, 'dp', axis=1, tiled=True)]
    ppermute x0 -> x20, waiting for transfers between devices: none -> 77.1 us  [the longest x6 54.3 us: shift_x(): return lax.ppermute(v, 'dp', pairs)]
    ppermute x0 -> x20, starting transfers between devices: none -> 69.6 us  [the longest x14 52 us: shift_z(): return lax.ppermute(v, 'dp', pairs)]
    unnamed x1 -> x0, blocking collectives: 61.9 us -> none
    all_to_all x4 -> x2, starting transfers between devices: 56.2 us -> 18.3 us  [exchange(): lax.all_to_all(v, 'expert', split_axis=0, concat_axis=0, tiled=True)]
    gather x19 -> x0, local copies, waits for them, and re-layouts: 28 us -> none  [the longest x8 13.3 us: on_device(): grad_rows = jnp.take(flat_grads, index, axis=0).astype(jnp.float32)]
    unnamed x8 -> x0, starting transfers between devices: 26.6 us -> none
  transfers between devices with their start and end apart: 14 -> 22, of which waited for: 4 -> 9; matrix products, arithmetic and copies ran while one was open for 22% -> 0% of each run, Pallas kernels for 0% -> 1%
where the time goes in v1:
time: 188 us; the launch traced here: 187 us
  starting transfers between devices  87.9 us (47%)
  waiting for transfers between devices  77.1 us (41%)
  local copies, waits for them, and re-layouts  12 us (6%)
  Pallas kernels  8.61 us (5%)
    ppermute x6, waiting for transfers between devices, shift_x(): return lax.ppermute(v, 'dp', pairs)  54.3 us
    ppermute x14, starting transfers between devices, shift_z(): return lax.ppermute(v, 'dp', pairs)  52 us
    ppermute x14, waiting for transfers between devices, shift_z(): return lax.ppermute(v, 'dp', pairs)  22.7 us
    all_to_all x2, starting transfers between devices, exchange(): lax.all_to_all(v, 'expert', split_axis=0, concat_axis=0, tiled=True)  18.3 us
    ppermute x6, starting transfers between devices, shift_x(): return lax.ppermute(v, 'dp', pairs)  17.6 us
    unnamed x41, local copies, waits for them, and re-layouts  12 us
    pallas_call x1, Pallas kernels, on_device(): call(expert_kernel, [((ROWS, 2 * D), BF)] + [quarter] * NX, scratch=[pltp...  4.74 us
  transfers between devices with their start and end apart: 22, of which 9 were waited for; matrix products, arithmetic and copies ran while one was open for 0% of the time, Pallas kernels for 1%

profile of v1, /device:TPU:7, one launch (start us, length us, event | category | flops | bytes accessed | tf_op | source)
XLA Modules:
  0.0 186.5 jit_solution(13497966117806229464)
XLA Ops:
  2.9 10.8 %collective-permute-start.6 = (bf16[32,1280]{1,0:T(8,128)(2,1)S(1)}, bf16[32,1280]{1,0:T(8,128)(2,1)S(1)}, u32[]{:S(2)}, u32[]{:S(2)}) collective-permute-start(bf16[32,1280]{1,0:T(8,128)(2,1)S(1)} %shard_map.119), channel_id=1, source_target_pairs={{0,448},{16,464},{32,480},{48,496},{64,0},{80,16},{96,32},{112,48}... | collective-permute-start | bytes 245768 | tf_op jit(solution)/shard_map/ppermute | solution.py:200
  13.7 2.2 %collective-permute-start.5 = (bf16[32,1280]{1,0:T(8,128)(2,1)S(1)}, bf16[32,1280]{1,0:T(8,128)(2,1)S(1)}, u32[]{:S(2)}, u32[]{:S(2)}) collective-permute-start(bf16[32,1280]{1,0:T(8,128)(2,1)S(1)} %shard_map.119), channel_id=1, source_target_pairs={{0,384},{16,400},{32,416},{48,432},{64,448},{80,464},{96,480},{112... | collective-permute-start | bytes 245768 | tf_op jit(solution)/shard_map/ppermute | solution.py:200
  15.9 1.9 %collective-permute-start.4 = (bf16[32,1280]{1,0:T(8,128)(2,1)S(1)}, bf16[32,1280]{1,0:T(8,128)(2,1)S(1)}, u32[]{:S(2)}, u32[]{:S(2)}) collective-permute-start(bf16[32,1280]{1,0:T(8,128)(2,1)S(1)} %shard_map.119), channel_id=1, source_target_pairs={{0,320},{16,336},{32,352},{48,368},{64,384},{80,400},{96,416},{112... | collective-permute-start | bytes 245768 | tf_op jit(solution)/shard_map/ppermute | solution.py:200
  17.8 7.3 %collective-permute-start.3 = (bf16[32,1280]{1,0:T(8,128)(2,1)S(1)}, bf16[32,1280]{1,0:T(8,128)(2,1)S(1)}, u32[]{:S(2)}, u32[]{:S(2)}) collective-permute-start(bf16[32,1280]{1,0:T(8,128)(2,1)S(1)} %shard_map.119), channel_id=1, source_target_pairs={{0,256},{16,272},{32,288},{48,304},{64,320},{80,336},{96,352},{112... | collective-permute-start | bytes 245768 | tf_op jit(solution)/shard_map/ppermute | solution.py:200
  25.1 3.1 %collective-permute-start = (bf16[32,1280]{1,0:T(8,128)(2,1)S(1)}, bf16[32,1280]{1,0:T(8,128)(2,1)S(1)}, u32[]{:S(2)}, u32[]{:S(2)}) collective-permute-start(bf16[32,1280]{1,0:T(8,128)(2,1)S(1)} %shard_map.119), channel_id=1, source_target_pairs={{0,64},{16,80},{32,96},{48,112},{64,128},{80,144},{96,160},{112,17... | collective-permute-start | bytes 245768 | tf_op jit(solution)/shard_map/ppermute | solution.py:200
  31.7 9.2 %all-to-all-start = ((bf16[16,16,2048]{2,1,0:T(8,128)(2,1)}), bf16[16,16,2048]{2,1,0:T(8,128)(2,1)S(1)}, u32[]{:S(2)}, u32[]{:S(2)}) async-start(bf16[16,16,2048]{2,1,0:T(8,128)(2,1)} %bitcast.2), calls=%async_computation | async-start | bytes 2097152 | tf_op jit(solution)/shard_map/all_to_all | solution.py:210
  40.9 1.9 %collective-permute-start.1 = (bf16[32,1280]{1,0:T(8,128)(2,1)S(1)}, bf16[32,1280]{1,0:T(8,128)(2,1)S(1)}, u32[]{:S(2)}, u32[]{:S(2)}) collective-permute-start(bf16[32,1280]{1,0:T(8,128)(2,1)S(1)} %shard_map.119), channel_id=1, source_target_pairs={{0,128},{16,144},{32,160},{48,176},{64,192},{80,208},{96,224},{112... | collective-permute-start | bytes 245768 | tf_op jit(solution)/shard_map/ppermute | solution.py:200
  42.8 8.1 %collective-permute-done.1 = bf16[32,1280]{1,0:T(8,128)(2,1)S(1)} collective-permute-done((bf16[32,1280]{1,0:T(8,128)(2,1)S(1)}, bf16[32,1280]{1,0:T(8,128)(2,1)S(1)}, u32[]{:S(2)}, u32[]{:S(2)}) %collective-permute-start.1) | collective-permute-done | bytes 81952 | tf_op jit(solution)/shard_map/ppermute | solution.py:200
  50.9 1.9 %collective-permute-start.2 = (bf16[32,1280]{1,0:T(8,128)(2,1)S(1)}, bf16[32,1280]{1,0:T(8,128)(2,1)S(1)}, u32[]{:S(2)}, u32[]{:S(2)}) collective-permute-start(bf16[32,1280]{1,0:T(8,128)(2,1)S(1)} %shard_map.119), channel_id=1, source_target_pairs={{0,192},{16,208},{32,224},{48,240},{64,256},{80,272},{96,288},{112... | collective-permute-start | bytes 245768 | tf_op jit(solution)/shard_map/ppermute | solution.py:200
  52.8 7.7 %collective-permute-done.2 = bf16[32,1280]{1,0:T(8,128)(2,1)S(1)} collective-permute-done((bf16[32,1280]{1,0:T(8,128)(2,1)S(1)}, bf16[32,1280]{1,0:T(8,128)(2,1)S(1)}, u32[]{:S(2)}, u32[]{:S(2)}) %collective-permute-start.2) | collective-permute-done | bytes 81952 | tf_op jit(solution)/shard_map/ppermute | solution.py:200
  60.6 2.5 %collective-permute-start.9 = (bf16[256,1280]{1,0:T(8,128)(2,1)S(1)}, bf16[256,1280]{1,0:T(8,128)(2,1)S(1)}, u32[]{:S(2)}, u32[]{:S(2)}) collective-permute-start(bf16[256,1280]{1,0:T(8,128)(2,1)S(1)} %constant_dynamic-update-slice_fusion.b0_ref), channel_id=1, source_target_pairs={{0,48},{16,0},{32,16},{48,32},{64,112},{80,64},{96,80},{112,96},{1... | collective-permute-start | bytes 1966088 | tf_op jit(solution)/shard_map/ppermute | solution.py:205
  63.1 2.7 %collective-permute-start.8 = (bf16[256,1280]{1,0:T(8,128)(2,1)S(1)}, bf16[256,1280]{1,0:T(8,128)(2,1)S(1)}, u32[]{:S(2)}, u32[]{:S(2)}) collective-permute-start(bf16[256,1280]{1,0:T(8,128)(2,1)S(1)} %constant_dynamic-update-slice_fusion.b0_ref), channel_id=1, source_target_pairs={{0,32},{16,48},{32,0},{48,16},{64,96},{80,112},{96,64},{112,80},{1... | collective-permute-start | bytes 1966088 | tf_op jit(solution)/shard_map/ppermute | solution.py:205
  65.8 3.7 %collective-permute-start.7 = (bf16[256,1280]{1,0:T(8,128)(2,1)S(1)}, bf16[256,1280]{1,0:T(8,128)(2,1)S(1)}, u32[]{:S(2)}, u32[]{:S(2)}) collective-permute-start(bf16[256,1280]{1,0:T(8,128)(2,1)S(1)} %constant_dynamic-update-slice_fusion.b0_ref), channel_id=1, source_target_pairs={{0,16},{16,32},{32,48},{48,0},{64,80},{80,96},{96,112},{112,64},{1... | collective-permute-start | bytes 1966088 | tf_op jit(solution)/shard_map/ppermute | solution.py:205
  69.5 10.9 %collective-permute-done.9.b3_ref = bf16[256,1280]{1,0:T(8,128)(2,1)S(1)} collective-permute-done((bf16[256,1280]{1,0:T(8,128)(2,1)S(1)}, bf16[256,1280]{1,0:T(8,128)(2,1)S(1)}, u32[]{:S(2)}, u32[]{:S(2)}) %collective-permute-start.9) | collective-permute-done | bytes 655392 | tf_op jit(solution)/shard_map/ppermute | solution.py:205
  81.2 10.7 %collective-permute-done.8.b2_ref = bf16[256,1280]{1,0:T(8,128)(2,1)S(1)} collective-permute-done((bf16[256,1280]{1,0:T(8,128)(2,1)S(1)}, bf16[256,1280]{1,0:T(8,128)(2,1)S(1)}, u32[]{:S(2)}, u32[]{:S(2)}) %collective-permute-start.8) | collective-permute-done | bytes 655392 | tf_op jit(solution)/shard_map/ppermute | solution.py:205
  92.8 3.1 %collective-permute-done.7.b1_ref = bf16[256,1280]{1,0:T(8,128)(2,1)S(1)} collective-permute-done((bf16[256,1280]{1,0:T(8,128)(2,1)S(1)}, bf16[256,1280]{1,0:T(8,128)(2,1)S(1)}, u32[]{:S(2)}, u32[]{:S(2)}) %collective-permute-start.7) | collective-permute-done | bytes 655392 | tf_op jit(solution)/shard_map/ppermute | solution.py:205
  100.0 4.7 %shard_map.120 = (bf16[256,2048]{1,0:T(8,128)(2,1)}, bf16[256,1280]{1,0:T(8,128)(2,1)S(1)}, bf16[256,1280]{1,0:T(8,128)(2,1)S(1)}, bf16[256,1280]{1,0:T(8,128)(2,1)S(1)}, bf16[256,1280]{1,0:T(8,128)(2,1)S(1)}) custom-call(bf16[256,2048]{1,0:T(8,128)(2,1)S(1)} %bitcast.14, bf16[256,1280]{1,0:T(8,128)(2,1)S(1)} %constant_dynamic-update-slice_fusion.b0_ref, ...), custom_call_target="tpu_custom_call" | custom-call | flops 1811939328 | bytes 8388608 | tf_op jit(solution)/shard_map/pallas_call | solution.py:223
  106.5 9.1 %all-to-all-start.1 = ((bf16[16,16,2048]{2,1,0:T(8,128)(2,1)}), bf16[16,16,2048]{2,1,0:T(8,128)(2,1)S(1)}, u32[]{:S(2)}, u32[]{:S(2)}) async-start(bf16[16,16,2048]{2,1,0:T(8,128)(2,1)} %bitcast.7), calls=%async_computation.1 | async-start | bytes 2097152 | tf_op jit(solution)/shard_map/all_to_all | solution.py:210
  115.6 4.3 %collective-permute-start.10 = (bf16[256,1280]{1,0:T(8,128)(2,1)}, bf16[256,1280]{1,0:T(8,128)(2,1)S(1)}, u32[]{:S(2)}, u32[]{:S(2)}) collective-permute-start(bf16[256,1280]{1,0:T(8,128)(2,1)} %copy-done.14), channel_id=1, source_target_pairs={{0,16},{16,32},{32,48},{48,0},{64,80},{80,96},{96,112},{112,64},{1... | collective-permute-start | bytes 1966088 | tf_op jit(solution)/shard_map/ppermute | solution.py:205
  119.9 1.9 %collective-permute-start.11 = (bf16[256,1280]{1,0:T(8,128)(2,1)S(1)}, bf16[256,1280]{1,0:T(8,128)(2,1)S(1)}, u32[]{:S(2)}, u32[]{:S(2)}) collective-permute-start(bf16[256,1280]{1,0:T(8,128)(2,1)S(1)} %copy-done.11), channel_id=1, source_target_pairs={{0,32},{16,48},{32,0},{48,16},{64,96},{80,112},{96,64},{112,80},{1... | collective-permute-start | bytes 1966088 | tf_op jit(solution)/shard_map/ppermute | solution.py:205
  121.8 2.5 %collective-permute-start.12 = (bf16[256,1280]{1,0:T(8,128)(2,1)S(1)}, bf16[256,1280]{1,0:T(8,128)(2,1)S(1)}, u32[]{:S(2)}, u32[]{:S(2)}) collective-permute-start(bf16[256,1280]{1,0:T(8,128)(2,1)S(1)} %get-tuple-element.32), channel_id=1, source_target_pairs={{0,48},{16,0},{32,16},{48,32},{64,112},{80,64},{96,80},{112,96},{1... | collective-permute-start | bytes 1966088 | tf_op jit(solution)/shard_map/ppermute | solution.py:205
  124.3 23.8 %collective-permute-done.10.b_ref = bf16[256,1280]{1,0:T(8,128)(2,1)S(1)} collective-permute-done((bf16[256,1280]{1,0:T(8,128)(2,1)}, bf16[256,1280]{1,0:T(8,128)(2,1)S(1)}, u32[]{:S(2)}, u32[]{:S(2)}) %collective-permute-start.10) | collective-permute-done | bytes 655392 | tf_op jit(solution)/shard_map/ppermute | solution.py:205
  148.1 5.8 %collective-permute-done.12.d_ref = bf16[256,1280]{1,0:T(8,128)(2,1)S(1)} collective-permute-done((bf16[256,1280]{1,0:T(8,128)(2,1)S(1)}, bf16[256,1280]{1,0:T(8,128)(2,1)S(1)}, u32[]{:S(2)}, u32[]{:S(2)}) %collective-permute-start.12) | collective-permute-done | bytes 655392 | tf_op jit(solution)/shard_map/ppermute | solution.py:205
  154.3 1.9 %collective-permute-start.13 = (bf16[32,1280]{1,0:T(8,128)(2,1)S(1)}, bf16[32,1280]{1,0:T(8,128)(2,1)S(1)}, u32[]{:S(2)}, u32[]{:S(2)}) collective-permute-start(bf16[32,1280]{1,0:T(8,128)(2,1)S(1)} %get-tuple-element.34), channel_id=1, source_target_pairs={{0,64},{16,80},{32,96},{48,112},{64,128},{80,144},{96,160},{112,17... | collective-permute-start | bytes 245768 | tf_op jit(solution)/shard_map/ppermute | solution.py:200
  156.2 2.2 %collective-permute-start.14 = (bf16[32,1280]{1,0:T(8,128)(2,1)S(1)}, bf16[32,1280]{1,0:T(8,128)(2,1)S(1)}, u32[]{:S(2)}, u32[]{:S(2)}) collective-permute-start(bf16[32,1280]{1,0:T(8,128)(2,1)S(1)} %get-tuple-element.35), channel_id=1, source_target_pairs={{0,128},{16,144},{32,160},{48,176},{64,192},{80,208},{96,224},{112... | collective-permute-start | bytes 245768 | tf_op jit(solution)/shard_map/ppermute | solution.py:200
  158.4 4.8 %collective-permute-start.15 = (bf16[32,1280]{1,0:T(8,128)(2,1)S(1)}, bf16[32,1280]{1,0:T(8,128)(2,1)S(1)}, u32[]{:S(2)}, u32[]{:S(2)}) collective-permute-start(bf16[32,1280]{1,0:T(8,128)(2,1)S(1)} %get-tuple-element.36), channel_id=1, source_target_pairs={{0,192},{16,208},{32,224},{48,240},{64,256},{80,272},{96,288},{112... | collective-permute-start | bytes 245768 | tf_op jit(solution)/shard_map/ppermute | solution.py:200
  163.2 4.4 %collective-permute-start.16 = (bf16[32,1280]{1,0:T(8,128)(2,1)S(1)}, bf16[32,1280]{1,0:T(8,128)(2,1)S(1)}, u32[]{:S(2)}, u32[]{:S(2)}) collective-permute-start(bf16[32,1280]{1,0:T(8,128)(2,1)S(1)} %get-tuple-element.37), channel_id=1, source_target_pairs={{0,256},{16,272},{32,288},{48,304},{64,320},{80,336},{96,352},{112... | collective-permute-start | bytes 245768 | tf_op jit(solution)/shard_map/ppermute | solution.py:200
  167.6 3.6 %collective-permute-start.17 = (bf16[32,1280]{1,0:T(8,128)(2,1)S(1)}, bf16[32,1280]{1,0:T(8,128)(2,1)S(1)}, u32[]{:S(2)}, u32[]{:S(2)}) collective-permute-start(bf16[32,1280]{1,0:T(8,128)(2,1)S(1)} %get-tuple-element.38), channel_id=1, source_target_pairs={{0,320},{16,336},{32,352},{48,368},{64,384},{80,400},{96,416},{112... | collective-permute-start | bytes 245768 | tf_op jit(solution)/shard_map/ppermute | solution.py:200
  171.2 3.8 %collective-permute-start.18 = (bf16[32,1280]{1,0:T(8,128)(2,1)S(1)}, bf16[32,1280]{1,0:T(8,128)(2,1)S(1)}, u32[]{:S(2)}, u32[]{:S(2)}) collective-permute-start(bf16[32,1280]{1,0:T(8,128)(2,1)S(1)} %get-tuple-element.39), channel_id=1, source_target_pairs={{0,384},{16,400},{32,416},{48,432},{64,448},{80,464},{96,480},{112... | collective-permute-start | bytes 245768 | tf_op jit(solution)/shard_map/ppermute | solution.py:200
  175.0 2.2 %collective-permute-start.19 = (bf16[32,1280]{1,0:T(8,128)(2,1)S(1)}, bf16[32,1280]{1,0:T(8,128)(2,1)S(1)}, u32[]{:S(2)}, u32[]{:S(2)}) collective-permute-start(bf16[32,1280]{1,0:T(8,128)(2,1)S(1)} %get-tuple-element.40), channel_id=1, source_target_pairs={{0,448},{16,464},{32,480},{48,496},{64,0},{80,16},{96,32},{112,48}... | collective-permute-start | bytes 245768 | tf_op jit(solution)/shard_map/ppermute | solution.py:200
  177.3 4.2 %collective-permute-done.18.refs_6_ = bf16[32,1280]{1,0:T(8,128)(2,1)S(1)} collective-permute-done((bf16[32,1280]{1,0:T(8,128)(2,1)S(1)}, bf16[32,1280]{1,0:T(8,128)(2,1)S(1)}, u32[]{:S(2)}, u32[]{:S(2)}) %collective-permute-start.18) | collective-permute-done | bytes 81952 | tf_op jit(solution)/shard_map/ppermute | solution.py:200
  181.5 2.8 %collective-permute-done.19.refs_7_ = bf16[32,1280]{1,0:T(8,128)(2,1)S(1)} collective-permute-done((bf16[32,1280]{1,0:T(8,128)(2,1)S(1)}, bf16[32,1280]{1,0:T(8,128)(2,1)S(1)}, u32[]{:S(2)}, u32[]{:S(2)}) %collective-permute-start.19) | collective-permute-done | bytes 81952 | tf_op jit(solution)/shard_map/ppermute | solution.py:200
  (60 shorter events, 15.9 us)
Async XLA Ops:
  2.9 25.3 %copy-start.6 = (s32[128,8]{0,1:T(8,128)S(1)}, s32[128,8]{0,1:T(8,128)}, u32[]{:S(2)}) copy-start(s32[128,8]{0,1:T(8,128)} %param.8) | copy-start | bytes 12292
  2.9 25.3 %copy-start.7 = (f32[128,8]{0,1:T(8,128)S(1)}, f32[128,8]{0,1:T(8,128)}, u32[]{:S(2)}) copy-start(f32[128,8]{0,1:T(8,128)} %param.9) | copy-start | bytes 12292
  2.9 57.7 %collective-permute-start.6 = (bf16[32,1280]{1,0:T(8,128)(2,1)S(1)}, bf16[32,1280]{1,0:T(8,128)(2,1)S(1)}, u32[]{:S(2)}, u32[]{:S(2)}) collective-permute-start(bf16[32,1280]{1,0:T(8,128)(2,1)S(1)} %shard_map.119), channel_id=1, source_target_pairs={{0,448},{16,464},{32,480},{48,496},{64,0},{80,16},{96,32},{112,48}... | collective-permute-start | bytes 245768 | tf_op jit(solution)/shard_map/ppermute | solution.py:200
  13.7 46.8 %collective-permute-start.5 = (bf16[32,1280]{1,0:T(8,128)(2,1)S(1)}, bf16[32,1280]{1,0:T(8,128)(2,1)S(1)}, u32[]{:S(2)}, u32[]{:S(2)}) collective-permute-start(bf16[32,1280]{1,0:T(8,128)(2,1)S(1)} %shard_map.119), channel_id=1, source_target_pairs={{0,384},{16,400},{32,416},{48,432},{64,448},{80,464},{96,480},{112... | collective-permute-start | bytes 245768 | tf_op jit(solution)/shard_map/ppermute | solution.py:200
  15.9 44.6 %collective-permute-start.4 = (bf16[32,1280]{1,0:T(8,128)(2,1)S(1)}, bf16[32,1280]{1,0:T(8,128)(2,1)S(1)}, u32[]{:S(2)}, u32[]{:S(2)}) collective-permute-start(bf16[32,1280]{1,0:T(8,128)(2,1)S(1)} %shard_map.119), channel_id=1, source_target_pairs={{0,320},{16,336},{32,352},{48,368},{64,384},{80,400},{96,416},{112... | collective-permute-start | bytes 245768 | tf_op jit(solution)/shard_map/ppermute | solution.py:200
  17.8 42.7 %collective-permute-start.3 = (bf16[32,1280]{1,0:T(8,128)(2,1)S(1)}, bf16[32,1280]{1,0:T(8,128)(2,1)S(1)}, u32[]{:S(2)}, u32[]{:S(2)}) collective-permute-start(bf16[32,1280]{1,0:T(8,128)(2,1)S(1)} %shard_map.119), channel_id=1, source_target_pairs={{0,256},{16,272},{32,288},{48,304},{64,320},{80,336},{96,352},{112... | collective-permute-start | bytes 245768 | tf_op jit(solution)/shard_map/ppermute | solution.py:200
  25.1 15.8 %collective-permute-start = (bf16[32,1280]{1,0:T(8,128)(2,1)S(1)}, bf16[32,1280]{1,0:T(8,128)(2,1)S(1)}, u32[]{:S(2)}, u32[]{:S(2)}) collective-permute-start(bf16[32,1280]{1,0:T(8,128)(2,1)S(1)} %shard_map.119), channel_id=1, source_target_pairs={{0,64},{16,80},{32,96},{48,112},{64,128},{80,144},{96,160},{112,17... | collective-permute-start | bytes 245768 | tf_op jit(solution)/shard_map/ppermute | solution.py:200
  28.2 1.0 copy-start
  29.2 0.9 copy-start.2
  31.7 65.1 %all-to-all-start = ((bf16[16,16,2048]{2,1,0:T(8,128)(2,1)}), bf16[16,16,2048]{2,1,0:T(8,128)(2,1)S(1)}, u32[]{:S(2)}, u32[]{:S(2)}) async-start(bf16[16,16,2048]{2,1,0:T(8,128)(2,1)} %bitcast.2), calls=%async_computation | async-start | bytes 2097152 | tf_op jit(solution)/shard_map/all_to_all | solution.py:210
  40.9 10.0 %collective-permute-start.1 = (bf16[32,1280]{1,0:T(8,128)(2,1)S(1)}, bf16[32,1280]{1,0:T(8,128)(2,1)S(1)}, u32[]{:S(2)}, u32[]{:S(2)}) collective-permute-start(bf16[32,1280]{1,0:T(8,128)(2,1)S(1)} %shard_map.119), channel_id=1, source_target_pairs={{0,128},{16,144},{32,160},{48,176},{64,192},{80,208},{96,224},{112... | collective-permute-start | bytes 245768 | tf_op jit(solution)/shard_map/ppermute | solution.py:200
  50.9 9.6 %collective-permute-start.2 = (bf16[32,1280]{1,0:T(8,128)(2,1)S(1)}, bf16[32,1280]{1,0:T(8,128)(2,1)S(1)}, u32[]{:S(2)}, u32[]{:S(2)}) collective-permute-start(bf16[32,1280]{1,0:T(8,128)(2,1)S(1)} %shard_map.119), channel_id=1, source_target_pairs={{0,192},{16,208},{32,224},{48,240},{64,256},{80,272},{96,288},{112... | collective-permute-start | bytes 245768 | tf_op jit(solution)/shard_map/ppermute | solution.py:200
  60.6 19.8 %collective-permute-start.9 = (bf16[256,1280]{1,0:T(8,128)(2,1)S(1)}, bf16[256,1280]{1,0:T(8,128)(2,1)S(1)}, u32[]{:S(2)}, u32[]{:S(2)}) collective-permute-start(bf16[256,1280]{1,0:T(8,128)(2,1)S(1)} %constant_dynamic-update-slice_fusion.b0_ref), channel_id=1, source_target_pairs={{0,48},{16,0},{32,16},{48,32},{64,112},{80,64},{96,80},{112,96},{1... | collective-permute-start | bytes 1966088 | tf_op jit(solution)/shard_map/ppermute | solution.py:205
  63.1 28.9 %collective-permute-start.8 = (bf16[256,1280]{1,0:T(8,128)(2,1)S(1)}, bf16[256,1280]{1,0:T(8,128)(2,1)S(1)}, u32[]{:S(2)}, u32[]{:S(2)}) collective-permute-start(bf16[256,1280]{1,0:T(8,128)(2,1)S(1)} %constant_dynamic-update-slice_fusion.b0_ref), channel_id=1, source_target_pairs={{0,32},{16,48},{32,0},{48,16},{64,96},{80,112},{96,64},{112,80},{1... | collective-permute-start | bytes 1966088 | tf_op jit(solution)/shard_map/ppermute | solution.py:205
  65.8 30.1 %collective-permute-start.7 = (bf16[256,1280]{1,0:T(8,128)(2,1)S(1)}, bf16[256,1280]{1,0:T(8,128)(2,1)S(1)}, u32[]{:S(2)}, u32[]{:S(2)}) collective-permute-start(bf16[256,1280]{1,0:T(8,128)(2,1)S(1)} %constant_dynamic-update-slice_fusion.b0_ref), channel_id=1, source_target_pairs={{0,16},{16,32},{32,48},{48,0},{64,80},{80,96},{96,112},{112,64},{1... | collective-permute-start | bytes 1966088 | tf_op jit(solution)/shard_map/ppermute | solution.py:205
  95.9 0.9 copy-start.15
  96.7 1.1 copy-start.9
  97.8 1.1 copy-start.13
  98.9 1.1 copy-start.16
  106.5 13.4 %copy-start.11 = (bf16[256,1280]{1,0:T(8,128)(2,1)S(1)}, bf16[256,1280]{1,0:T(8,128)(2,1)}, u32[]{:S(2)}) copy-start(bf16[256,1280]{1,0:T(8,128)(2,1)} %copy-done.10) | copy-start | bytes 1966084
  106.5 78.5 %all-to-all-start.1 = ((bf16[16,16,2048]{2,1,0:T(8,128)(2,1)}), bf16[16,16,2048]{2,1,0:T(8,128)(2,1)S(1)}, u32[]{:S(2)}, u32[]{:S(2)}) async-start(bf16[16,16,2048]{2,1,0:T(8,128)(2,1)} %bitcast.7), calls=%async_computation.1 | async-start | bytes 2097152 | tf_op jit(solution)/shard_map/all_to_all | solution.py:210
  115.6 32.5 %collective-permute-start.10 = (bf16[256,1280]{1,0:T(8,128)(2,1)}, bf16[256,1280]{1,0:T(8,128)(2,1)S(1)}, u32[]{:S(2)}, u32[]{:S(2)}) collective-permute-start(bf16[256,1280]{1,0:T(8,128)(2,1)} %copy-done.14), channel_id=1, source_target_pairs={{0,16},{16,32},{32,48},{48,0},{64,80},{80,96},{96,112},{112,64},{1... | collective-permute-start | bytes 1966088 | tf_op jit(solution)/shard_map/ppermute | solution.py:205
  119.9 28.3 %collective-permute-start.11 = (bf16[256,1280]{1,0:T(8,128)(2,1)S(1)}, bf16[256,1280]{1,0:T(8,128)(2,1)S(1)}, u32[]{:S(2)}, u32[]{:S(2)}) collective-permute-start(bf16[256,1280]{1,0:T(8,128)(2,1)S(1)} %copy-done.11), channel_id=1, source_target_pairs={{0,32},{16,48},{32,0},{48,16},{64,96},{80,112},{96,64},{112,80},{1... | collective-permute-start | bytes 1966088 | tf_op jit(solution)/shard_map/ppermute | solution.py:205
  121.8 32.2 %collective-permute-start.12 = (bf16[256,1280]{1,0:T(8,128)(2,1)S(1)}, bf16[256,1280]{1,0:T(8,128)(2,1)S(1)}, u32[]{:S(2)}, u32[]{:S(2)}) collective-permute-start(bf16[256,1280]{1,0:T(8,128)(2,1)S(1)} %get-tuple-element.32), channel_id=1, source_target_pairs={{0,48},{16,0},{32,16},{48,32},{64,112},{80,64},{96,80},{112,96},{1... | collective-permute-start | bytes 1966088 | tf_op jit(solution)/shard_map/ppermute | solution.py:205
  154.3 16.9 %collective-permute-start.13 = (bf16[32,1280]{1,0:T(8,128)(2,1)S(1)}, bf16[32,1280]{1,0:T(8,128)(2,1)S(1)}, u32[]{:S(2)}, u32[]{:S(2)}) collective-permute-start(bf16[32,1280]{1,0:T(8,128)(2,1)S(1)} %get-tuple-element.34), channel_id=1, source_target_pairs={{0,64},{16,80},{32,96},{48,112},{64,128},{80,144},{96,160},{112,17... | collective-permute-start | bytes 245768 | tf_op jit(solution)/shard_map/ppermute | solution.py:200
  156.2 18.8 %collective-permute-start.14 = (bf16[32,1280]{1,0:T(8,128)(2,1)S(1)}, bf16[32,1280]{1,0:T(8,128)(2,1)S(1)}, u32[]{:S(2)}, u32[]{:S(2)}) collective-permute-start(bf16[32,1280]{1,0:T(8,128)(2,1)S(1)} %get-tuple-element.35), channel_id=1, source_target_pairs={{0,128},{16,144},{32,160},{48,176},{64,192},{80,208},{96,224},{112... | collective-permute-start | bytes 245768 | tf_op jit(solution)/shard_map/ppermute | solution.py:200
  158.4 18.9 %collective-permute-start.15 = (bf16[32,1280]{1,0:T(8,128)(2,1)S(1)}, bf16[32,1280]{1,0:T(8,128)(2,1)S(1)}, u32[]{:S(2)}, u32[]{:S(2)}) collective-permute-start(bf16[32,1280]{1,0:T(8,128)(2,1)S(1)} %get-tuple-element.36), channel_id=1, source_target_pairs={{0,192},{16,208},{32,224},{48,240},{64,256},{80,272},{96,288},{112... | collective-permute-start | bytes 245768 | tf_op jit(solution)/shard_map/ppermute | solution.py:200
  163.2 14.1 %collective-permute-start.16 = (bf16[32,1280]{1,0:T(8,128)(2,1)S(1)}, bf16[32,1280]{1,0:T(8,128)(2,1)S(1)}, u32[]{:S(2)}, u32[]{:S(2)}) collective-permute-start(bf16[32,1280]{1,0:T(8,128)(2,1)S(1)} %get-tuple-element.37), channel_id=1, source_target_pairs={{0,256},{16,272},{32,288},{48,304},{64,320},{80,336},{96,352},{112... | collective-permute-start | bytes 245768 | tf_op jit(solution)/shard_map/ppermute | solution.py:200
  167.6 9.7 %collective-permute-start.17 = (bf16[32,1280]{1,0:T(8,128)(2,1)S(1)}, bf16[32,1280]{1,0:T(8,128)(2,1)S(1)}, u32[]{:S(2)}, u32[]{:S(2)}) collective-permute-start(bf16[32,1280]{1,0:T(8,128)(2,1)S(1)} %get-tuple-element.38), channel_id=1, source_target_pairs={{0,320},{16,336},{32,352},{48,368},{64,384},{80,400},{96,416},{112... | collective-permute-start | bytes 245768 | tf_op jit(solution)/shard_map/ppermute | solution.py:200
  171.2 10.3 %collective-permute-start.18 = (bf16[32,1280]{1,0:T(8,128)(2,1)S(1)}, bf16[32,1280]{1,0:T(8,128)(2,1)S(1)}, u32[]{:S(2)}, u32[]{:S(2)}) collective-permute-start(bf16[32,1280]{1,0:T(8,128)(2,1)S(1)} %get-tuple-element.39), channel_id=1, source_target_pairs={{0,384},{16,400},{32,416},{48,432},{64,448},{80,464},{96,480},{112... | collective-permute-start | bytes 245768 | tf_op jit(solution)/shard_map/ppermute | solution.py:200
  175.0 9.2 %collective-permute-start.19 = (bf16[32,1280]{1,0:T(8,128)(2,1)S(1)}, bf16[32,1280]{1,0:T(8,128)(2,1)S(1)}, u32[]{:S(2)}, u32[]{:S(2)}) collective-permute-start(bf16[32,1280]{1,0:T(8,128)(2,1)S(1)} %get-tuple-element.40), channel_id=1, source_target_pairs={{0,448},{16,464},{32,480},{48,496},{64,0},{80,16},{96,32},{112,48}... | collective-permute-start | bytes 245768 | tf_op jit(solution)/shard_map/ppermute | solution.py:200
  184.3 1.0 copy-start.1
  (7 other events, 5.6 us)

commit v2 on v1

v2 whole, which is shorter than its diff:
```python
import jax
import jax.numpy as jnp
from jax import lax
from jax.experimental import pallas as pl
from jax.experimental.pallas import tpu as pltpu
from jax.sharding import PartitionSpec as P

FLIGHT = 16
CAP = 16
NZ = 8
NX = 4
TOK = 128
D = 1024
FF = 384
ROWS = FLIGHT * CAP
FD = FF // (NZ * NX)
SH = D // (NZ * NX)
PW = 2 * FF + D // 2
BF = jnp.bfloat16
F32 = jnp.float32
MIB = 1 << 20


def dot(a, b, dims):
    return lax.dot_general(a, b, (dims, ((), ())), preferred_element_type=F32)


def nn(a, b):
    return dot(a, b, ((1,), (0,)))


def tn(a, b):
    return dot(a, b, ((0,), (0,)))


def nt(a, b):
    return dot(a, b, ((1,), (1,)))


def route_rows(ids_t, weights_t):
    live = ids_t < FLIGHT
    expert = jnp.sum(jnp.where(live, ids_t, 0), axis=0, keepdims=True)
    weight = jnp.sum(jnp.where(live, weights_t, 0.0), axis=0, keepdims=True)
    alive = jnp.max(live.astype(jnp.int32), axis=0, keepdims=True) > 0
    return live, expert, weight, alive


def place(ids_t, weights_t):
    live, expert, weight, alive = route_rows(ids_t, weights_t)
    named = (lax.broadcasted_iota(jnp.int32, (FLIGHT, TOK), 0) == expert) & alive
    before = lax.broadcasted_iota(jnp.int32, (TOK, TOK), 0) < lax.broadcasted_iota(
        jnp.int32, (TOK, TOK), 1
    )
    rank = nn(named.astype(F32).astype(BF), before.astype(F32).astype(BF))
    slot = jnp.sum(jnp.where(named, rank, 0.0), axis=0, keepdims=True).astype(jnp.int32)
    row = jnp.where(alive, expert * CAP + slot, -1)
    mask = lax.broadcasted_iota(jnp.int32, (ROWS, TOK), 0) == row
    return live, weight, mask


def column_of(row):
    eye = lax.broadcasted_iota(jnp.int32, (TOK, TOK), 0) == lax.broadcasted_iota(
        jnp.int32, (TOK, TOK), 1
    )
    return jnp.sum(jnp.where(eye, row, 0.0), axis=1, keepdims=True)


def row_of(column):
    eye = lax.broadcasted_iota(jnp.int32, (TOK, TOK), 0) == lax.broadcasted_iota(
        jnp.int32, (TOK, TOK), 1
    )
    return jnp.sum(jnp.where(eye, column, 0.0), axis=0, keepdims=True)


def pack_kernel(gate_ref, up_ref, down_ref, out_ref, gate, up, sems):
    copies = [
        pltpu.make_async_copy(gate_ref, gate, sems.at[0]),
        pltpu.make_async_copy(up_ref, up, sems.at[1]),
    ]
    for copy in copies:
        copy.start()
    down = jnp.concatenate(
        [down_ref[...].astype(F32), jnp.zeros((16 - FD, D), F32)], axis=0
    ).astype(BF)
    for i in range(NZ):
        out_ref[i, :16, 2 * FF :] = down[:, : D // 2]
        out_ref[i, 16:, 2 * FF :] = down[:, D // 2 :]
    for copy in copies:
        copy.wait()
    for i in range(NZ):
        out_ref[i, :, :FF] = gate[...]
        out_ref[i, :, FF : 2 * FF] = up[...]


def dispatch_kernel(ids_ref, weights_ref, tokens_ref, upstream_ref, out_ref):
    live, weight, mask = place(ids_ref[...], weights_ref[...])
    picker = mask.astype(F32).astype(BF)
    out_ref[:, :D] = nn(picker, tokens_ref[...]).astype(BF)
    row_weight = jnp.sum(jnp.where(mask, weight, 0.0), axis=1, keepdims=True)
    out_ref[:, D:] = (row_weight * nn(picker, upstream_ref[...])).astype(BF)


def expert_kernel(*refs):
    recv_ref, weights_ref = refs[:2]
    (sent_ref, q_own, q_right_lo, q_right_hi, q_left_lo, q_left_hi, q_far_lo, q_far_hi) = refs[2:10]
    recv, sent, full, grads, sems = refs[10:]
    x = lax.axis_index("dp") % NX
    to_right, to_left, across = (lax.rem(x + k, NX) for k in (1, NX - 1, 2))
    low, high = pl.ds(0, NZ // 2), pl.ds(NZ // 2, NZ // 2)
    every = pl.ds(0, NZ)

    def spots(buffer):
        return (
            buffer.at[every, x],
            buffer.at[low, to_left],
            buffer.at[high, to_right],
            buffer.at[high, to_left],
            buffer.at[low, to_right],
            buffer.at[low, across],
            buffer.at[high, across],
        )

    starts = [0] + [NZ + i * (NZ // 2) for i in range(7)]
    pieces = [weights_ref.at[pl.ds(a, b - a)] for a, b in zip(starts[:-1], starts[1:])]
    fetches = [pltpu.make_async_copy(recv_ref, recv, sems.at[0])]
    for i, (piece, spot) in enumerate(zip(pieces, spots(full))):
        fetches.append(pltpu.make_async_copy(piece, spot, sems.at[1 + i]))
    for fetch in fetches:
        fetch.start()
    column = lax.broadcasted_iota(jnp.int32, (FF, 16 * NZ * NX), 1)
    of_row = (column // 16) * FD + column % 16
    row = lax.broadcasted_iota(jnp.int32, (FF, 16 * NZ * NX), 0)
    unpad = ((row == of_row) & (column % 16 < FD)).astype(F32).astype(BF)
    for fetch in fetches:
        fetch.wait()

    gate = full[:, :, :, :FF].reshape(D, FF)
    up = full[:, :, :, FF : 2 * FF].reshape(D, FF)
    upper = full[:, :, :16, 2 * FF :].reshape(16 * NZ * NX, D // 2)
    lower = full[:, :, 16:, 2 * FF :].reshape(16 * NZ * NX, D // 2)
    down = jnp.concatenate([nn(unpad, upper).astype(BF), nn(unpad, lower).astype(BF)], axis=1)
    rows, scaled = recv[:, :D], recv[:, D:]
    pre_gate = nn(rows, gate)
    pre_up = nn(rows, up)
    grad_hidden = nt(scaled, down)
    sigma = jax.nn.sigmoid(pre_gate)
    silu = pre_gate * sigma
    hidden = (silu * pre_up).astype(BF)
    sent[:, :D] = nn(hidden, down).astype(BF)
    grad_gate_pre = (grad_hidden * pre_up * sigma * (1.0 + pre_gate * (1.0 - sigma))).astype(BF)
    grad_up_pre = (grad_hidden * silu).astype(BF)
    sent[:, D:] = (nt(grad_gate_pre, gate) + nt(grad_up_pre, up)).astype(BF)
    stores = [pltpu.make_async_copy(sent, sent_ref, sems.at[0])]
    stores[0].start()
    grads[:, :, :, :FF] = tn(rows, grad_gate_pre).astype(BF).reshape(NZ, NX, SH, FF)
    grads[:, :, :, FF : 2 * FF] = tn(rows, grad_up_pre).astype(BF).reshape(NZ, NX, SH, FF)
    hidden_padded = nn(hidden, unpad).astype(BF)
    part_down = tn(hidden_padded, scaled).astype(BF)
    grads[:, :, :16, 2 * FF :] = part_down[:, : D // 2].reshape(NZ, NX, 16, D // 2)
    grads[:, :, 16:, 2 * FF :] = part_down[:, D // 2 :].reshape(NZ, NX, 16, D // 2)
    pieces = (q_own, q_left_lo, q_right_hi, q_left_hi, q_right_lo, q_far_lo, q_far_hi)
    for i, (piece, spot) in enumerate(zip(pieces, spots(grads))):
        stores.append(pltpu.make_async_copy(spot, piece, sems.at[1 + i]))
        stores[-1].start()
    for store in stores:
        store.wait()


def add_far_kernel(right_ref, left_ref, low_ref, high_ref, to_right_ref, to_left_ref):
    to_right_ref[...] = (right_ref[...].astype(F32) + low_ref[...].astype(F32)).astype(BF)
    to_left_ref[...] = (left_ref[...].astype(F32) + high_ref[...].astype(F32)).astype(BF)


def sum_x_kernel(own_ref, left_lo, left_hi, right_lo, right_hi, after_ref, out_ref):
    del after_ref
    h = NZ // 2
    low = left_lo[...].astype(F32) + right_lo[...].astype(F32)
    out_ref[:h] = (own_ref[:h].astype(F32) + low).astype(BF)
    high = left_hi[...].astype(F32) + right_hi[...].astype(F32)
    out_ref[h:] = (own_ref[h:].astype(F32) + high).astype(BF)


def sum_z_kernel(parts_ref, gate_ref, up_ref, down_ref):
    total = parts_ref[0].astype(F32)
    for z in range(1, NZ):
        total = total + parts_ref[z].astype(F32)
    gate_ref[...] = total[:, :FF].astype(BF)
    up_ref[...] = total[:, FF : 2 * FF].astype(BF)
    down_ref[:, : D // 2] = total[:FD, 2 * FF :].astype(BF)
    down_ref[:, D // 2 :] = total[16 : 16 + FD, 2 * FF :].astype(BF)


def combine_kernel(ids_ref, weights_ref, upstream_ref, home_ref, mixed_ref, tokens_ref, route_ref):
    live, weight, mask = place(ids_ref[...], weights_ref[...])
    picker = mask.astype(F32).astype(BF)
    tokens_ref[...] = tn(picker, home_ref[:, D:]).astype(BF)
    picked = tn(picker, home_ref[:, :D])
    mixed_ref[...] = (column_of(weight) * picked).astype(BF)
    inner = jnp.sum(upstream_ref[...].astype(F32) * picked, axis=1, keepdims=True)
    route_ref[...] = jnp.where(live, row_of(inner), 0.0)


def call(kernel, outs, scratch=(), vmem=16 * MIB, flops=0, moved=MIB, spaces=None, any_outs=False):
    shapes = [jax.ShapeDtypeStruct(s, t) for s, t in outs]
    single = len(shapes) == 1
    specs = {}
    if spaces is not None:
        specs["in_specs"] = [pl.BlockSpec(memory_space=a or pltpu.VMEM) for a in spaces]
    if any_outs:
        specs["out_specs"] = [pl.BlockSpec(memory_space=pl.ANY)] * len(outs)
    return pl.pallas_call(
        kernel,
        out_shape=shapes[0] if single else shapes,
        scratch_shapes=list(scratch),
        compiler_params=pltpu.CompilerParams(vmem_limit_bytes=vmem),
        cost_estimate=pl.CostEstimate(flops=flops, bytes_accessed=moved, transcendentals=0),
        **specs,
    )


def swap_z(v):
    groups = [[z * NX + x for z in range(NZ)] for x in range(NX)]
    return lax.all_to_all(
        v, "dp", split_axis=0, concat_axis=0, tiled=True, axis_index_groups=groups
    )


def shift_x(v, k):
    pairs = [(z * NX + x, z * NX + (x + k) % NX) for z in range(NZ) for x in range(NX)]
    return lax.ppermute(v, "dp", pairs)


def exchange(v):
    v = v.reshape(FLIGHT, CAP, 2 * D)
    return lax.all_to_all(v, "expert", split_axis=0, concat_axis=0, tiled=True).reshape(ROWS, 2 * D)


def on_device(tokens, route_ids, route_weights, upstream, w_gate, w_up, w_down):
    ids_t, weights_t = route_ids.T, route_weights.T
    shard = pltpu.VMEM((SH, FF), BF)
    copies = call(
        pack_kernel,
        [((NZ, SH, PW), BF)],
        scratch=[shard, shard, pltpu.SemaphoreType.DMA((2,))],
        vmem=58 * MIB,
        spaces=(pl.ANY, pl.ANY, None),
    )(w_gate[0], w_up[0], w_down[0])
    own = swap_z(copies)
    sent = call(dispatch_kernel, [((ROWS, 2 * D), BF)], flops=4 * ROWS * TOK * D)(
        ids_t, weights_t, tokens, upstream
    )
    recv = exchange(sent)
    half = NZ // 2
    low, high = own[:half], own[half:]
    left_lo, right_hi = shift_x(low, 1), shift_x(high, NX - 1)
    left_hi, right_lo = shift_x(high, 1), shift_x(low, NX - 1)
    far_lo, far_hi = shift_x(left_lo, 1), shift_x(right_hi, NX - 1)
    whole, part = ((NZ, SH, PW), BF), ((half, SH, PW), BF)
    tile = pltpu.VMEM((ROWS, 2 * D), BF)
    matrix = pltpu.VMEM((NZ, NX, SH, PW), BF)
    back, q_own, q_right_lo, q_right_hi, q_left_lo, q_left_hi, q_far_lo, q_far_hi = call(
        expert_kernel,
        [((ROWS, 2 * D), BF), whole] + [part] * 6,
        scratch=[tile, tile, matrix, matrix, pltpu.SemaphoreType.DMA((8,))],
        vmem=48 * MIB,
        flops=18 * ROWS * D * FF,
        moved=8 * MIB,
        spaces=(pl.ANY,) * 2,
        any_outs=True,
    )(
        recv,
        jnp.concatenate([own, left_lo, right_hi, left_hi, right_lo, far_lo, far_hi], axis=0),
    )
    home = exchange(back)
    add_lo, add_hi = shift_x(q_far_lo, 1), shift_x(q_far_hi, NX - 1)
    from_left_hi, from_right_lo = shift_x(q_right_hi, 1), shift_x(q_left_lo, NX - 1)
    to_right, to_left = call(add_far_kernel, [part, part], moved=2 * MIB)(
        q_right_lo, q_left_hi, add_lo, add_hi
    )
    from_left_lo, from_right_hi = shift_x(to_right, 1), shift_x(to_left, NX - 1)
    total = call(sum_x_kernel, [whole], moved=3 * MIB, spaces=(None,) * 5 + (pl.ANY,))(
        q_own, from_left_lo, from_left_hi, from_right_lo, from_right_hi, home
    )
    parts = swap_z(total)
    grad_gate, grad_up, grad_down = call(
        sum_z_kernel, [((SH, FF), BF), ((SH, FF), BF), ((FD, D), BF)]
    )(parts)
    mixed, grad_tokens, grad_route = call(
        combine_kernel,
        [((TOK, D), BF), ((TOK, D), BF), ((8, TOK), F32)],
        flops=4 * ROWS * TOK * D,
        moved=2 * MIB,
    )(ids_t, weights_t, upstream, home)
    return (mixed, grad_tokens, grad_route.T, grad_gate[None], grad_up[None], grad_down[None])


def solution(mesh):
    rows, held = P(("dp", "expert"), None), P("expert", "dp", None)
    return jax.shard_map(
        on_device,
        mesh=mesh,
        in_specs=(rows, rows, rows, rows, held, held, held),
        out_specs=(rows, rows, rows, held, held, held),
        check_vma=False,
    )
```

time: 188 us -> 141 us (0.75)
  waiting for transfers between devices: 77.1 us -> 50.9 us
  starting transfers between devices: 87.9 us -> 65.9 us
  Pallas kernels: 8.61 us -> 13.4 us
  local copies, waits for them, and re-layouts: 12 us -> 8.71 us
    ppermute x14 -> x0, starting transfers between devices: 52 us -> none  [shift_z(): return lax.ppermute(v, 'dp', pairs)]
    ppermute x6 -> x12, waiting for transfers between devices: 54.3 us -> 15.6 us  [shift_x(): return lax.ppermute(v, 'dp', pairs)]
    all_to_all x0 -> x2, waiting for transfers between devices: none -> 35.3 us  [swap_z(): lax.all_to_all(v, 'dp', split_axis=0, concat_axis=0, tiled=True, axis_ind...]
    ppermute x14 -> x0, waiting for transfers between devices: 22.7 us -> none  [shift_z(): return lax.ppermute(v, 'dp', pairs)]
    ppermute x6 -> x12, starting transfers between devices: 17.6 us -> 35.4 us  [shift_x(): return lax.ppermute(v, 'dp', pairs)]
    all_to_all x0 -> x2, starting transfers between devices: none -> 13.6 us  [swap_z(): lax.all_to_all(v, 'dp', split_axis=0, concat_axis=0, tiled=True, axis_ind...]
    pallas_call x4 -> x5, Pallas kernels: 5.78 us -> 10.5 us  [the longest x1 6.21 us: on_device(): call(expert_kernel, [((ROWS, 2 * D), BF), whole] + [part] * 6, scratch=[t...]
    unnamed x41 -> x20, local copies, waits for them, and re-layouts: 12 us -> 7.91 us
  transfers between devices with their start and end apart: 22 -> 16, of which waited for: 9 -> 8; matrix products, arithmetic and copies ran while one was open for 0% -> 4% of each run, Pallas kernels for 1% -> 2%
where the time goes in v2:
time: 141 us; the launch traced here: 140 us
  starting transfers between devices  65.9 us (47%)
  waiting for transfers between devices  50.9 us (36%)
  Pallas kernels  13.4 us (10%)
  local copies, waits for them, and re-layouts  8.71 us (6%)
    ppermute x12, starting transfers between devices, shift_x(): return lax.ppermute(v, 'dp', pairs)  35.4 us
    all_to_all x2, waiting for transfers between devices, swap_z(): lax.all_to_all(v, 'dp', split_axis=0, concat_axis=0, tiled=True, axis_ind...  35.3 us
    all_to_all x2, starting transfers between devices, exchange(): lax.all_to_all(v, 'expert', split_axis=0, concat_axis=0, tiled=True)  16.9 us
    ppermute x12, waiting for transfers between devices, shift_x(): return lax.ppermute(v, 'dp', pairs)  15.6 us
    all_to_all x2, starting transfers between devices, swap_z(): lax.all_to_all(v, 'dp', split_axis=0, concat_axis=0, tiled=True, axis_ind...  13.6 us
    unnamed x20, local copies, waits for them, and re-layouts  7.91 us
    pallas_call x1, Pallas kernels, on_device(): call(expert_kernel, [((ROWS, 2 * D), BF), whole] + [part] * 6, scratch=[t...  6.21 us
  transfers between devices with their start and end apart: 16, of which 8 were waited for; matrix products, arithmetic and copies ran while one was open for 4% of the time, Pallas kernels for 2%

profile of v2, /device:TPU:7, one launch (start us, length us, event | category | flops | bytes accessed | tf_op | source)
XLA Modules:
  0.0 139.7 jit_solution(1943084420058836367)
XLA Ops:
  0.6 2.4 %shard_map.119 = bf16[8,32,1280]{2,1,0:T(8,128)(2,1)} custom-call(bf16[32,384]{1,0:T(8,128)(2,1)} %bitcast.21, bf16[32,384]{1,0:T(8,128)(2,1)} %bitcast.22, bf16[12,1024]{1,0:T(8,128)(2,1)} %bitcast.20), custom_call_target="tpu_custom_call" | custom-call | bytes 1048576 | tf_op jit(solution)/shard_map/pallas_call | solution.py:241
  3.0 10.0 %all-to-all-start.1 = ((bf16[8,32,1280]{2,1,0:T(8,128)(2,1)}), bf16[8,32,1280]{2,1,0:T(8,128)(2,1)S(1)}, u32[]{:S(2)}, u32[]{:S(2)}) async-start(bf16[8,32,1280]{2,1,0:T(8,128)(2,1)} %shard_map.119), calls=%async_computation.1 | async-start | bytes 1310720 | tf_op jit(solution)/shard_map/all_to_all | solution.py:223
  13.1 0.9 copy-done
  14.0 0.9 copy-done.2
  16.4 1.5 %shard_map.118 = bf16[256,2048]{1,0:T(8,128)(2,1)} custom-call(s32[8,128]{1,0:T(8,128)S(1)} %bitcast.16, f32[8,128]{1,0:T(8,128)S(1)} %bitcast.18, bf16[128,1024]{1,0:T(8,128)(2,1)S(1)} %copy-done.2, bf16[128,1024]{1,0:T(8,128)(2,1)S(1)} %copy-done), custom_call_target="tpu_custom_call" | custom-call | flops 134217728 | bytes 1048576 | tf_op jit(solution)/shard_map/pallas_call | solution.py:249
  17.9 15.9 %all-to-all-done.1 = bf16[8,32,1280]{2,1,0:T(8,128)(2,1)S(1)} async-done(((bf16[8,32,1280]{2,1,0:T(8,128)(2,1)}), bf16[8,32,1280]{2,1,0:T(8,128)(2,1)S(1)}, u32[]{:S(2)}, u32[]{:S(2)}) %all-to-all-start.1) | async-done | bytes 655392 | tf_op jit(solution)/shard_map/all_to_all | solution.py:223
  33.9 7.6 %all-to-all-start = ((bf16[16,16,2048]{2,1,0:T(8,128)(2,1)}), bf16[16,16,2048]{2,1,0:T(8,128)(2,1)S(1)}, u32[]{:S(2)}, u32[]{:S(2)}) async-start(bf16[16,16,2048]{2,1,0:T(8,128)(2,1)} %bitcast.2), calls=%async_computation | async-start | bytes 2097152 | tf_op jit(solution)/shard_map/all_to_all | solution.py:235
  41.5 2.1 %collective-permute-start = (bf16[4,32,1280]{2,1,0:T(8,128)(2,1)S(1)}, bf16[4,32,1280]{2,1,0:T(8,128)(2,1)S(1)}, u32[]{:S(2)}, u32[]{:S(2)}) collective-permute-start(bf16[4,32,1280]{2,1,0:T(8,128)(2,1)S(1)} %get-tuple-element.39), channel_id=1, source_target_pairs={{0,16},{16,32},{32,48},{48,0},{64,80},{80,96},{96,112},{112,64},{1... | collective-permute-start | bytes 983048 | tf_op jit(solution)/shard_map/ppermute | solution.py:230
  43.6 3.2 %collective-permute-start.1 = (bf16[4,32,1280]{2,1,0:T(8,128)(2,1)S(1)}, bf16[4,32,1280]{2,1,0:T(8,128)(2,1)S(1)}, u32[]{:S(2)}, u32[]{:S(2)}) collective-permute-start(bf16[4,32,1280]{2,1,0:T(8,128)(2,1)S(1)} %get-tuple-element.38), channel_id=1, source_target_pairs={{0,48},{16,0},{32,16},{48,32},{64,112},{80,64},{96,80},{112,96},{1... | collective-permute-start | bytes 983048 | tf_op jit(solution)/shard_map/ppermute | solution.py:230
  46.8 3.3 %collective-permute-start.2 = (bf16[4,32,1280]{2,1,0:T(8,128)(2,1)S(1)}, bf16[4,32,1280]{2,1,0:T(8,128)(2,1)S(1)}, u32[]{:S(2)}, u32[]{:S(2)}) collective-permute-start(bf16[4,32,1280]{2,1,0:T(8,128)(2,1)S(1)} %get-tuple-element.38), channel_id=1, source_target_pairs={{0,16},{16,32},{32,48},{48,0},{64,80},{80,96},{96,112},{112,64},{1... | collective-permute-start | bytes 983048 | tf_op jit(solution)/shard_map/ppermute | solution.py:230
  50.2 2.0 %collective-permute-start.3 = (bf16[4,32,1280]{2,1,0:T(8,128)(2,1)S(1)}, bf16[4,32,1280]{2,1,0:T(8,128)(2,1)S(1)}, u32[]{:S(2)}, u32[]{:S(2)}) collective-permute-start(bf16[4,32,1280]{2,1,0:T(8,128)(2,1)S(1)} %get-tuple-element.39), channel_id=1, source_target_pairs={{0,48},{16,0},{32,16},{48,32},{64,112},{80,64},{96,80},{112,96},{1... | collective-permute-start | bytes 983048 | tf_op jit(solution)/shard_map/ppermute | solution.py:230
  52.1 0.9 constant_dynamic-update-slice_fusion.6
  53.0 4.5 %collective-permute-start.4 = (bf16[4,32,1280]{2,1,0:T(8,128)(2,1)S(1)}, bf16[4,32,1280]{2,1,0:T(8,128)(2,1)S(1)}, u32[]{:S(2)}, u32[]{:S(2)}) collective-permute-start(bf16[4,32,1280]{2,1,0:T(8,128)(2,1)S(1)} %collective-permute-done), channel_id=1, source_target_pairs={{0,16},{16,32},{32,48},{48,0},{64,80},{80,96},{96,112},{112,64},{1... | collective-permute-start | bytes 983048 | tf_op jit(solution)/shard_map/ppermute | solution.py:230
  57.5 0.8 constant_dynamic-update-slice_fusion.5
  58.3 1.9 %collective-permute-start.5 = (bf16[4,32,1280]{2,1,0:T(8,128)(2,1)S(1)}, bf16[4,32,1280]{2,1,0:T(8,128)(2,1)S(1)}, u32[]{:S(2)}, u32[]{:S(2)}) collective-permute-start(bf16[4,32,1280]{2,1,0:T(8,128)(2,1)S(1)} %collective-permute-done.1), channel_id=1, source_target_pairs={{0,48},{16,0},{32,16},{48,32},{64,112},{80,64},{96,80},{112,96},{1... | collective-permute-start | bytes 983048 | tf_op jit(solution)/shard_map/ppermute | solution.py:230
  61.7 0.9 collective-permute-done.3
  63.3 3.4 %collective-permute-done.4 = bf16[4,32,1280]{2,1,0:T(8,128)(2,1)S(1)} collective-permute-done((bf16[4,32,1280]{2,1,0:T(8,128)(2,1)S(1)}, bf16[4,32,1280]{2,1,0:T(8,128)(2,1)S(1)}, u32[]{:S(2)}, u32[]{:S(2)}) %collective-permute-start.4) | collective-permute-done | bytes 327712 | tf_op jit(solution)/shard_map/ppermute | solution.py:230
  67.5 1.6 %collective-permute-done.5 = bf16[4,32,1280]{2,1,0:T(8,128)(2,1)S(1)} collective-permute-done((bf16[4,32,1280]{2,1,0:T(8,128)(2,1)S(1)}, bf16[4,32,1280]{2,1,0:T(8,128)(2,1)S(1)}, u32[]{:S(2)}, u32[]{:S(2)}) %collective-permute-start.5) | collective-permute-done | bytes 327712 | tf_op jit(solution)/shard_map/ppermute | solution.py:230
  69.9 6.2 %shard_map.120 = (bf16[256,2048]{1,0:T(8,128)(2,1)}, bf16[8,32,1280]{2,1,0:T(8,128)(2,1)S(1)}, bf16[4,32,1280]{2,1,0:T(8,128)(2,1)S(1)}, bf16[4,32,1280]{2,1,0:T...) custom-call(bf16[256,2048]{1,0:T(8,128)(2,1)S(1)} %bitcast.15, ...), custom_call_target="tpu_custom_call" | custom-call | flops 1811939328 | bytes 8388608 | tf_op jit(solution)/shard_map/pallas_call | solution.py:261
  76.1 9.3 %all-to-all-start.2 = ((bf16[16,16,2048]{2,1,0:T(8,128)(2,1)}), bf16[16,16,2048]{2,1,0:T(8,128)(2,1)S(1)}, u32[]{:S(2)}, u32[]{:S(2)}) async-start(bf16[16,16,2048]{2,1,0:T(8,128)(2,1)} %bitcast.7), calls=%async_computation.2 | async-start | bytes 2097152 | tf_op jit(solution)/shard_map/all_to_all | solution.py:235
  85.3 1.9 %collective-permute-start.6 = (bf16[4,32,1280]{2,1,0:T(8,128)(2,1)}, bf16[4,32,1280]{2,1,0:T(8,128)(2,1)S(1)}, u32[]{:S(2)}, u32[]{:S(2)}) collective-permute-start(bf16[4,32,1280]{2,1,0:T(8,128)(2,1)} %get-tuple-element.29), channel_id=1, source_target_pairs={{0,16},{16,32},{32,48},{48,0},{64,80},{80,96},{96,112},{112,64},{1... | collective-permute-start | bytes 983048 | tf_op jit(solution)/shard_map/ppermute | solution.py:230
  87.3 3.4 %collective-permute-start.7 = (bf16[4,32,1280]{2,1,0:T(8,128)(2,1)S(1)}, bf16[4,32,1280]{2,1,0:T(8,128)(2,1)S(1)}, u32[]{:S(2)}, u32[]{:S(2)}) collective-permute-start(bf16[4,32,1280]{2,1,0:T(8,128)(2,1)S(1)} %get-tuple-element.30), channel_id=1, source_target_pairs={{0,48},{16,0},{32,16},{48,32},{64,112},{80,64},{96,80},{112,96},{1... | collective-permute-start | bytes 983048 | tf_op jit(solution)/shard_map/ppermute | solution.py:230
  90.7 1.9 %collective-permute-start.10 = (bf16[4,32,1280]{2,1,0:T(8,128)(2,1)}, bf16[4,32,1280]{2,1,0:T(8,128)(2,1)S(1)}, u32[]{:S(2)}, u32[]{:S(2)}) collective-permute-start(bf16[4,32,1280]{2,1,0:T(8,128)(2,1)} %get-tuple-element.33), channel_id=1, source_target_pairs={{0,48},{16,0},{32,16},{48,32},{64,112},{80,64},{96,80},{112,96},{1... | collective-permute-start | bytes 983048 | tf_op jit(solution)/shard_map/ppermute | solution.py:230
  92.6 4.6 %collective-permute-start.9 = (bf16[4,32,1280]{2,1,0:T(8,128)(2,1)}, bf16[4,32,1280]{2,1,0:T(8,128)(2,1)S(1)}, u32[]{:S(2)}, u32[]{:S(2)}) collective-permute-start(bf16[4,32,1280]{2,1,0:T(8,128)(2,1)} %get-tuple-element.32), channel_id=1, source_target_pairs={{0,16},{16,32},{32,48},{48,0},{64,80},{80,96},{96,112},{112,64},{1... | collective-permute-start | bytes 983048 | tf_op jit(solution)/shard_map/ppermute | solution.py:230
  97.2 2.5 %collective-permute-done.7.high_ref = bf16[4,32,1280]{2,1,0:T(8,128)(2,1)S(1)} collective-permute-done((bf16[4,32,1280]{2,1,0:T(8,128)(2,1)S(1)}, bf16[4,32,1280]{2,1,0:T(8,128)(2,1)S(1)}, u32[]{:S(2)}, u32[]{:S(2)}) %collective-permute-start.7) | collective-permute-done | bytes 327712 | tf_op jit(solution)/shard_map/ppermute | solution.py:230
  99.8 2.1 %collective-permute-start.11 = (bf16[4,32,1280]{2,1,0:T(8,128)(2,1)S(1)}, bf16[4,32,1280]{2,1,0:T(8,128)(2,1)S(1)}, u32[]{:S(2)}, u32[]{:S(2)}) collective-permute-start(bf16[4,32,1280]{2,1,0:T(8,128)(2,1)S(1)} %get-tuple-element.34), channel_id=1, source_target_pairs={{0,48},{16,0},{32,16},{48,32},{64,112},{80,64},{96,80},{112,96},{1... | collective-permute-start | bytes 983048 | tf_op jit(solution)/shard_map/ppermute | solution.py:230
  101.9 4.6 %collective-permute-start.8 = (bf16[4,32,1280]{2,1,0:T(8,128)(2,1)S(1)}, bf16[4,32,1280]{2,1,0:T(8,128)(2,1)S(1)}, u32[]{:S(2)}, u32[]{:S(2)}) collective-permute-start(bf16[4,32,1280]{2,1,0:T(8,128)(2,1)S(1)} %get-tuple-element.31), channel_id=1, source_target_pairs={{0,16},{16,32},{32,48},{48,0},{64,80},{80,96},{96,112},{112,64},{1... | collective-permute-start | bytes 983048 | tf_op jit(solution)/shard_map/ppermute | solution.py:230
  106.7 7.0 %collective-permute-done.11.right_hi = bf16[4,32,1280]{2,1,0:T(8,128)(2,1)S(1)} collective-permute-done((bf16[4,32,1280]{2,1,0:T(8,128)(2,1)S(1)}, bf16[4,32,1280]{2,1,0:T(8,128)(2,1)S(1)}, u32[]{:S(2)}, u32[]{:S(2)}) %collective-permute-start.11) | collective-permute-done | bytes 327712 | tf_op jit(solution)/shard_map/ppermute | solution.py:230
  113.7 1.1 shard_map.123
  114.8 3.5 %all-to-all-start.3 = ((bf16[8,32,1280]{2,1,0:T(8,128)(2,1)}), bf16[8,32,1280]{2,1,0:T(8,128)(2,1)S(1)}, u32[]{:S(2)}, u32[]{:S(2)}) async-start(bf16[8,32,1280]{2,1,0:T(8,128)(2,1)} %shard_map.123), calls=%async_computation.3 | async-start | bytes 1310720 | tf_op jit(solution)/shard_map/all_to_all | solution.py:223
  118.3 1.3 shard_map.121
  119.6 19.4 %all-to-all-done.3.parts_ref = bf16[8,32,1280]{2,1,0:T(8,128)(2,1)S(1)} async-done(((bf16[8,32,1280]{2,1,0:T(8,128)(2,1)}), bf16[8,32,1280]{2,1,0:T(8,128)(2,1)S(1)}, u32[]{:S(2)}, u32[]{:S(2)}) %all-to-all-start.3) | async-done | bytes 655392 | tf_op jit(solution)/shard_map/all_to_all | solution.py:223
  (29 shorter events, 6.2 us)
Async XLA Ops:
  3.0 30.8 %all-to-all-start.1 = ((bf16[8,32,1280]{2,1,0:T(8,128)(2,1)}), bf16[8,32,1280]{2,1,0:T(8,128)(2,1)S(1)}, u32[]{:S(2)}, u32[]{:S(2)}) async-start(bf16[8,32,1280]{2,1,0:T(8,128)(2,1)} %shard_map.119), calls=%async_computation.1 | async-start | bytes 1310720 | tf_op jit(solution)/shard_map/all_to_all | solution.py:223
  13.1 0.9 copy-start
  14.0 0.9 copy-start.2
  15.0 0.7 copy-start.3
  15.7 0.7 copy-start.5
  33.9 36.0 %all-to-all-start = ((bf16[16,16,2048]{2,1,0:T(8,128)(2,1)}), bf16[16,16,2048]{2,1,0:T(8,128)(2,1)S(1)}, u32[]{:S(2)}, u32[]{:S(2)}) async-start(bf16[16,16,2048]{2,1,0:T(8,128)(2,1)} %bitcast.2), calls=%async_computation | async-start | bytes 2097152 | tf_op jit(solution)/shard_map/all_to_all | solution.py:235
  41.5 11.5 %collective-permute-start = (bf16[4,32,1280]{2,1,0:T(8,128)(2,1)S(1)}, bf16[4,32,1280]{2,1,0:T(8,128)(2,1)S(1)}, u32[]{:S(2)}, u32[]{:S(2)}) collective-permute-start(bf16[4,32,1280]{2,1,0:T(8,128)(2,1)S(1)} %get-tuple-element.39), channel_id=1, source_target_pairs={{0,16},{16,32},{32,48},{48,0},{64,80},{80,96},{96,112},{112,64},{1... | collective-permute-start | bytes 983048 | tf_op jit(solution)/shard_map/ppermute | solution.py:230
  43.6 14.6 %collective-permute-start.1 = (bf16[4,32,1280]{2,1,0:T(8,128)(2,1)S(1)}, bf16[4,32,1280]{2,1,0:T(8,128)(2,1)S(1)}, u32[]{:S(2)}, u32[]{:S(2)}) collective-permute-start(bf16[4,32,1280]{2,1,0:T(8,128)(2,1)S(1)} %get-tuple-element.38), channel_id=1, source_target_pairs={{0,48},{16,0},{32,16},{48,32},{64,112},{80,64},{96,80},{112,96},{1... | collective-permute-start | bytes 983048 | tf_op jit(solution)/shard_map/ppermute | solution.py:230
  46.8 14.1 %collective-permute-start.2 = (bf16[4,32,1280]{2,1,0:T(8,128)(2,1)S(1)}, bf16[4,32,1280]{2,1,0:T(8,128)(2,1)S(1)}, u32[]{:S(2)}, u32[]{:S(2)}) collective-permute-start(bf16[4,32,1280]{2,1,0:T(8,128)(2,1)S(1)} %get-tuple-element.38), channel_id=1, source_target_pairs={{0,16},{16,32},{32,48},{48,0},{64,80},{80,96},{96,112},{112,64},{1... | collective-permute-start | bytes 983048 | tf_op jit(solution)/shard_map/ppermute | solution.py:230
  50.2 12.4 %collective-permute-start.3 = (bf16[4,32,1280]{2,1,0:T(8,128)(2,1)S(1)}, bf16[4,32,1280]{2,1,0:T(8,128)(2,1)S(1)}, u32[]{:S(2)}, u32[]{:S(2)}) collective-permute-start(bf16[4,32,1280]{2,1,0:T(8,128)(2,1)S(1)} %get-tuple-element.39), channel_id=1, source_target_pairs={{0,48},{16,0},{32,16},{48,32},{64,112},{80,64},{96,80},{112,96},{1... | collective-permute-start | bytes 983048 | tf_op jit(solution)/shard_map/ppermute | solution.py:230
  53.0 13.7 %collective-permute-start.4 = (bf16[4,32,1280]{2,1,0:T(8,128)(2,1)S(1)}, bf16[4,32,1280]{2,1,0:T(8,128)(2,1)S(1)}, u32[]{:S(2)}, u32[]{:S(2)}) collective-permute-start(bf16[4,32,1280]{2,1,0:T(8,128)(2,1)S(1)} %collective-permute-done), channel_id=1, source_target_pairs={{0,16},{16,32},{32,48},{48,0},{64,80},{80,96},{96,112},{112,64},{1... | collective-permute-start | bytes 983048 | tf_op jit(solution)/shard_map/ppermute | solution.py:230
  58.3 10.8 %collective-permute-start.5 = (bf16[4,32,1280]{2,1,0:T(8,128)(2,1)S(1)}, bf16[4,32,1280]{2,1,0:T(8,128)(2,1)S(1)}, u32[]{:S(2)}, u32[]{:S(2)}) collective-permute-start(bf16[4,32,1280]{2,1,0:T(8,128)(2,1)S(1)} %collective-permute-done.1), channel_id=1, source_target_pairs={{0,48},{16,0},{32,16},{48,32},{64,112},{80,64},{96,80},{112,96},{1... | collective-permute-start | bytes 983048 | tf_op jit(solution)/shard_map/ppermute | solution.py:230
  76.1 37.6 %all-to-all-start.2 = ((bf16[16,16,2048]{2,1,0:T(8,128)(2,1)}), bf16[16,16,2048]{2,1,0:T(8,128)(2,1)S(1)}, u32[]{:S(2)}, u32[]{:S(2)}) async-start(bf16[16,16,2048]{2,1,0:T(8,128)(2,1)} %bitcast.7), calls=%async_computation.2 | async-start | bytes 2097152 | tf_op jit(solution)/shard_map/all_to_all | solution.py:235
  85.3 11.8 %collective-permute-start.6 = (bf16[4,32,1280]{2,1,0:T(8,128)(2,1)}, bf16[4,32,1280]{2,1,0:T(8,128)(2,1)S(1)}, u32[]{:S(2)}, u32[]{:S(2)}) collective-permute-start(bf16[4,32,1280]{2,1,0:T(8,128)(2,1)} %get-tuple-element.29), channel_id=1, source_target_pairs={{0,16},{16,32},{32,48},{48,0},{64,80},{80,96},{96,112},{112,64},{1... | collective-permute-start | bytes 983048 | tf_op jit(solution)/shard_map/ppermute | solution.py:230
  87.3 12.4 %collective-permute-start.7 = (bf16[4,32,1280]{2,1,0:T(8,128)(2,1)S(1)}, bf16[4,32,1280]{2,1,0:T(8,128)(2,1)S(1)}, u32[]{:S(2)}, u32[]{:S(2)}) collective-permute-start(bf16[4,32,1280]{2,1,0:T(8,128)(2,1)S(1)} %get-tuple-element.30), channel_id=1, source_target_pairs={{0,48},{16,0},{32,16},{48,32},{64,112},{80,64},{96,80},{112,96},{1... | collective-permute-start | bytes 983048 | tf_op jit(solution)/shard_map/ppermute | solution.py:230
  90.7 16.0 %collective-permute-start.10 = (bf16[4,32,1280]{2,1,0:T(8,128)(2,1)}, bf16[4,32,1280]{2,1,0:T(8,128)(2,1)S(1)}, u32[]{:S(2)}, u32[]{:S(2)}) collective-permute-start(bf16[4,32,1280]{2,1,0:T(8,128)(2,1)} %get-tuple-element.33), channel_id=1, source_target_pairs={{0,48},{16,0},{32,16},{48,32},{64,112},{80,64},{96,80},{112,96},{1... | collective-permute-start | bytes 983048 | tf_op jit(solution)/shard_map/ppermute | solution.py:230
  92.6 14.1 %collective-permute-start.9 = (bf16[4,32,1280]{2,1,0:T(8,128)(2,1)}, bf16[4,32,1280]{2,1,0:T(8,128)(2,1)S(1)}, u32[]{:S(2)}, u32[]{:S(2)}) collective-permute-start(bf16[4,32,1280]{2,1,0:T(8,128)(2,1)} %get-tuple-element.32), channel_id=1, source_target_pairs={{0,16},{16,32},{32,48},{48,0},{64,80},{80,96},{96,112},{112,64},{1... | collective-permute-start | bytes 983048 | tf_op jit(solution)/shard_map/ppermute | solution.py:230
  99.8 18.5 %copy-start.1 = (bf16[128,1024]{1,0:T(8,128)(2,1)S(1)}, bf16[128,1024]{1,0:T(8,128)(2,1)}, u32[]{:S(2)}) copy-start(bf16[128,1024]{1,0:T(8,128)(2,1)} %upstream_ref.3) | copy-start | bytes 786436
  99.8 18.5 %copy-start.4 = (s32[128,8]{0,1:T(8,128)S(1)}, s32[128,8]{0,1:T(8,128)}, u32[]{:S(2)}) copy-start(s32[128,8]{0,1:T(8,128)} %param.8) | copy-start | bytes 12292
  99.8 18.5 %copy-start.6 = (f32[128,8]{0,1:T(8,128)S(1)}, f32[128,8]{0,1:T(8,128)}, u32[]{:S(2)}) copy-start(f32[128,8]{0,1:T(8,128)} %param.9) | copy-start | bytes 12292
  99.8 13.9 %collective-permute-start.11 = (bf16[4,32,1280]{2,1,0:T(8,128)(2,1)S(1)}, bf16[4,32,1280]{2,1,0:T(8,128)(2,1)S(1)}, u32[]{:S(2)}, u32[]{:S(2)}) collective-permute-start(bf16[4,32,1280]{2,1,0:T(8,128)(2,1)S(1)} %get-tuple-element.34), channel_id=1, source_target_pairs={{0,48},{16,0},{32,16},{48,32},{64,112},{80,64},{96,80},{112,96},{1... | collective-permute-start | bytes 983048 | tf_op jit(solution)/shard_map/ppermute | solution.py:230
  101.9 11.8 %collective-permute-start.8 = (bf16[4,32,1280]{2,1,0:T(8,128)(2,1)S(1)}, bf16[4,32,1280]{2,1,0:T(8,128)(2,1)S(1)}, u32[]{:S(2)}, u32[]{:S(2)}) collective-permute-start(bf16[4,32,1280]{2,1,0:T(8,128)(2,1)S(1)} %get-tuple-element.31), channel_id=1, source_target_pairs={{0,16},{16,32},{32,48},{48,0},{64,80},{80,96},{96,112},{112,64},{1... | collective-permute-start | bytes 983048 | tf_op jit(solution)/shard_map/ppermute | solution.py:230
  114.8 24.2 %all-to-all-start.3 = ((bf16[8,32,1280]{2,1,0:T(8,128)(2,1)}), bf16[8,32,1280]{2,1,0:T(8,128)(2,1)S(1)}, u32[]{:S(2)}, u32[]{:S(2)}) async-start(bf16[8,32,1280]{2,1,0:T(8,128)(2,1)} %shard_map.123), calls=%async_computation.3 | async-start | bytes 1310720 | tf_op jit(solution)/shard_map/all_to_all | solution.py:223

commit v3 on v2

--- a/solution.py
+++ b/solution.py
@@ -15,7 +15,11 @@
 ROWS = FLIGHT * CAP
 FD = FF // (NZ * NX)
 SH = D // (NZ * NX)
-PW = 2 * FF + D // 2
+PW = 2 * FF
+PH = SH + 16
+DN = 16 * NZ * NX
+TW = D - PW
+STACK = FD // 3
 BF = jnp.bfloat16
 F32 = jnp.float32
 MIB = 1 << 20
@@ -53,8 +57,9 @@
     )
     rank = nn(named.astype(F32).astype(BF), before.astype(F32).astype(BF))
     slot = jnp.sum(jnp.where(named, rank, 0.0), axis=0, keepdims=True).astype(jnp.int32)
-    row = jnp.where(alive, expert * CAP + slot, -1)
-    mask = lax.broadcasted_iota(jnp.int32, (ROWS, TOK), 0) == row
+    core = lax.axis_index("expert") % 2
+    row = jnp.where(expert % 2 == core, 0, ROWS // 2) + (expert // 2) * CAP + slot
+    mask = lax.broadcasted_iota(jnp.int32, (ROWS, TOK), 0) == jnp.where(alive, row, -1)
     return live, weight, mask
 
 
@@ -79,25 +84,61 @@
     ]
     for copy in copies:
         copy.start()
-    down = jnp.concatenate(
-        [down_ref[...].astype(F32), jnp.zeros((16 - FD, D), F32)], axis=0
-    ).astype(BF)
+    down = down_ref[...].astype(F32)
+    tail = [down[i * STACK : (i + 1) * STACK, PW:] for i in range(3)]
+    packed = jnp.concatenate([down[:, :PW], jnp.concatenate(tail, axis=1)], axis=0)
     for i in range(NZ):
-        out_ref[i, :16, 2 * FF :] = down[:, : D // 2]
-        out_ref[i, 16:, 2 * FF :] = down[:, D // 2 :]
+        out_ref[i, SH:, :] = packed.astype(BF)
     for copy in copies:
         copy.wait()
     for i in range(NZ):
-        out_ref[i, :, :FF] = gate[...]
-        out_ref[i, :, FF : 2 * FF] = up[...]
-
-
-def dispatch_kernel(ids_ref, weights_ref, tokens_ref, upstream_ref, out_ref):
+        out_ref[i, :SH, :FF] = gate[...]
+        out_ref[i, :SH, FF:] = up[...]
+
+
+def unpad_matrices():
+    f = lax.broadcasted_iota(jnp.int32, (FF, DN), 0)
+    j = lax.broadcasted_iota(jnp.int32, (FF, DN), 1)
+    base = (f // FD) * 16
+    r = f % FD
+    body = (j == base + r).astype(F32).astype(BF)
+    tails = []
+    for i in range(3):
+        here = (r // STACK == i) & (j == base + FD + r % STACK)
+        tails.append(here.astype(F32).astype(BF))
+    return body, tails
+
+
+def dispatch_kernel(ids_ref, weights_ref, tokens_ref, upstream_ref, keep_ref, give_ref):
     live, weight, mask = place(ids_ref[...], weights_ref[...])
     picker = mask.astype(F32).astype(BF)
-    out_ref[:, :D] = nn(picker, tokens_ref[...]).astype(BF)
     row_weight = jnp.sum(jnp.where(mask, weight, 0.0), axis=1, keepdims=True)
-    out_ref[:, D:] = (row_weight * nn(picker, upstream_ref[...])).astype(BF)
+    rows = nn(picker, tokens_ref[...]).astype(BF)
+    scaled = (row_weight * nn(picker, upstream_ref[...])).astype(BF)
+    keep_ref[:, :D] = rows[: ROWS // 2]
+    keep_ref[:, D:] = scaled[: ROWS // 2]
+    give_ref[:, :D] = rows[ROWS // 2 :]
+    give_ref[:, D:] = scaled[ROWS // 2 :]
+
+
+def merge_kernel(keep_ref, got_ref, out_ref, sems):
+    core = lax.axis_index("expert") % 2
+    copies = [
+        pltpu.make_async_copy(keep_ref, out_ref.at[:, core], sems.at[0]),
+        pltpu.make_async_copy(got_ref, out_ref.at[:, 1 - core], sems.at[1]),
+    ]
+    for copy in copies:
+        copy.start()
+    for copy in copies:
+        copy.wait()
+
+
+def give_kernel(home_ref, after_ref, give_ref, sem):
+    del after_ref
+    core = lax.axis_index("expert") % 2
+    copy = pltpu.make_async_copy(home_ref.at[:, 1 - core], give_ref, sem)
+    copy.start()
+    copy.wait()
 
 
 def expert_kernel(*refs):
@@ -127,18 +168,15 @@
         fetches.append(pltpu.make_async_copy(piece, spot, sems.at[1 + i]))
     for fetch in fetches:
         fetch.start()
-    column = lax.broadcasted_iota(jnp.int32, (FF, 16 * NZ * NX), 1)
-    of_row = (column // 16) * FD + column % 16
-    row = lax.broadcasted_iota(jnp.int32, (FF, 16 * NZ * NX), 0)
-    unpad = ((row == of_row) & (column % 16 < FD)).astype(F32).astype(BF)
+    body, tails = unpad_matrices()
     for fetch in fetches:
         fetch.wait()
 
-    gate = full[:, :, :, :FF].reshape(D, FF)
-    up = full[:, :, :, FF : 2 * FF].reshape(D, FF)
-    upper = full[:, :, :16, 2 * FF :].reshape(16 * NZ * NX, D // 2)
-    lower = full[:, :, 16:, 2 * FF :].reshape(16 * NZ * NX, D // 2)
-    down = jnp.concatenate([nn(unpad, upper).astype(BF), nn(unpad, lower).astype(BF)], axis=1)
+    gate = full[:, :, :SH, :FF].reshape(D, FF)
+    up = full[:, :, :SH, FF:].reshape(D, FF)
+    packed = full[:, :, SH:, :].reshape(DN, PW)
+    last = sum(nn(tails[i], packed[:, i * TW : (i + 1) * TW]) for i in range(3))
+    down = jnp.concatenate([nn(body, packed).astype(BF), last.astype(BF)], axis=1)
     rows, scaled = recv[:, :D], recv[:, D:]
     pre_gate = nn(rows, gate)
     pre_up = nn(rows, up)
@@ -152,12 +190,13 @@
     sent[:, D:] = (nt(grad_gate_pre, gate) + nt(grad_up_pre, up)).astype(BF)
     stores = [pltpu.make_async_copy(sent, sent_ref, sems.at[0])]
     stores[0].start()
-    grads[:, :, :, :FF] = tn(rows, grad_gate_pre).astype(BF).reshape(NZ, NX, SH, FF)
-    grads[:, :, :, FF : 2 * FF] = tn(rows, grad_up_pre).astype(BF).reshape(NZ, NX, SH, FF)
-    hidden_padded = nn(hidden, unpad).astype(BF)
-    part_down = tn(hidden_padded, scaled).astype(BF)
-    grads[:, :, :16, 2 * FF :] = part_down[:, : D // 2].reshape(NZ, NX, 16, D // 2)
-    grads[:, :, 16:, 2 * FF :] = part_down[:, D // 2 :].reshape(NZ, NX, 16, D // 2)
+    grads[:, :, :SH, :FF] = tn(rows, grad_gate_pre).astype(BF).reshape(NZ, NX, SH, FF)
+    grads[:, :, :SH, FF:] = tn(rows, grad_up_pre).astype(BF).reshape(NZ, NX, SH, FF)
+    hidden_body = nn(hidden, body).astype(BF)
+    for i in range(3):
+        cols = slice(i * TW, (i + 1) * TW)
+        part = tn(hidden_body, scaled[:, cols]) + tn(nn(hidden, tails[i]).astype(BF), scaled[:, PW:])
+        grads[:, :, SH:, cols] = part.astype(BF).reshape(NZ, NX, 16, TW)
     pieces = (q_own, q_left_lo, q_right_hi, q_left_hi, q_right_lo, q_far_lo, q_far_hi)
     for i, (piece, spot) in enumerate(zip(pieces, spots(grads))):
         stores.append(pltpu.make_async_copy(spot, piece, sems.at[1 + i]))
@@ -184,30 +223,45 @@
     total = parts_ref[0].astype(F32)
     for z in range(1, NZ):
         total = total + parts_ref[z].astype(F32)
-    gate_ref[...] = total[:, :FF].astype(BF)
-    up_ref[...] = total[:, FF : 2 * FF].astype(BF)
-    down_ref[:, : D // 2] = total[:FD, 2 * FF :].astype(BF)
-    down_ref[:, D // 2 :] = total[16 : 16 + FD, 2 * FF :].astype(BF)
-
-
-def combine_kernel(ids_ref, weights_ref, upstream_ref, home_ref, mixed_ref, tokens_ref, route_ref):
+    gate_ref[...] = total[:SH, :FF].astype(BF)
+    up_ref[...] = total[:SH, FF:].astype(BF)
+    tail = [total[SH + FD :, i * TW : (i + 1) * TW] for i in range(3)]
+    down_ref[:, :PW] = total[SH : SH + FD, :].astype(BF)
+    down_ref[:, PW:] = jnp.concatenate(tail, axis=0).astype(BF)
+
+
+def combine_kernel(
+    ids_ref, weights_ref, upstream_ref, home_ref, got_ref, mixed_ref, tokens_ref, route_ref, rows, sems
+):
+    core = lax.axis_index("expert") % 2
+    copies = [
+        pltpu.make_async_copy(home_ref.at[:, core], rows.at[0], sems.at[0]),
+        pltpu.make_async_copy(got_ref, rows.at[1], sems.at[1]),
+    ]
+    for copy in copies:
+        copy.start()
     live, weight, mask = place(ids_ref[...], weights_ref[...])
     picker = mask.astype(F32).astype(BF)
-    tokens_ref[...] = tn(picker, home_ref[:, D:]).astype(BF)
-    picked = tn(picker, home_ref[:, :D])
+    for copy in copies:
+        copy.wait()
+    home = rows[...].reshape(ROWS, 2 * D)
+    tokens_ref[...] = tn(picker, home[:, D:]).astype(BF)
+    picked = tn(picker, home[:, :D])
     mixed_ref[...] = (column_of(weight) * picked).astype(BF)
     inner = jnp.sum(upstream_ref[...].astype(F32) * picked, axis=1, keepdims=True)
     route_ref[...] = jnp.where(live, row_of(inner), 0.0)
 
 
-def call(kernel, outs, scratch=(), vmem=16 * MIB, flops=0, moved=MIB, spaces=None, any_outs=False):
+def call(kernel, outs, scratch=(), vmem=16 * MIB, flops=0, moved=MIB, spaces=None, out_spaces=None):
     shapes = [jax.ShapeDtypeStruct(s, t) for s, t in outs]
     single = len(shapes) == 1
     specs = {}
     if spaces is not None:
         specs["in_specs"] = [pl.BlockSpec(memory_space=a or pltpu.VMEM) for a in spaces]
-    if any_outs:
-        specs["out_specs"] = [pl.BlockSpec(memory_space=pl.ANY)] * len(outs)
+    if out_spaces is not None:
+        specs["out_specs"] = [pl.BlockSpec(memory_space=a) for a in out_spaces]
+        if single:
+            specs["out_specs"] = specs["out_specs"][0]
     return pl.pallas_call(
         kernel,
         out_shape=shapes[0] if single else shapes,
@@ -218,10 +272,12 @@
     )
 
 
+Z_GROUPS = [[z * NX + x for z in range(NZ)] for x in range(NX)]
+
+
 def swap_z(v):
-    groups = [[z * NX + x for z in range(NZ)] for x in range(NX)]
     return lax.all_to_all(
-        v, "dp", split_axis=0, concat_axis=0, tiled=True, axis_index_groups=groups
+        v, "dp", split_axis=0, concat_axis=0, tiled=True, axis_index_groups=Z_GROUPS
     )
 
 
@@ -230,34 +286,51 @@
     return lax.ppermute(v, "dp", pairs)
 
 
+NY = FLIGHT // 2
+Y_GROUPS = [[2 * y + core for y in range(NY)] for core in range(2)]
+
+
+def swap_core(v):
+    return lax.ppermute(v, "expert", [(i, i ^ 1) for i in range(FLIGHT)])
+
+
 def exchange(v):
-    v = v.reshape(FLIGHT, CAP, 2 * D)
-    return lax.all_to_all(v, "expert", split_axis=0, concat_axis=0, tiled=True).reshape(ROWS, 2 * D)
+    return lax.all_to_all(
+        v, "expert", split_axis=0, concat_axis=0, tiled=True, axis_index_groups=Y_GROUPS
+    )
 
 
 def on_device(tokens, route_ids, route_weights, upstream, w_gate, w_up, w_down):
     ids_t, weights_t = route_ids.T, route_weights.T
-    shard = pltpu.VMEM((SH, FF), BF)
+    held = pltpu.VMEM((SH, FF), BF)
     copies = call(
         pack_kernel,
-        [((NZ, SH, PW), BF)],
-        scratch=[shard, shard, pltpu.SemaphoreType.DMA((2,))],
+        [((NZ, PH, PW), BF)],
+        scratch=[held, held, pltpu.SemaphoreType.DMA((2,))],
         vmem=58 * MIB,
         spaces=(pl.ANY, pl.ANY, None),
     )(w_gate[0], w_up[0], w_down[0])
+    both, one = ((NY, 2, CAP, 2 * D), BF), ((NY, CAP, 2 * D), BF)
+    keep, give = call(
+        dispatch_kernel, [((ROWS // 2, 2 * D), BF)] * 2, vmem=58 * MIB, flops=4 * ROWS * TOK * D
+    )(ids_t, weights_t, tokens, upstream)
+    sent = call(
+        merge_kernel,
+        [both],
+        scratch=[pltpu.SemaphoreType.DMA((2,))],
+        spaces=(pl.ANY, pl.ANY),
+        out_spaces=(pl.ANY,),
+    )(keep.reshape(one[0]), swap_core(give).reshape(one[0]))
     own = swap_z(copies)
-    sent = call(dispatch_kernel, [((ROWS, 2 * D), BF)], flops=4 * ROWS * TOK * D)(
-        ids_t, weights_t, tokens, upstream
-    )
-    recv = exchange(sent)
+    recv = exchange(sent).reshape(ROWS, 2 * D)
     half = NZ // 2
     low, high = own[:half], own[half:]
     left_lo, right_hi = shift_x(low, 1), shift_x(high, NX - 1)
     left_hi, right_lo = shift_x(high, 1), shift_x(low, NX - 1)
     far_lo, far_hi = shift_x(left_lo, 1), shift_x(right_hi, NX - 1)
-    whole, part = ((NZ, SH, PW), BF), ((half, SH, PW), BF)
+    whole, part = ((NZ, PH, PW), BF), ((half, PH, PW), BF)
     tile = pltpu.VMEM((ROWS, 2 * D), BF)
-    matrix = pltpu.VMEM((NZ, NX, SH, PW), BF)
+    matrix = pltpu.VMEM((NZ, NX, PH, PW), BF)
     back, q_own, q_right_lo, q_right_hi, q_left_lo, q_left_hi, q_far_lo, q_far_hi = call(
         expert_kernel,
         [((ROWS, 2 * D), BF), whole] + [part] * 6,
@@ -266,12 +339,12 @@
         flops=18 * ROWS * D * FF,
         moved=8 * MIB,
         spaces=(pl.ANY,) * 2,
-        any_outs=True,
+        out_spaces=(pl.ANY,) * 8,
     )(
         recv,
         jnp.concatenate([own, left_lo, right_hi, left_hi, right_lo, far_lo, far_hi], axis=0),
     )
-    home = exchange(back)
+    home = exchange(back.reshape(both[0]))
     add_lo, add_hi = shift_x(q_far_lo, 1), shift_x(q_far_hi, NX - 1)
     from_left_hi, from_right_lo = shift_x(q_right_hi, 1), shift_x(q_left_lo, NX - 1)
     to_right, to_left = call(add_far_kernel, [part, part], moved=2 * MIB)(
@@ -280,6 +353,15 @@
     from_left_lo, from_right_hi = shift_x(to_right, 1), shift_x(to_left, NX - 1)
     total = call(sum_x_kernel, [whole], moved=3 * MIB, spaces=(None,) * 5 + (pl.ANY,))(
         q_own, from_left_lo, from_left_hi, from_right_lo, from_right_hi, home
+    )
+    got = swap_core(
+        call(
+            give_kernel,
+            [one],
+            scratch=[pltpu.SemaphoreType.DMA],
+            spaces=(pl.ANY, pl.ANY),
+            out_spaces=(pl.ANY,),
+        )(home, total)
     )
     parts = swap_z(total)
     grad_gate, grad_up, grad_down = call(
@@ -288,9 +370,11 @@
     mixed, grad_tokens, grad_route = call(
         combine_kernel,
         [((TOK, D), BF), ((TOK, D), BF), ((8, TOK), F32)],
+        scratch=[pltpu.VMEM((2,) + one[0], BF), pltpu.SemaphoreType.DMA((2,))],
         flops=4 * ROWS * TOK * D,
         moved=2 * MIB,
-    )(ids_t, weights_t, upstream, home)
+        spaces=(None, None, None, pl.ANY, pl.ANY),
+    )(ids_t, weights_t, upstream, home, got)
     return (mixed, grad_tokens, grad_route.T, grad_gate[None], grad_up[None], grad_down[None])
 
 

time: 141 us -> 134 us (0.950)
  the two profiles are of different devices: /device:TPU:7 before, /device:TPU:3 now
where the time goes in v3:
time: 134 us; the launch traced here: 133 us
  starting transfers between devices  63.5 us (47%)
  waiting for transfers between devices  45.9 us (34%)
  Pallas kernels  16.3 us (12%)
  local copies, waits for them, and re-layouts  6.32 us (5%)
    ppermute x12, starting transfers between devices, shift_x(): return lax.ppermute(v, 'dp', pairs)  34.2 us
    all_to_all x2, waiting for transfers between devices, swap_z(): lax.all_to_all(v, 'dp', split_axis=0, concat_axis=0, tiled=True, axis_ind...  24 us
    all_to_all x2, starting transfers between devices, swap_z(): lax.all_to_all(v, 'dp', split_axis=0, concat_axis=0, tiled=True, axis_ind...  13.7 us
    ppermute x12, waiting for transfers between devices, shift_x(): return lax.ppermute(v, 'dp', pairs)  10.8 us
    all_to_all x2, starting transfers between devices, exchange(): lax.all_to_all(v, 'expert', split_axis=0, concat_axis=0, tiled=True, axis...  10.4 us
    all_to_all x2, waiting for transfers between devices, exchange(): lax.all_to_all(v, 'expert', split_axis=0, concat_axis=0, tiled=True, axis...  7.87 us
    pallas_call x1, Pallas kernels, on_device(): call(expert_kernel, [((ROWS, 2 * D), BF), whole] + [part] * 6, scratch=[t...  7.03 us
    unnamed x14, local copies, waits for them, and re-layouts  5.55 us
  transfers between devices with their start and end apart: 18, of which 11 were waited for; matrix products, arithmetic and copies ran while one was open for 4% of the time, Pallas kernels for 4%

profile of v3, /device:TPU:3, one launch (start us, length us, event | category | flops | bytes accessed | tf_op | source)
XLA Modules:
  0.0 132.9 jit_solution(7117771082965392629)
XLA Ops:
  0.6 2.4 %shard_map.120 = bf16[8,48,768]{2,1,0:T(8,128)(2,1)} custom-call(bf16[32,384]{1,0:T(8,128)(2,1)} %bitcast.21, bf16[32,384]{1,0:T(8,128)(2,1)} %bitcast.22, bf16[12,1024]{1,0:T(8,128)(2,1)} %bitcast.20), custom_call_target="tpu_custom_call" | custom-call | bytes 1048576 | tf_op jit(solution)/shard_map/pallas_call | solution.py:306
  3.0 10.0 %all-to-all-start.1 = ((bf16[8,48,768]{2,1,0:T(8,128)(2,1)}), bf16[8,48,768]{2,1,0:T(8,128)(2,1)S(1)}, u32[]{:S(2)}, u32[]{:S(2)}) async-start(bf16[8,48,768]{2,1,0:T(8,128)(2,1)} %shard_map.120), calls=%async_computation.1 | async-start | bytes 1179648 | tf_op jit(solution)/shard_map/all_to_all | solution.py:279
  13.1 2.6 %shard_map.118 = (bf16[128,2048]{1,0:T(8,128)(2,1)}, bf16[128,2048]{1,0:T(8,128)(2,1)}) custom-call(s32[8,128]{1,0:T(8,128)} %bitcast.16, f32[8,128]{1,0:T(8,128)} %bitcast.18, bf16[128,1024]{1,0:T(8,128)(2,1)} %tokens_ref.1, bf16[128,1024]{1,0:T(8,128)(2,1)} %upstream_ref.3), custom_call_target="tpu_custom_call" | custom-call | flops 134217728 | bytes 1048576 | tf_op jit(solution)/shard_map/pallas_call | solution.py:314
  15.7 2.9 %collective-permute-start = (bf16[128,2048]{1,0:T(8,128)(2,1)}, bf16[128,2048]{1,0:T(8,128)(2,1)S(1)}, u32[]{:S(2)}, u32[]{:S(2)}) collective-permute-start(bf16[128,2048]{1,0:T(8,128)(2,1)} %get-tuple-element.25), channel_id=1, source_target_pairs={{0,1},{1,0},{2,3},{3,2},{4,5},{5,4},{6,7},{7,6},{8,9},{9,8},{10,11... | collective-permute-start | bytes 1572872 | tf_op jit(solution)/shard_map/ppermute | solution.py:294
  18.5 1.7 %collective-permute-done = bf16[128,2048]{1,0:T(8,128)(2,1)S(1)} collective-permute-done((bf16[128,2048]{1,0:T(8,128)(2,1)}, bf16[128,2048]{1,0:T(8,128)(2,1)S(1)}, u32[]{:S(2)}, u32[]{:S(2)}) %collective-permute-start) | collective-permute-done | bytes 524320 | tf_op jit(solution)/shard_map/ppermute | solution.py:294
  20.3 1.0 copy-done.1
  22.3 10.1 %all-to-all-done.1 = bf16[8,48,768]{2,1,0:T(8,128)(2,1)S(1)} async-done(((bf16[8,48,768]{2,1,0:T(8,128)(2,1)}), bf16[8,48,768]{2,1,0:T(8,128)(2,1)S(1)}, u32[]{:S(2)}, u32[]{:S(2)}) %all-to-all-start.1) | async-done | bytes 589856 | tf_op jit(solution)/shard_map/all_to_all | solution.py:279
  32.4 6.8 %all-to-all-start = ((bf16[8,2,16,2048]{3,2,1,0:T(8,128)(2,1)}), bf16[8,2,16,2048]{3,2,1,0:T(8,128)(2,1)S(1)}, u32[]{:S(2)}, u32[]{:S(2)}) async-start(bf16[8,2,16,2048]{3,2,1,0:T(8,128)(2,1)} %shard_map.119), calls=%async_computation | async-start | bytes 2097152 | tf_op jit(solution)/shard_map/all_to_all | solution.py:298
  39.3 3.1 %collective-permute-start.1 = (bf16[4,48,768]{2,1,0:T(8,128)(2,1)S(1)}, bf16[4,48,768]{2,1,0:T(8,128)(2,1)S(1)}, u32[]{:S(2)}, u32[]{:S(2)}) collective-permute-start(bf16[4,48,768]{2,1,0:T(8,128)(2,1)S(1)} %get-tuple-element.43), channel_id=1, source_target_pairs={{0,16},{16,32},{32,48},{48,0},{64,80},{80,96},{96,112},{112,64},{1... | collective-permute-start | bytes 884744 | tf_op jit(solution)/shard_map/ppermute | solution.py:286
  42.4 2.2 %collective-permute-start.2 = (bf16[4,48,768]{2,1,0:T(8,128)(2,1)S(1)}, bf16[4,48,768]{2,1,0:T(8,128)(2,1)S(1)}, u32[]{:S(2)}, u32[]{:S(2)}) collective-permute-start(bf16[4,48,768]{2,1,0:T(8,128)(2,1)S(1)} %get-tuple-element.42), channel_id=1, source_target_pairs={{0,48},{16,0},{32,16},{48,32},{64,112},{80,64},{96,80},{112,96},{1... | collective-permute-start | bytes 884744 | tf_op jit(solution)/shard_map/ppermute | solution.py:286
  44.6 3.1 %collective-permute-start.3 = (bf16[4,48,768]{2,1,0:T(8,128)(2,1)S(1)}, bf16[4,48,768]{2,1,0:T(8,128)(2,1)S(1)}, u32[]{:S(2)}, u32[]{:S(2)}) collective-permute-start(bf16[4,48,768]{2,1,0:T(8,128)(2,1)S(1)} %get-tuple-element.42), channel_id=1, source_target_pairs={{0,16},{16,32},{32,48},{48,0},{64,80},{80,96},{96,112},{112,64},{1... | collective-permute-start | bytes 884744 | tf_op jit(solution)/shard_map/ppermute | solution.py:286
  47.7 2.2 %collective-permute-start.4 = (bf16[4,48,768]{2,1,0:T(8,128)(2,1)S(1)}, bf16[4,48,768]{2,1,0:T(8,128)(2,1)S(1)}, u32[]{:S(2)}, u32[]{:S(2)}) collective-permute-start(bf16[4,48,768]{2,1,0:T(8,128)(2,1)S(1)} %get-tuple-element.43), channel_id=1, source_target_pairs={{0,48},{16,0},{32,16},{48,32},{64,112},{80,64},{96,80},{112,96},{1... | collective-permute-start | bytes 884744 | tf_op jit(solution)/shard_map/ppermute | solution.py:286
  50.7 3.1 %collective-permute-start.5 = (bf16[4,48,768]{2,1,0:T(8,128)(2,1)S(1)}, bf16[4,48,768]{2,1,0:T(8,128)(2,1)S(1)}, u32[]{:S(2)}, u32[]{:S(2)}) collective-permute-start(bf16[4,48,768]{2,1,0:T(8,128)(2,1)S(1)} %collective-permute-done.1), channel_id=1, source_target_pairs={{0,16},{16,32},{32,48},{48,0},{64,80},{80,96},{96,112},{112,64},{1... | collective-permute-start | bytes 884744 | tf_op jit(solution)/shard_map/ppermute | solution.py:286
  54.6 3.4 %collective-permute-start.6 = (bf16[4,48,768]{2,1,0:T(8,128)(2,1)S(1)}, bf16[4,48,768]{2,1,0:T(8,128)(2,1)S(1)}, u32[]{:S(2)}, u32[]{:S(2)}) collective-permute-start(bf16[4,48,768]{2,1,0:T(8,128)(2,1)S(1)} %collective-permute-done.2), channel_id=1, source_target_pairs={{0,48},{16,0},{32,16},{48,32},{64,112},{80,64},{96,80},{112,96},{1... | collective-permute-start | bytes 884744 | tf_op jit(solution)/shard_map/ppermute | solution.py:286
  61.5 2.3 %collective-permute-done.6 = bf16[4,48,768]{2,1,0:T(8,128)(2,1)S(1)} collective-permute-done((bf16[4,48,768]{2,1,0:T(8,128)(2,1)S(1)}, bf16[4,48,768]{2,1,0:T(8,128)(2,1)S(1)}, u32[]{:S(2)}, u32[]{:S(2)}) %collective-permute-start.6) | collective-permute-done | bytes 294944 | tf_op jit(solution)/shard_map/ppermute | solution.py:286
  64.5 4.0 %all-to-all-done = bf16[8,2,16,2048]{3,2,1,0:T(8,128)(2,1)S(1)} async-done(((bf16[8,2,16,2048]{3,2,1,0:T(8,128)(2,1)}), bf16[8,2,16,2048]{3,2,1,0:T(8,128)(2,1)S(1)}, u32[]{:S(2)}, u32[]{:S(2)}) %all-to-all-start) | async-done | bytes 1048608 | tf_op jit(solution)/shard_map/all_to_all | solution.py:298
  68.5 7.0 %shard_map.121 = (bf16[256,2048]{1,0:T(8,128)(2,1)}, bf16[8,48,768]{2,1,0:T(8,128)(2,1)S(1)}, bf16[4,48,768]{2,1,0:T(8,128)(2,1)S(1)}, bf16[4,48,768]{2,1,0:T(8,...) custom-call(bf16[256,2048]{1,0:T(8,128)(2,1)S(1)} %bitcast.13, ...), custom_call_target="tpu_custom_call" | custom-call | flops 1811939328 | bytes 8388608 | tf_op jit(solution)/shard_map/pallas_call | solution.py:334
  75.5 3.6 %all-to-all-start.2 = ((bf16[8,2,16,2048]{3,2,1,0:T(8,128)(2,1)}), bf16[8,2,16,2048]{3,2,1,0:T(8,128)(2,1)S(1)}, u32[]{:S(2)}, u32[]{:S(2)}) async-start(bf16[8,2,16,2048]{3,2,1,0:T(8,128)(2,1)} %bitcast.8), calls=%async_computation.2 | async-start | bytes 2097152 | tf_op jit(solution)/shard_map/all_to_all | solution.py:298
  79.1 3.1 %collective-permute-start.7 = (bf16[4,48,768]{2,1,0:T(8,128)(2,1)}, bf16[4,48,768]{2,1,0:T(8,128)(2,1)S(1)}, u32[]{:S(2)}, u32[]{:S(2)}) collective-permute-start(bf16[4,48,768]{2,1,0:T(8,128)(2,1)} %get-tuple-element.30), channel_id=1, source_target_pairs={{0,16},{16,32},{32,48},{48,0},{64,80},{80,96},{96,112},{112,64},{1... | collective-permute-start | bytes 884744 | tf_op jit(solution)/shard_map/ppermute | solution.py:286
  82.2 2.2 %collective-permute-start.8 = (bf16[4,48,768]{2,1,0:T(8,128)(2,1)}, bf16[4,48,768]{2,1,0:T(8,128)(2,1)S(1)}, u32[]{:S(2)}, u32[]{:S(2)}) collective-permute-start(bf16[4,48,768]{2,1,0:T(8,128)(2,1)} %get-tuple-element.31), channel_id=1, source_target_pairs={{0,48},{16,0},{32,16},{48,32},{64,112},{80,64},{96,80},{112,96},{1... | collective-permute-start | bytes 884744 | tf_op jit(solution)/shard_map/ppermute | solution.py:286
  84.4 3.1 %collective-permute-start.10 = (bf16[4,48,768]{2,1,0:T(8,128)(2,1)S(1)}, bf16[4,48,768]{2,1,0:T(8,128)(2,1)S(1)}, u32[]{:S(2)}, u32[]{:S(2)}) collective-permute-start(bf16[4,48,768]{2,1,0:T(8,128)(2,1)S(1)} %get-tuple-element.33), channel_id=1, source_target_pairs={{0,16},{16,32},{32,48},{48,0},{64,80},{80,96},{96,112},{112,64},{1... | collective-permute-start | bytes 884744 | tf_op jit(solution)/shard_map/ppermute | solution.py:286
  87.5 2.4 %collective-permute-start.11 = (bf16[4,48,768]{2,1,0:T(8,128)(2,1)S(1)}, bf16[4,48,768]{2,1,0:T(8,128)(2,1)S(1)}, u32[]{:S(2)}, u32[]{:S(2)}) collective-permute-start(bf16[4,48,768]{2,1,0:T(8,128)(2,1)S(1)} %get-tuple-element.34), channel_id=1, source_target_pairs={{0,48},{16,0},{32,16},{48,32},{64,112},{80,64},{96,80},{112,96},{1... | collective-permute-start | bytes 884744 | tf_op jit(solution)/shard_map/ppermute | solution.py:286
  90.3 4.4 %collective-permute-start.12 = (bf16[4,48,768]{2,1,0:T(8,128)(2,1)S(1)}, bf16[4,48,768]{2,1,0:T(8,128)(2,1)S(1)}, u32[]{:S(2)}, u32[]{:S(2)}) collective-permute-start(bf16[4,48,768]{2,1,0:T(8,128)(2,1)S(1)} %get-tuple-element.35), channel_id=1, source_target_pairs={{0,48},{16,0},{32,16},{48,32},{64,112},{80,64},{96,80},{112,96},{1... | collective-permute-start | bytes 884744 | tf_op jit(solution)/shard_map/ppermute | solution.py:286
  94.7 1.9 %collective-permute-start.9 = (bf16[4,48,768]{2,1,0:T(8,128)(2,1)S(1)}, bf16[4,48,768]{2,1,0:T(8,128)(2,1)S(1)}, u32[]{:S(2)}, u32[]{:S(2)}) collective-permute-start(bf16[4,48,768]{2,1,0:T(8,128)(2,1)S(1)} %get-tuple-element.32), channel_id=1, source_target_pairs={{0,16},{16,32},{32,48},{48,0},{64,80},{80,96},{96,112},{112,64},{1... | collective-permute-start | bytes 884744 | tf_op jit(solution)/shard_map/ppermute | solution.py:286
  96.7 1.3 %collective-permute-done.11.right_lo = bf16[4,48,768]{2,1,0:T(8,128)(2,1)S(1)} collective-permute-done((bf16[4,48,768]{2,1,0:T(8,128)(2,1)S(1)}, bf16[4,48,768]{2,1,0:T(8,128)(2,1)S(1)}, u32[]{:S(2)}, u32[]{:S(2)}) %collective-permute-start.11) | collective-permute-done | bytes 294944 | tf_op jit(solution)/shard_map/ppermute | solution.py:286
  98.0 6.3 %collective-permute-done.12.right_hi = bf16[4,48,768]{2,1,0:T(8,128)(2,1)S(1)} collective-permute-done((bf16[4,48,768]{2,1,0:T(8,128)(2,1)S(1)}, bf16[4,48,768]{2,1,0:T(8,128)(2,1)S(1)}, u32[]{:S(2)}, u32[]{:S(2)}) %collective-permute-start.12) | collective-permute-done | bytes 294944 | tf_op jit(solution)/shard_map/ppermute | solution.py:286
  104.3 3.9 %all-to-all-done.2.after_ref.home_ref = bf16[8,2,16,2048]{3,2,1,0:T(8,128)(2,1)S(1)} async-done(((bf16[8,2,16,2048]{3,2,1,0:T(8,128)(2,1)}), bf16[8,2,16,2048]{3,2,1,0:T(8,128)(2,1)S(1)}, u32[]{:S(2)}, u32[]{:S(2)}) %all-to-all-start.2) | async-done | bytes 1048608 | tf_op jit(solution)/shard_map/all_to_all | solution.py:298
  109.2 3.7 %all-to-all-start.3 = ((bf16[8,48,768]{2,1,0:T(8,128)(2,1)}), bf16[8,48,768]{2,1,0:T(8,128)(2,1)S(1)}, u32[]{:S(2)}, u32[]{:S(2)}) async-start(bf16[8,48,768]{2,1,0:T(8,128)(2,1)} %shard_map.123.after_ref), calls=%async_computation.3 | async-start | bytes 1179648 | tf_op jit(solution)/shard_map/all_to_all | solution.py:279
  113.0 2.4 %collective-permute-start.13 = (bf16[8,16,2048]{2,1,0:T(8,128)(2,1)S(1)}, bf16[8,16,2048]{2,1,0:T(8,128)(2,1)S(1)}, u32[]{:S(2)}, u32[]{:S(2)}) collective-permute-start(bf16[8,16,2048]{2,1,0:T(8,128)(2,1)S(1)} %shard_map.124), channel_id=1, source_target_pairs={{0,1},{1,0},{2,3},{3,2},{4,5},{5,4},{6,7},{7,6},{8,9},{9,8},{10,11... | collective-permute-start | bytes 1572872 | tf_op jit(solution)/shard_map/ppermute | solution.py:294
  115.4 1.5 %collective-permute-done.13.got_ref = bf16[8,16,2048]{2,1,0:T(8,128)(2,1)S(1)} collective-permute-done((bf16[8,16,2048]{2,1,0:T(8,128)(2,1)S(1)}, bf16[8,16,2048]{2,1,0:T(8,128)(2,1)S(1)}, u32[]{:S(2)}, u32[]{:S(2)}) %collective-permute-start.13) | collective-permute-done | bytes 524320 | tf_op jit(solution)/shard_map/ppermute | solution.py:294
  116.9 1.4 %shard_map.125 = (bf16[128,1024]{1,0:T(8,128)(2,1)}, bf16[128,1024]{1,0:T(8,128)(2,1)}, f32[8,128]{1,0:T(8,128)}) custom-call(s32[8,128]{1,0:T(8,128)S(1)} %bitcast.17, f32[8,128]{1,0:T(8,128)S(1)} %bitcast.19, bf16[128,1024]{1,0:T(8,128)(2,1)S(1)} %copy-done, bf16[8,2,16,2048]{3,2,1,0:T(8,128)(2,1)S(1)} %all-to-all-done.2.after_ref.home_ref, ...), custom_call_target="tpu_custom_call" | custom-call | flops 134217728 | bytes 2097152 | tf_op jit(solution)/shard_map/pallas_call | solution.py:370
  118.3 13.9 %all-to-all-done.3.parts_ref = bf16[8,48,768]{2,1,0:T(8,128)(2,1)S(1)} async-done(((bf16[8,48,768]{2,1,0:T(8,128)(2,1)}), bf16[8,48,768]{2,1,0:T(8,128)(2,1)S(1)}, u32[]{:S(2)}, u32[]{:S(2)}) %all-to-all-start.3) | async-done | bytes 589856 | tf_op jit(solution)/shard_map/all_to_all | solution.py:279
  (29 shorter events, 9.0 us)
Async XLA Ops:
  3.0 29.4 %all-to-all-start.1 = ((bf16[8,48,768]{2,1,0:T(8,128)(2,1)}), bf16[8,48,768]{2,1,0:T(8,128)(2,1)S(1)}, u32[]{:S(2)}, u32[]{:S(2)}) async-start(bf16[8,48,768]{2,1,0:T(8,128)(2,1)} %shard_map.120), calls=%async_computation.1 | async-start | bytes 1179648 | tf_op jit(solution)/shard_map/all_to_all | solution.py:279
  15.7 4.6 %collective-permute-start = (bf16[128,2048]{1,0:T(8,128)(2,1)}, bf16[128,2048]{1,0:T(8,128)(2,1)S(1)}, u32[]{:S(2)}, u32[]{:S(2)}) collective-permute-start(bf16[128,2048]{1,0:T(8,128)(2,1)} %get-tuple-element.25), channel_id=1, source_target_pairs={{0,1},{1,0},{2,3},{3,2},{4,5},{5,4},{6,7},{7,6},{8,9},{9,8},{10,11... | collective-permute-start | bytes 1572872 | tf_op jit(solution)/shard_map/ppermute | solution.py:294
  20.3 1.0 copy-start.1
  32.4 36.1 %all-to-all-start = ((bf16[8,2,16,2048]{3,2,1,0:T(8,128)(2,1)}), bf16[8,2,16,2048]{3,2,1,0:T(8,128)(2,1)S(1)}, u32[]{:S(2)}, u32[]{:S(2)}) async-start(bf16[8,2,16,2048]{3,2,1,0:T(8,128)(2,1)} %shard_map.119), calls=%async_computation | async-start | bytes 2097152 | tf_op jit(solution)/shard_map/all_to_all | solution.py:298
  39.3 11.5 %collective-permute-start.1 = (bf16[4,48,768]{2,1,0:T(8,128)(2,1)S(1)}, bf16[4,48,768]{2,1,0:T(8,128)(2,1)S(1)}, u32[]{:S(2)}, u32[]{:S(2)}) collective-permute-start(bf16[4,48,768]{2,1,0:T(8,128)(2,1)S(1)} %get-tuple-element.43), channel_id=1, source_target_pairs={{0,16},{16,32},{32,48},{48,0},{64,80},{80,96},{96,112},{112,64},{1... | collective-permute-start | bytes 884744 | tf_op jit(solution)/shard_map/ppermute | solution.py:286
  42.4 12.2 %collective-permute-start.2 = (bf16[4,48,768]{2,1,0:T(8,128)(2,1)S(1)}, bf16[4,48,768]{2,1,0:T(8,128)(2,1)S(1)}, u32[]{:S(2)}, u32[]{:S(2)}) collective-permute-start(bf16[4,48,768]{2,1,0:T(8,128)(2,1)S(1)} %get-tuple-element.42), channel_id=1, source_target_pairs={{0,48},{16,0},{32,16},{48,32},{64,112},{80,64},{96,80},{112,96},{1... | collective-permute-start | bytes 884744 | tf_op jit(solution)/shard_map/ppermute | solution.py:286
  44.6 14.1 %collective-permute-start.3 = (bf16[4,48,768]{2,1,0:T(8,128)(2,1)S(1)}, bf16[4,48,768]{2,1,0:T(8,128)(2,1)S(1)}, u32[]{:S(2)}, u32[]{:S(2)}) collective-permute-start(bf16[4,48,768]{2,1,0:T(8,128)(2,1)S(1)} %get-tuple-element.42), channel_id=1, source_target_pairs={{0,16},{16,32},{32,48},{48,0},{64,80},{80,96},{96,112},{112,64},{1... | collective-permute-start | bytes 884744 | tf_op jit(solution)/shard_map/ppermute | solution.py:286
  47.7 11.7 %collective-permute-start.4 = (bf16[4,48,768]{2,1,0:T(8,128)(2,1)S(1)}, bf16[4,48,768]{2,1,0:T(8,128)(2,1)S(1)}, u32[]{:S(2)}, u32[]{:S(2)}) collective-permute-start(bf16[4,48,768]{2,1,0:T(8,128)(2,1)S(1)} %get-tuple-element.43), channel_id=1, source_target_pairs={{0,48},{16,0},{32,16},{48,32},{64,112},{80,64},{96,80},{112,96},{1... | collective-permute-start | bytes 884744 | tf_op jit(solution)/shard_map/ppermute | solution.py:286
  50.7 10.0 %collective-permute-start.5 = (bf16[4,48,768]{2,1,0:T(8,128)(2,1)S(1)}, bf16[4,48,768]{2,1,0:T(8,128)(2,1)S(1)}, u32[]{:S(2)}, u32[]{:S(2)}) collective-permute-start(bf16[4,48,768]{2,1,0:T(8,128)(2,1)S(1)} %collective-permute-done.1), channel_id=1, source_target_pairs={{0,16},{16,32},{32,48},{48,0},{64,80},{80,96},{96,112},{112,64},{1... | collective-permute-start | bytes 884744 | tf_op jit(solution)/shard_map/ppermute | solution.py:286
  54.6 9.2 %collective-permute-start.6 = (bf16[4,48,768]{2,1,0:T(8,128)(2,1)S(1)}, bf16[4,48,768]{2,1,0:T(8,128)(2,1)S(1)}, u32[]{:S(2)}, u32[]{:S(2)}) collective-permute-start(bf16[4,48,768]{2,1,0:T(8,128)(2,1)S(1)} %collective-permute-done.2), channel_id=1, source_target_pairs={{0,48},{16,0},{32,16},{48,32},{64,112},{80,64},{96,80},{112,96},{1... | collective-permute-start | bytes 884744 | tf_op jit(solution)/shard_map/ppermute | solution.py:286
  75.5 32.7 %all-to-all-start.2 = ((bf16[8,2,16,2048]{3,2,1,0:T(8,128)(2,1)}), bf16[8,2,16,2048]{3,2,1,0:T(8,128)(2,1)S(1)}, u32[]{:S(2)}, u32[]{:S(2)}) async-start(bf16[8,2,16,2048]{3,2,1,0:T(8,128)(2,1)} %bitcast.8), calls=%async_computation.2 | async-start | bytes 2097152 | tf_op jit(solution)/shard_map/all_to_all | solution.py:298
  79.1 10.9 %collective-permute-start.7 = (bf16[4,48,768]{2,1,0:T(8,128)(2,1)}, bf16[4,48,768]{2,1,0:T(8,128)(2,1)S(1)}, u32[]{:S(2)}, u32[]{:S(2)}) collective-permute-start(bf16[4,48,768]{2,1,0:T(8,128)(2,1)} %get-tuple-element.30), channel_id=1, source_target_pairs={{0,16},{16,32},{32,48},{48,0},{64,80},{80,96},{96,112},{112,64},{1... | collective-permute-start | bytes 884744 | tf_op jit(solution)/shard_map/ppermute | solution.py:286
  82.2 8.0 %collective-permute-start.8 = (bf16[4,48,768]{2,1,0:T(8,128)(2,1)}, bf16[4,48,768]{2,1,0:T(8,128)(2,1)S(1)}, u32[]{:S(2)}, u32[]{:S(2)}) collective-permute-start(bf16[4,48,768]{2,1,0:T(8,128)(2,1)} %get-tuple-element.31), channel_id=1, source_target_pairs={{0,48},{16,0},{32,16},{48,32},{64,112},{80,64},{96,80},{112,96},{1... | collective-permute-start | bytes 884744 | tf_op jit(solution)/shard_map/ppermute | solution.py:286
  84.4 12.3 %collective-permute-start.10 = (bf16[4,48,768]{2,1,0:T(8,128)(2,1)S(1)}, bf16[4,48,768]{2,1,0:T(8,128)(2,1)S(1)}, u32[]{:S(2)}, u32[]{:S(2)}) collective-permute-start(bf16[4,48,768]{2,1,0:T(8,128)(2,1)S(1)} %get-tuple-element.33), channel_id=1, source_target_pairs={{0,16},{16,32},{32,48},{48,0},{64,80},{80,96},{96,112},{112,64},{1... | collective-permute-start | bytes 884744 | tf_op jit(solution)/shard_map/ppermute | solution.py:286
  87.5 10.5 %collective-permute-start.11 = (bf16[4,48,768]{2,1,0:T(8,128)(2,1)S(1)}, bf16[4,48,768]{2,1,0:T(8,128)(2,1)S(1)}, u32[]{:S(2)}, u32[]{:S(2)}) collective-permute-start(bf16[4,48,768]{2,1,0:T(8,128)(2,1)S(1)} %get-tuple-element.34), channel_id=1, source_target_pairs={{0,48},{16,0},{32,16},{48,32},{64,112},{80,64},{96,80},{112,96},{1... | collective-permute-start | bytes 884744 | tf_op jit(solution)/shard_map/ppermute | solution.py:286
  90.3 14.0 %collective-permute-start.12 = (bf16[4,48,768]{2,1,0:T(8,128)(2,1)S(1)}, bf16[4,48,768]{2,1,0:T(8,128)(2,1)S(1)}, u32[]{:S(2)}, u32[]{:S(2)}) collective-permute-start(bf16[4,48,768]{2,1,0:T(8,128)(2,1)S(1)} %get-tuple-element.35), channel_id=1, source_target_pairs={{0,48},{16,0},{32,16},{48,32},{64,112},{80,64},{96,80},{112,96},{1... | collective-permute-start | bytes 884744 | tf_op jit(solution)/shard_map/ppermute | solution.py:286
  94.7 9.6 %collective-permute-start.9 = (bf16[4,48,768]{2,1,0:T(8,128)(2,1)S(1)}, bf16[4,48,768]{2,1,0:T(8,128)(2,1)S(1)}, u32[]{:S(2)}, u32[]{:S(2)}) collective-permute-start(bf16[4,48,768]{2,1,0:T(8,128)(2,1)S(1)} %get-tuple-element.32), channel_id=1, source_target_pairs={{0,16},{16,32},{32,48},{48,0},{64,80},{80,96},{96,112},{112,64},{1... | collective-permute-start | bytes 884744 | tf_op jit(solution)/shard_map/ppermute | solution.py:286
  109.2 7.7 %copy-start = (bf16[128,1024]{1,0:T(8,128)(2,1)S(1)}, bf16[128,1024]{1,0:T(8,128)(2,1)}, u32[]{:S(2)}) copy-start(bf16[128,1024]{1,0:T(8,128)(2,1)} %upstream_ref.3) | copy-start | bytes 786436
  109.2 7.7 %copy-start.2 = (s32[128,8]{0,1:T(8,128)S(1)}, s32[128,8]{0,1:T(8,128)}, u32[]{:S(2)}) copy-start(s32[128,8]{0,1:T(8,128)} %param.8) | copy-start | bytes 12292
  109.2 7.7 %copy-start.3 = (f32[128,8]{0,1:T(8,128)S(1)}, f32[128,8]{0,1:T(8,128)}, u32[]{:S(2)}) copy-start(f32[128,8]{0,1:T(8,128)} %param.9) | copy-start | bytes 12292
  109.2 23.0 %all-to-all-start.3 = ((bf16[8,48,768]{2,1,0:T(8,128)(2,1)}), bf16[8,48,768]{2,1,0:T(8,128)(2,1)S(1)}, u32[]{:S(2)}, u32[]{:S(2)}) async-start(bf16[8,48,768]{2,1,0:T(8,128)(2,1)} %shard_map.123.after_ref), calls=%async_computation.3 | async-start | bytes 1179648 | tf_op jit(solution)/shard_map/all_to_all | solution.py:279
  113.0 3.9 %collective-permute-start.13 = (bf16[8,16,2048]{2,1,0:T(8,128)(2,1)S(1)}, bf16[8,16,2048]{2,1,0:T(8,128)(2,1)S(1)}, u32[]{:S(2)}, u32[]{:S(2)}) collective-permute-start(bf16[8,16,2048]{2,1,0:T(8,128)(2,1)S(1)} %shard_map.124), channel_id=1, source_target_pairs={{0,1},{1,0},{2,3},{3,2},{4,5},{5,4},{6,7},{7,6},{8,9},{9,8},{10,11... | collective-permute-start | bytes 1572872 | tf_op jit(solution)/shard_map/ppermute | solution.py:294

commit v4 on v3

--- a/solution.py
+++ b/solution.py
@@ -17,7 +17,6 @@
 SH = D // (NZ * NX)
 PW = 2 * FF
 PH = SH + 16
-DN = 16 * NZ * NX
 TW = D - PW
 STACK = FD // 3
 BF = jnp.bfloat16
@@ -77,36 +76,31 @@
     return jnp.sum(jnp.where(eye, column, 0.0), axis=0, keepdims=True)
 
 
-def pack_kernel(gate_ref, up_ref, down_ref, out_ref, gate, up, sems):
-    copies = [
-        pltpu.make_async_copy(gate_ref, gate, sems.at[0]),
-        pltpu.make_async_copy(up_ref, up, sems.at[1]),
-    ]
-    for copy in copies:
-        copy.start()
+def pack_kernel(gate_ref, up_ref, down_ref, out_ref):
     down = down_ref[...].astype(F32)
     tail = [down[i * STACK : (i + 1) * STACK, PW:] for i in range(3)]
-    packed = jnp.concatenate([down[:, :PW], jnp.concatenate(tail, axis=1)], axis=0)
+    packed = jnp.concatenate([down[:, :PW], jnp.concatenate(tail, axis=1)], axis=0).astype(BF)
     for i in range(NZ):
-        out_ref[i, SH:, :] = packed.astype(BF)
-    for copy in copies:
-        copy.wait()
-    for i in range(NZ):
-        out_ref[i, :SH, :FF] = gate[...]
-        out_ref[i, :SH, FF:] = up[...]
-
-
-def unpad_matrices():
-    f = lax.broadcasted_iota(jnp.int32, (FF, DN), 0)
-    j = lax.broadcasted_iota(jnp.int32, (FF, DN), 1)
-    base = (f // FD) * 16
-    r = f % FD
-    body = (j == base + r).astype(F32).astype(BF)
-    tails = []
-    for i in range(3):
-        here = (r // STACK == i) & (j == base + FD + r % STACK)
-        tails.append(here.astype(F32).astype(BF))
-    return body, tails
+        out_ref[i, SH:, :] = packed
+        out_ref[i, :SH, :FF] = gate_ref[...]
+        out_ref[i, :SH, FF:] = up_ref[...]
+
+
+def unpack_down(full, wide):
+    for p in range(NZ * NX):
+        block = full[p // NX, p % NX, SH:, :].astype(F32)
+        wide[p * FD : (p + 1) * FD, :PW] = block[:FD]
+        for i in range(3):
+            at = p * FD + i * STACK
+            wide[at : at + STACK, PW:] = block[FD:, i * TW : (i + 1) * TW]
+
+
+def pack_down(wide, grads):
+    for p in range(NZ * NX):
+        at = p * FD
+        tail = [wide[at + i * STACK : at + (i + 1) * STACK, PW:] for i in range(3)]
+        rows = jnp.concatenate([wide[at : at + FD, :PW], jnp.concatenate(tail, axis=1)], axis=0)
+        grads[p // NX, p % NX, SH:, :] = rows.astype(BF)
 
 
 def dispatch_kernel(ids_ref, weights_ref, tokens_ref, upstream_ref, keep_ref, give_ref):
@@ -142,9 +136,9 @@
 
 
 def expert_kernel(*refs):
-    recv_ref, weights_ref = refs[:2]
-    (sent_ref, q_own, q_right_lo, q_right_hi, q_left_lo, q_left_hi, q_far_lo, q_far_hi) = refs[2:10]
-    recv, sent, full, grads, sems = refs[10:]
+    recv_ref, near_ref, *far_refs = refs[:4]
+    (sent_ref, q_own, q_right_lo, q_right_hi, q_left_lo, q_left_hi, q_far_lo, q_far_hi) = refs[4:12]
+    recv, sent, full, grads, wide, sems = refs[12:]
     x = lax.axis_index("dp") % NX
     to_right, to_left, across = (lax.rem(x + k, NX) for k in (1, NX - 1, 2))
     low, high = pl.ds(0, NZ // 2), pl.ds(NZ // 2, NZ // 2)
@@ -161,22 +155,20 @@
             buffer.at[high, across],
         )
 
-    starts = [0] + [NZ + i * (NZ // 2) for i in range(7)]
-    pieces = [weights_ref.at[pl.ds(a, b - a)] for a, b in zip(starts[:-1], starts[1:])]
+    starts = [0] + [NZ + i * (NZ // 2) for i in range(5)]
+    pieces = [near_ref.at[pl.ds(a, b - a)] for a, b in zip(starts[:-1], starts[1:])] + far_refs
     fetches = [pltpu.make_async_copy(recv_ref, recv, sems.at[0])]
     for i, (piece, spot) in enumerate(zip(pieces, spots(full))):
         fetches.append(pltpu.make_async_copy(piece, spot, sems.at[1 + i]))
     for fetch in fetches:
         fetch.start()
-    body, tails = unpad_matrices()
     for fetch in fetches:
         fetch.wait()
 
     gate = full[:, :, :SH, :FF].reshape(D, FF)
     up = full[:, :, :SH, FF:].reshape(D, FF)
-    packed = full[:, :, SH:, :].reshape(DN, PW)
-    last = sum(nn(tails[i], packed[:, i * TW : (i + 1) * TW]) for i in range(3))
-    down = jnp.concatenate([nn(body, packed).astype(BF), last.astype(BF)], axis=1)
+    unpack_down(full, wide)
+    down = wide[...].astype(BF)
     rows, scaled = recv[:, :D], recv[:, D:]
     pre_gate = nn(rows, gate)
     pre_up = nn(rows, up)
@@ -192,11 +184,8 @@
     stores[0].start()
     grads[:, :, :SH, :FF] = tn(rows, grad_gate_pre).astype(BF).reshape(NZ, NX, SH, FF)
     grads[:, :, :SH, FF:] = tn(rows, grad_up_pre).astype(BF).reshape(NZ, NX, SH, FF)
-    hidden_body = nn(hidden, body).astype(BF)
-    for i in range(3):
-        cols = slice(i * TW, (i + 1) * TW)
-        part = tn(hidden_body, scaled[:, cols]) + tn(nn(hidden, tails[i]).astype(BF), scaled[:, PW:])
-        grads[:, :, SH:, cols] = part.astype(BF).reshape(NZ, NX, 16, TW)
+    wide[...] = tn(hidden, scaled)
+    pack_down(wide, grads)
     pieces = (q_own, q_left_lo, q_right_hi, q_left_hi, q_right_lo, q_far_lo, q_far_hi)
     for i, (piece, spot) in enumerate(zip(pieces, spots(grads))):
         stores.append(pltpu.make_async_copy(spot, piece, sems.at[1 + i]))
@@ -302,14 +291,7 @@
 
 def on_device(tokens, route_ids, route_weights, upstream, w_gate, w_up, w_down):
     ids_t, weights_t = route_ids.T, route_weights.T
-    held = pltpu.VMEM((SH, FF), BF)
-    copies = call(
-        pack_kernel,
-        [((NZ, PH, PW), BF)],
-        scratch=[held, held, pltpu.SemaphoreType.DMA((2,))],
-        vmem=58 * MIB,
-        spaces=(pl.ANY, pl.ANY, None),
-    )(w_gate[0], w_up[0], w_down[0])
+    copies = call(pack_kernel, [((NZ, PH, PW), BF)], vmem=58 * MIB)(w_gate[0], w_up[0], w_down[0])
     both, one = ((NY, 2, CAP, 2 * D), BF), ((NY, CAP, 2 * D), BF)
     keep, give = call(
         dispatch_kernel, [((ROWS // 2, 2 * D), BF)] * 2, vmem=58 * MIB, flops=4 * ROWS * TOK * D
@@ -334,15 +316,24 @@
     back, q_own, q_right_lo, q_right_hi, q_left_lo, q_left_hi, q_far_lo, q_far_hi = call(
         expert_kernel,
         [((ROWS, 2 * D), BF), whole] + [part] * 6,
-        scratch=[tile, tile, matrix, matrix, pltpu.SemaphoreType.DMA((8,))],
+        scratch=[
+            tile,
+            tile,
+            matrix,
+            matrix,
+            pltpu.VMEM((FF, D), F32),
+            pltpu.SemaphoreType.DMA((8,)),
+        ],
         vmem=48 * MIB,
         flops=18 * ROWS * D * FF,
         moved=8 * MIB,
-        spaces=(pl.ANY,) * 2,
+        spaces=(pl.ANY,) * 4,
         out_spaces=(pl.ANY,) * 8,
     )(
         recv,
-        jnp.concatenate([own, left_lo, right_hi, left_hi, right_lo, far_lo, far_hi], axis=0),
+        jnp.concatenate([own, left_lo, right_hi, left_hi, right_lo], axis=0),
+        far_lo,
+        far_hi,
     )
     home = exchange(back.reshape(both[0]))
     add_lo, add_hi = shift_x(q_far_lo, 1), shift_x(q_far_hi, NX - 1)

time: 134 us -> 131 us (0.978)
  the two profiles are of different devices: /device:TPU:3 before, /device:TPU:7 now
where the time goes in v4:
time: 131 us; the launch traced here: 130 us
  starting transfers between devices  65.4 us (50%)
  waiting for transfers between devices  49.1 us (37%)
  Pallas kernels  13.9 us (11%)
    ppermute x12, starting transfers between devices, shift_x(): return lax.ppermute(v, 'dp', pairs)  35.4 us
    all_to_all x2, waiting for transfers between devices, swap_z(): lax.all_to_all(v, 'dp', split_axis=0, concat_axis=0, tiled=True, axis_ind...  23.3 us
    ppermute x12, waiting for transfers between devices, shift_x(): return lax.ppermute(v, 'dp', pairs)  15 us
    all_to_all x2, starting transfers between devices, swap_z(): lax.all_to_all(v, 'dp', split_axis=0, concat_axis=0, tiled=True, axis_ind...  13.7 us
    all_to_all x2, starting transfers between devices, exchange(): lax.all_to_all(v, 'expert', split_axis=0, concat_axis=0, tiled=True, axis...  10.4 us
    all_to_all x2, waiting for transfers between devices, exchange(): lax.all_to_all(v, 'expert', split_axis=0, concat_axis=0, tiled=True, axis...  7.48 us
    ppermute x2, starting transfers between devices, swap_core(): return lax.ppermute(v, 'expert', [(i, i ^ 1) for i in range(FLIGHT)])  5.91 us
    pallas_call x1, Pallas kernels, on_device(): call(expert_kernel, [((ROWS, 2 * D), BF), whole] + [part] * 6, scratch=[t...  5.26 us
  transfers between devices with their start and end apart: 18, of which 12 were waited for; matrix products, arithmetic and copies ran while one was open for 0% of the time, Pallas kernels for 4%

profile of v4, /device:TPU:7, one launch (start us, length us, event | category | flops | bytes accessed | tf_op | source)
XLA Modules:
  0.0 130.4 jit_solution(14282949966899113601)
XLA Ops:
  0.6 1.7 %shard_map.120 = bf16[8,48,768]{2,1,0:T(8,128)(2,1)} custom-call(bf16[32,384]{1,0:T(8,128)(2,1)} %bitcast.21, bf16[32,384]{1,0:T(8,128)(2,1)} %bitcast.22, bf16[12,1024]{1,0:T(8,128)(2,1)} %bitcast.20), custom_call_target="tpu_custom_call" | custom-call | bytes 1048576 | tf_op jit(solution)/shard_map/pallas_call | solution.py:294
  2.3 10.0 %all-to-all-start.1 = ((bf16[8,48,768]{2,1,0:T(8,128)(2,1)}), bf16[8,48,768]{2,1,0:T(8,128)(2,1)S(1)}, u32[]{:S(2)}, u32[]{:S(2)}) async-start(bf16[8,48,768]{2,1,0:T(8,128)(2,1)} %shard_map.120), calls=%async_computation.1 | async-start | bytes 1179648 | tf_op jit(solution)/shard_map/all_to_all | solution.py:268
  12.3 2.6 %shard_map.118 = (bf16[128,2048]{1,0:T(8,128)(2,1)}, bf16[128,2048]{1,0:T(8,128)(2,1)}) custom-call(s32[8,128]{1,0:T(8,128)} %bitcast.16, f32[8,128]{1,0:T(8,128)} %bitcast.18, bf16[128,1024]{1,0:T(8,128)(2,1)} %tokens_ref.1, bf16[128,1024]{1,0:T(8,128)(2,1)} %upstream_ref.3), custom_call_target="tpu_custom_call" | custom-call | flops 134217728 | bytes 1048576 | tf_op jit(solution)/shard_map/pallas_call | solution.py:296
  14.9 2.9 %collective-permute-start = (bf16[128,2048]{1,0:T(8,128)(2,1)}, bf16[128,2048]{1,0:T(8,128)(2,1)S(1)}, u32[]{:S(2)}, u32[]{:S(2)}) collective-permute-start(bf16[128,2048]{1,0:T(8,128)(2,1)} %get-tuple-element.25), channel_id=1, source_target_pairs={{0,1},{1,0},{2,3},{3,2},{4,5},{5,4},{6,7},{7,6},{8,9},{9,8},{10,11... | collective-permute-start | bytes 1572872 | tf_op jit(solution)/shard_map/ppermute | solution.py:283
  17.8 1.7 %collective-permute-done = bf16[128,2048]{1,0:T(8,128)(2,1)S(1)} collective-permute-done((bf16[128,2048]{1,0:T(8,128)(2,1)}, bf16[128,2048]{1,0:T(8,128)(2,1)S(1)}, u32[]{:S(2)}, u32[]{:S(2)}) %collective-permute-start) | collective-permute-done | bytes 524320 | tf_op jit(solution)/shard_map/ppermute | solution.py:283
  19.5 1.0 copy-done.1
  21.6 10.1 %all-to-all-done.1 = bf16[8,48,768]{2,1,0:T(8,128)(2,1)S(1)} async-done(((bf16[8,48,768]{2,1,0:T(8,128)(2,1)}), bf16[8,48,768]{2,1,0:T(8,128)(2,1)S(1)}, u32[]{:S(2)}, u32[]{:S(2)}) %all-to-all-start.1) | async-done | bytes 589856 | tf_op jit(solution)/shard_map/all_to_all | solution.py:268
  31.7 6.8 %all-to-all-start = ((bf16[8,2,16,2048]{3,2,1,0:T(8,128)(2,1)}), bf16[8,2,16,2048]{3,2,1,0:T(8,128)(2,1)S(1)}, u32[]{:S(2)}, u32[]{:S(2)}) async-start(bf16[8,2,16,2048]{3,2,1,0:T(8,128)(2,1)} %shard_map.119), calls=%async_computation | async-start | bytes 2097152 | tf_op jit(solution)/shard_map/all_to_all | solution.py:287
  38.6 2.5 %collective-permute-start.2 = (bf16[4,48,768]{2,1,0:T(8,128)(2,1)S(1)}, bf16[4,48,768]{2,1,0:T(8,128)(2,1)S(1)}, u32[]{:S(2)}, u32[]{:S(2)}) collective-permute-start(bf16[4,48,768]{2,1,0:T(8,128)(2,1)S(1)} %get-tuple-element.42), channel_id=1, source_target_pairs={{0,48},{16,0},{32,16},{48,32},{64,112},{80,64},{96,80},{112,96},{1... | collective-permute-start | bytes 884744 | tf_op jit(solution)/shard_map/ppermute | solution.py:275
  41.0 4.0 %collective-permute-start.1 = (bf16[4,48,768]{2,1,0:T(8,128)(2,1)S(1)}, bf16[4,48,768]{2,1,0:T(8,128)(2,1)S(1)}, u32[]{:S(2)}, u32[]{:S(2)}) collective-permute-start(bf16[4,48,768]{2,1,0:T(8,128)(2,1)S(1)} %get-tuple-element.43), channel_id=1, source_target_pairs={{0,16},{16,32},{32,48},{48,0},{64,80},{80,96},{96,112},{112,64},{1... | collective-permute-start | bytes 884744 | tf_op jit(solution)/shard_map/ppermute | solution.py:275
  45.1 1.9 %collective-permute-start.3 = (bf16[4,48,768]{2,1,0:T(8,128)(2,1)S(1)}, bf16[4,48,768]{2,1,0:T(8,128)(2,1)S(1)}, u32[]{:S(2)}, u32[]{:S(2)}) collective-permute-start(bf16[4,48,768]{2,1,0:T(8,128)(2,1)S(1)} %get-tuple-element.42), channel_id=1, source_target_pairs={{0,16},{16,32},{32,48},{48,0},{64,80},{80,96},{96,112},{112,64},{1... | collective-permute-start | bytes 884744 | tf_op jit(solution)/shard_map/ppermute | solution.py:275
  47.0 3.4 %collective-permute-start.4 = (bf16[4,48,768]{2,1,0:T(8,128)(2,1)S(1)}, bf16[4,48,768]{2,1,0:T(8,128)(2,1)S(1)}, u32[]{:S(2)}, u32[]{:S(2)}) collective-permute-start(bf16[4,48,768]{2,1,0:T(8,128)(2,1)S(1)} %get-tuple-element.43), channel_id=1, source_target_pairs={{0,48},{16,0},{32,16},{48,32},{64,112},{80,64},{96,80},{112,96},{1... | collective-permute-start | bytes 884744 | tf_op jit(solution)/shard_map/ppermute | solution.py:275
  50.4 1.9 %collective-permute-start.6 = (bf16[4,48,768]{2,1,0:T(8,128)(2,1)S(1)}, bf16[4,48,768]{2,1,0:T(8,128)(2,1)S(1)}, u32[]{:S(2)}, u32[]{:S(2)}) collective-permute-start(bf16[4,48,768]{2,1,0:T(8,128)(2,1)S(1)} %collective-permute-done.2), channel_id=1, source_target_pairs={{0,48},{16,0},{32,16},{48,32},{64,112},{80,64},{96,80},{112,96},{1... | collective-permute-start | bytes 884744 | tf_op jit(solution)/shard_map/ppermute | solution.py:275
  52.4 4.6 %collective-permute-start.5 = (bf16[4,48,768]{2,1,0:T(8,128)(2,1)S(1)}, bf16[4,48,768]{2,1,0:T(8,128)(2,1)S(1)}, u32[]{:S(2)}, u32[]{:S(2)}) collective-permute-start(bf16[4,48,768]{2,1,0:T(8,128)(2,1)S(1)} %collective-permute-done.1), channel_id=1, source_target_pairs={{0,16},{16,32},{32,48},{48,0},{64,80},{80,96},{96,112},{112,64},{1... | collective-permute-start | bytes 884744 | tf_op jit(solution)/shard_map/ppermute | solution.py:275
  57.3 6.3 %collective-permute-done.6.refs_3_ = bf16[4,48,768]{2,1,0:T(8,128)(2,1)S(1)} collective-permute-done((bf16[4,48,768]{2,1,0:T(8,128)(2,1)S(1)}, bf16[4,48,768]{2,1,0:T(8,128)(2,1)S(1)}, u32[]{:S(2)}, u32[]{:S(2)}) %collective-permute-start.6) | collective-permute-done | bytes 294944 | tf_op jit(solution)/shard_map/ppermute | solution.py:275
  63.6 4.2 %all-to-all-done = bf16[8,2,16,2048]{3,2,1,0:T(8,128)(2,1)S(1)} async-done(((bf16[8,2,16,2048]{3,2,1,0:T(8,128)(2,1)}), bf16[8,2,16,2048]{3,2,1,0:T(8,128)(2,1)S(1)}, u32[]{:S(2)}, u32[]{:S(2)}) %all-to-all-start) | async-done | bytes 1048608 | tf_op jit(solution)/shard_map/all_to_all | solution.py:287
  67.8 5.3 %shard_map.121 = (bf16[256,2048]{1,0:T(8,128)(2,1)}, bf16[8,48,768]{2,1,0:T(8,128)(2,1)S(1)}, bf16[4,48,768]{2,1,0:T(8,128)(2,1)S(1)}, bf16[4,48,768]{2,1,0:T(8,...) custom-call(bf16[256,2048]{1,0:T(8,128)(2,1)S(1)} %bitcast.13, ...), custom_call_target="tpu_custom_call" | custom-call | flops 1811939328 | bytes 8388608 | tf_op jit(solution)/shard_map/pallas_call | solution.py:316
  73.0 3.6 %all-to-all-start.2 = ((bf16[8,2,16,2048]{3,2,1,0:T(8,128)(2,1)}), bf16[8,2,16,2048]{3,2,1,0:T(8,128)(2,1)S(1)}, u32[]{:S(2)}, u32[]{:S(2)}) async-start(bf16[8,2,16,2048]{3,2,1,0:T(8,128)(2,1)} %bitcast.8), calls=%async_computation.2 | async-start | bytes 2097152 | tf_op jit(solution)/shard_map/all_to_all | solution.py:287
  76.6 2.9 %collective-permute-start.7 = (bf16[4,48,768]{2,1,0:T(8,128)(2,1)}, bf16[4,48,768]{2,1,0:T(8,128)(2,1)S(1)}, u32[]{:S(2)}, u32[]{:S(2)}) collective-permute-start(bf16[4,48,768]{2,1,0:T(8,128)(2,1)} %get-tuple-element.30), channel_id=1, source_target_pairs={{0,16},{16,32},{32,48},{48,0},{64,80},{80,96},{96,112},{112,64},{1... | collective-permute-start | bytes 884744 | tf_op jit(solution)/shard_map/ppermute | solution.py:275
  79.5 2.4 %collective-permute-start.8 = (bf16[4,48,768]{2,1,0:T(8,128)(2,1)}, bf16[4,48,768]{2,1,0:T(8,128)(2,1)S(1)}, u32[]{:S(2)}, u32[]{:S(2)}) collective-permute-start(bf16[4,48,768]{2,1,0:T(8,128)(2,1)} %get-tuple-element.31), channel_id=1, source_target_pairs={{0,48},{16,0},{32,16},{48,32},{64,112},{80,64},{96,80},{112,96},{1... | collective-permute-start | bytes 884744 | tf_op jit(solution)/shard_map/ppermute | solution.py:275
  81.9 4.1 %collective-permute-start.10 = (bf16[4,48,768]{2,1,0:T(8,128)(2,1)S(1)}, bf16[4,48,768]{2,1,0:T(8,128)(2,1)S(1)}, u32[]{:S(2)}, u32[]{:S(2)}) collective-permute-start(bf16[4,48,768]{2,1,0:T(8,128)(2,1)S(1)} %get-tuple-element.33), channel_id=1, source_target_pairs={{0,16},{16,32},{32,48},{48,0},{64,80},{80,96},{96,112},{112,64},{1... | collective-permute-start | bytes 884744 | tf_op jit(solution)/shard_map/ppermute | solution.py:275
  86.0 1.9 %collective-permute-start.11 = (bf16[4,48,768]{2,1,0:T(8,128)(2,1)S(1)}, bf16[4,48,768]{2,1,0:T(8,128)(2,1)S(1)}, u32[]{:S(2)}, u32[]{:S(2)}) collective-permute-start(bf16[4,48,768]{2,1,0:T(8,128)(2,1)S(1)} %get-tuple-element.34), channel_id=1, source_target_pairs={{0,48},{16,0},{32,16},{48,32},{64,112},{80,64},{96,80},{112,96},{1... | collective-permute-start | bytes 884744 | tf_op jit(solution)/shard_map/ppermute | solution.py:275
  88.8 3.9 %collective-permute-start.9 = (bf16[4,48,768]{2,1,0:T(8,128)(2,1)S(1)}, bf16[4,48,768]{2,1,0:T(8,128)(2,1)S(1)}, u32[]{:S(2)}, u32[]{:S(2)}) collective-permute-start(bf16[4,48,768]{2,1,0:T(8,128)(2,1)S(1)} %get-tuple-element.32), channel_id=1, source_target_pairs={{0,16},{16,32},{32,48},{48,0},{64,80},{80,96},{96,112},{112,64},{1... | collective-permute-start | bytes 884744 | tf_op jit(solution)/shard_map/ppermute | solution.py:275
  92.7 1.9 %collective-permute-start.12 = (bf16[4,48,768]{2,1,0:T(8,128)(2,1)S(1)}, bf16[4,48,768]{2,1,0:T(8,128)(2,1)S(1)}, u32[]{:S(2)}, u32[]{:S(2)}) collective-permute-start(bf16[4,48,768]{2,1,0:T(8,128)(2,1)S(1)} %get-tuple-element.35), channel_id=1, source_target_pairs={{0,48},{16,0},{32,16},{48,32},{64,112},{80,64},{96,80},{112,96},{1... | collective-permute-start | bytes 884744 | tf_op jit(solution)/shard_map/ppermute | solution.py:275
  95.5 1.7 %collective-permute-done.9.left_lo = bf16[4,48,768]{2,1,0:T(8,128)(2,1)S(1)} collective-permute-done((bf16[4,48,768]{2,1,0:T(8,128)(2,1)S(1)}, bf16[4,48,768]{2,1,0:T(8,128)(2,1)S(1)}, u32[]{:S(2)}, u32[]{:S(2)}) %collective-permute-start.9) | collective-permute-done | bytes 294944 | tf_op jit(solution)/shard_map/ppermute | solution.py:275
  97.2 5.2 %collective-permute-done.12.right_hi = bf16[4,48,768]{2,1,0:T(8,128)(2,1)S(1)} collective-permute-done((bf16[4,48,768]{2,1,0:T(8,128)(2,1)S(1)}, bf16[4,48,768]{2,1,0:T(8,128)(2,1)S(1)}, u32[]{:S(2)}, u32[]{:S(2)}) %collective-permute-start.12) | collective-permute-done | bytes 294944 | tf_op jit(solution)/shard_map/ppermute | solution.py:275
  102.4 3.3 %all-to-all-done.2.after_ref.home_ref = bf16[8,2,16,2048]{3,2,1,0:T(8,128)(2,1)S(1)} async-done(((bf16[8,2,16,2048]{3,2,1,0:T(8,128)(2,1)}), bf16[8,2,16,2048]{3,2,1,0:T(8,128)(2,1)S(1)}, u32[]{:S(2)}, u32[]{:S(2)}) %all-to-all-start.2) | async-done | bytes 1048608 | tf_op jit(solution)/shard_map/all_to_all | solution.py:287
  106.7 3.7 %all-to-all-start.3 = ((bf16[8,48,768]{2,1,0:T(8,128)(2,1)}), bf16[8,48,768]{2,1,0:T(8,128)(2,1)S(1)}, u32[]{:S(2)}, u32[]{:S(2)}) async-start(bf16[8,48,768]{2,1,0:T(8,128)(2,1)} %shard_map.123.after_ref), calls=%async_computation.3 | async-start | bytes 1179648 | tf_op jit(solution)/shard_map/all_to_all | solution.py:268
  110.5 3.1 %collective-permute-start.13 = (bf16[8,16,2048]{2,1,0:T(8,128)(2,1)S(1)}, bf16[8,16,2048]{2,1,0:T(8,128)(2,1)S(1)}, u32[]{:S(2)}, u32[]{:S(2)}) collective-permute-start(bf16[8,16,2048]{2,1,0:T(8,128)(2,1)S(1)} %shard_map.124), channel_id=1, source_target_pairs={{0,1},{1,0},{2,3},{3,2},{4,5},{5,4},{6,7},{7,6},{8,9},{9,8},{10,11... | collective-permute-start | bytes 1572872 | tf_op jit(solution)/shard_map/ppermute | solution.py:283
  113.6 1.5 %collective-permute-done.13.got_ref = bf16[8,16,2048]{2,1,0:T(8,128)(2,1)S(1)} collective-permute-done((bf16[8,16,2048]{2,1,0:T(8,128)(2,1)S(1)}, bf16[8,16,2048]{2,1,0:T(8,128)(2,1)S(1)}, u32[]{:S(2)}, u32[]{:S(2)}) %collective-permute-start.13) | collective-permute-done | bytes 524320 | tf_op jit(solution)/shard_map/ppermute | solution.py:283
  115.1 1.4 %shard_map.125 = (bf16[128,1024]{1,0:T(8,128)(2,1)}, bf16[128,1024]{1,0:T(8,128)(2,1)}, f32[8,128]{1,0:T(8,128)}) custom-call(s32[8,128]{1,0:T(8,128)S(1)} %bitcast.17, f32[8,128]{1,0:T(8,128)S(1)} %bitcast.19, bf16[128,1024]{1,0:T(8,128)(2,1)S(1)} %copy-done, bf16[8,2,16,2048]{3,2,1,0:T(8,128)(2,1)S(1)} %all-to-all-done.2.after_ref.home_ref, ...), custom_call_target="tpu_custom_call" | custom-call | flops 134217728 | bytes 2097152 | tf_op jit(solution)/shard_map/pallas_call | solution.py:361
  116.5 13.2 %all-to-all-done.3.parts_ref = bf16[8,48,768]{2,1,0:T(8,128)(2,1)S(1)} async-done(((bf16[8,48,768]{2,1,0:T(8,128)(2,1)}), bf16[8,48,768]{2,1,0:T(8,128)(2,1)S(1)}, u32[]{:S(2)}, u32[]{:S(2)}) %all-to-all-start.3) | async-done | bytes 589856 | tf_op jit(solution)/shard_map/all_to_all | solution.py:268
  (29 shorter events, 5.0 us)
Async XLA Ops:
  2.3 29.4 %all-to-all-start.1 = ((bf16[8,48,768]{2,1,0:T(8,128)(2,1)}), bf16[8,48,768]{2,1,0:T(8,128)(2,1)S(1)}, u32[]{:S(2)}, u32[]{:S(2)}) async-start(bf16[8,48,768]{2,1,0:T(8,128)(2,1)} %shard_map.120), calls=%async_computation.1 | async-start | bytes 1179648 | tf_op jit(solution)/shard_map/all_to_all | solution.py:268
  14.9 4.6 %collective-permute-start = (bf16[128,2048]{1,0:T(8,128)(2,1)}, bf16[128,2048]{1,0:T(8,128)(2,1)S(1)}, u32[]{:S(2)}, u32[]{:S(2)}) collective-permute-start(bf16[128,2048]{1,0:T(8,128)(2,1)} %get-tuple-element.25), channel_id=1, source_target_pairs={{0,1},{1,0},{2,3},{3,2},{4,5},{5,4},{6,7},{7,6},{8,9},{9,8},{10,11... | collective-permute-start | bytes 1572872 | tf_op jit(solution)/shard_map/ppermute | solution.py:283
  19.5 1.0 copy-start.1
  31.7 36.1 %all-to-all-start = ((bf16[8,2,16,2048]{3,2,1,0:T(8,128)(2,1)}), bf16[8,2,16,2048]{3,2,1,0:T(8,128)(2,1)S(1)}, u32[]{:S(2)}, u32[]{:S(2)}) async-start(bf16[8,2,16,2048]{3,2,1,0:T(8,128)(2,1)} %shard_map.119), calls=%async_computation | async-start | bytes 2097152 | tf_op jit(solution)/shard_map/all_to_all | solution.py:287
  38.6 11.9 %collective-permute-start.2 = (bf16[4,48,768]{2,1,0:T(8,128)(2,1)S(1)}, bf16[4,48,768]{2,1,0:T(8,128)(2,1)S(1)}, u32[]{:S(2)}, u32[]{:S(2)}) collective-permute-start(bf16[4,48,768]{2,1,0:T(8,128)(2,1)S(1)} %get-tuple-element.42), channel_id=1, source_target_pairs={{0,48},{16,0},{32,16},{48,32},{64,112},{80,64},{96,80},{112,96},{1... | collective-permute-start | bytes 884744 | tf_op jit(solution)/shard_map/ppermute | solution.py:275
  41.0 11.3 %collective-permute-start.1 = (bf16[4,48,768]{2,1,0:T(8,128)(2,1)S(1)}, bf16[4,48,768]{2,1,0:T(8,128)(2,1)S(1)}, u32[]{:S(2)}, u32[]{:S(2)}) collective-permute-start(bf16[4,48,768]{2,1,0:T(8,128)(2,1)S(1)} %get-tuple-element.43), channel_id=1, source_target_pairs={{0,16},{16,32},{32,48},{48,0},{64,80},{80,96},{96,112},{112,64},{1... | collective-permute-start | bytes 884744 | tf_op jit(solution)/shard_map/ppermute | solution.py:275
  45.1 11.9 %collective-permute-start.3 = (bf16[4,48,768]{2,1,0:T(8,128)(2,1)S(1)}, bf16[4,48,768]{2,1,0:T(8,128)(2,1)S(1)}, u32[]{:S(2)}, u32[]{:S(2)}) collective-permute-start(bf16[4,48,768]{2,1,0:T(8,128)(2,1)S(1)} %get-tuple-element.42), channel_id=1, source_target_pairs={{0,16},{16,32},{32,48},{48,0},{64,80},{80,96},{96,112},{112,64},{1... | collective-permute-start | bytes 884744 | tf_op jit(solution)/shard_map/ppermute | solution.py:275
  47.0 10.3 %collective-permute-start.4 = (bf16[4,48,768]{2,1,0:T(8,128)(2,1)S(1)}, bf16[4,48,768]{2,1,0:T(8,128)(2,1)S(1)}, u32[]{:S(2)}, u32[]{:S(2)}) collective-permute-start(bf16[4,48,768]{2,1,0:T(8,128)(2,1)S(1)} %get-tuple-element.43), channel_id=1, source_target_pairs={{0,48},{16,0},{32,16},{48,32},{64,112},{80,64},{96,80},{112,96},{1... | collective-permute-start | bytes 884744 | tf_op jit(solution)/shard_map/ppermute | solution.py:275
  50.4 13.2 %collective-permute-start.6 = (bf16[4,48,768]{2,1,0:T(8,128)(2,1)S(1)}, bf16[4,48,768]{2,1,0:T(8,128)(2,1)S(1)}, u32[]{:S(2)}, u32[]{:S(2)}) collective-permute-start(bf16[4,48,768]{2,1,0:T(8,128)(2,1)S(1)} %collective-permute-done.2), channel_id=1, source_target_pairs={{0,48},{16,0},{32,16},{48,32},{64,112},{80,64},{96,80},{112,96},{1... | collective-permute-start | bytes 884744 | tf_op jit(solution)/shard_map/ppermute | solution.py:275
  52.4 11.2 %collective-permute-start.5 = (bf16[4,48,768]{2,1,0:T(8,128)(2,1)S(1)}, bf16[4,48,768]{2,1,0:T(8,128)(2,1)S(1)}, u32[]{:S(2)}, u32[]{:S(2)}) collective-permute-start(bf16[4,48,768]{2,1,0:T(8,128)(2,1)S(1)} %collective-permute-done.1), channel_id=1, source_target_pairs={{0,16},{16,32},{32,48},{48,0},{64,80},{80,96},{96,112},{112,64},{1... | collective-permute-start | bytes 884744 | tf_op jit(solution)/shard_map/ppermute | solution.py:275
  57.3 6.3 %copy-start.4 = (bf16[24,48,768]{2,1,0:T(8,128)(2,1)}, bf16[24,48,768]{2,1,0:T(8,128)(2,1)S(1)}, u32[]{:S(2)}) copy-start(bf16[24,48,768]{2,1,0:T(8,128)(2,1)S(1)} %constant_dynamic-update-slice_fusion.refs_1_) | copy-start | bytes 5308420
  73.0 32.7 %all-to-all-start.2 = ((bf16[8,2,16,2048]{3,2,1,0:T(8,128)(2,1)}), bf16[8,2,16,2048]{3,2,1,0:T(8,128)(2,1)S(1)}, u32[]{:S(2)}, u32[]{:S(2)}) async-start(bf16[8,2,16,2048]{3,2,1,0:T(8,128)(2,1)} %bitcast.8), calls=%async_computation.2 | async-start | bytes 2097152 | tf_op jit(solution)/shard_map/all_to_all | solution.py:287
  76.6 11.3 %collective-permute-start.7 = (bf16[4,48,768]{2,1,0:T(8,128)(2,1)}, bf16[4,48,768]{2,1,0:T(8,128)(2,1)S(1)}, u32[]{:S(2)}, u32[]{:S(2)}) collective-permute-start(bf16[4,48,768]{2,1,0:T(8,128)(2,1)} %get-tuple-element.30), channel_id=1, source_target_pairs={{0,16},{16,32},{32,48},{48,0},{64,80},{80,96},{96,112},{112,64},{1... | collective-permute-start | bytes 884744 | tf_op jit(solution)/shard_map/ppermute | solution.py:275
  79.5 9.2 %collective-permute-start.8 = (bf16[4,48,768]{2,1,0:T(8,128)(2,1)}, bf16[4,48,768]{2,1,0:T(8,128)(2,1)S(1)}, u32[]{:S(2)}, u32[]{:S(2)}) collective-permute-start(bf16[4,48,768]{2,1,0:T(8,128)(2,1)} %get-tuple-element.31), channel_id=1, source_target_pairs={{0,48},{16,0},{32,16},{48,32},{64,112},{80,64},{96,80},{112,96},{1... | collective-permute-start | bytes 884744 | tf_op jit(solution)/shard_map/ppermute | solution.py:275
  81.9 12.7 %collective-permute-start.10 = (bf16[4,48,768]{2,1,0:T(8,128)(2,1)S(1)}, bf16[4,48,768]{2,1,0:T(8,128)(2,1)S(1)}, u32[]{:S(2)}, u32[]{:S(2)}) collective-permute-start(bf16[4,48,768]{2,1,0:T(8,128)(2,1)S(1)} %get-tuple-element.33), channel_id=1, source_target_pairs={{0,16},{16,32},{32,48},{48,0},{64,80},{80,96},{96,112},{112,64},{1... | collective-permute-start | bytes 884744 | tf_op jit(solution)/shard_map/ppermute | solution.py:275
  86.0 9.5 %collective-permute-start.11 = (bf16[4,48,768]{2,1,0:T(8,128)(2,1)S(1)}, bf16[4,48,768]{2,1,0:T(8,128)(2,1)S(1)}, u32[]{:S(2)}, u32[]{:S(2)}) collective-permute-start(bf16[4,48,768]{2,1,0:T(8,128)(2,1)S(1)} %get-tuple-element.34), channel_id=1, source_target_pairs={{0,48},{16,0},{32,16},{48,32},{64,112},{80,64},{96,80},{112,96},{1... | collective-permute-start | bytes 884744 | tf_op jit(solution)/shard_map/ppermute | solution.py:275
  88.8 8.4 %collective-permute-start.9 = (bf16[4,48,768]{2,1,0:T(8,128)(2,1)S(1)}, bf16[4,48,768]{2,1,0:T(8,128)(2,1)S(1)}, u32[]{:S(2)}, u32[]{:S(2)}) collective-permute-start(bf16[4,48,768]{2,1,0:T(8,128)(2,1)S(1)} %get-tuple-element.32), channel_id=1, source_target_pairs={{0,16},{16,32},{32,48},{48,0},{64,80},{80,96},{96,112},{112,64},{1... | collective-permute-start | bytes 884744 | tf_op jit(solution)/shard_map/ppermute | solution.py:275
  92.7 9.7 %collective-permute-start.12 = (bf16[4,48,768]{2,1,0:T(8,128)(2,1)S(1)}, bf16[4,48,768]{2,1,0:T(8,128)(2,1)S(1)}, u32[]{:S(2)}, u32[]{:S(2)}) collective-permute-start(bf16[4,48,768]{2,1,0:T(8,128)(2,1)S(1)} %get-tuple-element.35), channel_id=1, source_target_pairs={{0,48},{16,0},{32,16},{48,32},{64,112},{80,64},{96,80},{112,96},{1... | collective-permute-start | bytes 884744 | tf_op jit(solution)/shard_map/ppermute | solution.py:275
  106.7 8.3 %copy-start = (bf16[128,1024]{1,0:T(8,128)(2,1)S(1)}, bf16[128,1024]{1,0:T(8,128)(2,1)}, u32[]{:S(2)}) copy-start(bf16[128,1024]{1,0:T(8,128)(2,1)} %upstream_ref.3) | copy-start | bytes 786436
  106.7 8.3 %copy-start.2 = (s32[128,8]{0,1:T(8,128)S(1)}, s32[128,8]{0,1:T(8,128)}, u32[]{:S(2)}) copy-start(s32[128,8]{0,1:T(8,128)} %param.8) | copy-start | bytes 12292
  106.7 8.3 %copy-start.3 = (f32[128,8]{0,1:T(8,128)S(1)}, f32[128,8]{0,1:T(8,128)}, u32[]{:S(2)}) copy-start(f32[128,8]{0,1:T(8,128)} %param.9) | copy-start | bytes 12292
  106.7 22.9 %all-to-all-start.3 = ((bf16[8,48,768]{2,1,0:T(8,128)(2,1)}), bf16[8,48,768]{2,1,0:T(8,128)(2,1)S(1)}, u32[]{:S(2)}, u32[]{:S(2)}) async-start(bf16[8,48,768]{2,1,0:T(8,128)(2,1)} %shard_map.123.after_ref), calls=%async_computation.3 | async-start | bytes 1179648 | tf_op jit(solution)/shard_map/all_to_all | solution.py:268
  110.5 4.6 %collective-permute-start.13 = (bf16[8,16,2048]{2,1,0:T(8,128)(2,1)S(1)}, bf16[8,16,2048]{2,1,0:T(8,128)(2,1)S(1)}, u32[]{:S(2)}, u32[]{:S(2)}) collective-permute-start(bf16[8,16,2048]{2,1,0:T(8,128)(2,1)S(1)} %shard_map.124), channel_id=1, source_target_pairs={{0,1},{1,0},{2,3},{3,2},{4,5},{5,4},{6,7},{7,6},{8,9},{9,8},{10,11... | collective-permute-start | bytes 1572872 | tf_op jit(solution)/shard_map/ppermute | solution.py:283

commit v5 on v4

--- a/solution.py
+++ b/solution.py
@@ -19,6 +19,7 @@
 PH = SH + 16
 TW = D - PW
 STACK = FD // 3
+LO = 3
 BF = jnp.bfloat16
 F32 = jnp.float32
 MIB = 1 << 20
@@ -138,13 +139,13 @@
 def expert_kernel(*refs):
     recv_ref, near_ref, *far_refs = refs[:4]
     (sent_ref, q_own, q_right_lo, q_right_hi, q_left_lo, q_left_hi, q_far_lo, q_far_hi) = refs[4:12]
-    recv, sent, full, grads, wide, sems = refs[12:]
+    sent, full, grads, wide, sems = refs[12:]
     x = lax.axis_index("dp") % NX
     to_right, to_left, across = (lax.rem(x + k, NX) for k in (1, NX - 1, 2))
-    low, high = pl.ds(0, NZ // 2), pl.ds(NZ // 2, NZ // 2)
     every = pl.ds(0, NZ)
 
-    def spots(buffer):
+    def spots(buffer, cut):
+        low, high = pl.ds(0, cut), pl.ds(cut, NZ - cut)
         return (
             buffer.at[every, x],
             buffer.at[low, to_left],
@@ -155,10 +156,13 @@
             buffer.at[high, across],
         )
 
-    starts = [0] + [NZ + i * (NZ // 2) for i in range(5)]
-    pieces = [near_ref.at[pl.ds(a, b - a)] for a, b in zip(starts[:-1], starts[1:])] + far_refs
-    fetches = [pltpu.make_async_copy(recv_ref, recv, sems.at[0])]
-    for i, (piece, spot) in enumerate(zip(pieces, spots(full))):
+    pieces, start = [], 0
+    for length in (NZ, LO, NZ - LO, NZ - LO, LO):
+        pieces.append(near_ref.at[pl.ds(start, length)])
+        start += length
+    pieces += far_refs
+    fetches = []
+    for i, (piece, spot) in enumerate(zip(pieces, spots(full, LO))):
         fetches.append(pltpu.make_async_copy(piece, spot, sems.at[1 + i]))
     for fetch in fetches:
         fetch.start()
@@ -169,7 +173,7 @@
     up = full[:, :, :SH, FF:].reshape(D, FF)
     unpack_down(full, wide)
     down = wide[...].astype(BF)
-    rows, scaled = recv[:, :D], recv[:, D:]
+    rows, scaled = recv_ref[:, :D], recv_ref[:, D:]
     pre_gate = nn(rows, gate)
     pre_up = nn(rows, up)
     grad_hidden = nt(scaled, down)
@@ -187,7 +191,7 @@
     wide[...] = tn(hidden, scaled)
     pack_down(wide, grads)
     pieces = (q_own, q_left_lo, q_right_hi, q_left_hi, q_right_lo, q_far_lo, q_far_hi)
-    for i, (piece, spot) in enumerate(zip(pieces, spots(grads))):
+    for i, (piece, spot) in enumerate(zip(pieces, spots(grads, NZ // 2))):
         stores.append(pltpu.make_async_copy(spot, piece, sems.at[1 + i]))
         stores[-1].start()
     for store in stores:
@@ -306,7 +310,7 @@
     own = swap_z(copies)
     recv = exchange(sent).reshape(ROWS, 2 * D)
     half = NZ // 2
-    low, high = own[:half], own[half:]
+    low, high = own[:LO], own[LO:]
     left_lo, right_hi = shift_x(low, 1), shift_x(high, NX - 1)
     left_hi, right_lo = shift_x(high, 1), shift_x(low, NX - 1)
     far_lo, far_hi = shift_x(left_lo, 1), shift_x(right_hi, NX - 1)
@@ -318,7 +322,6 @@
         [((ROWS, 2 * D), BF), whole] + [part] * 6,
         scratch=[
             tile,
-            tile,
             matrix,
             matrix,
             pltpu.VMEM((FF, D), F32),
@@ -327,7 +330,7 @@
         vmem=48 * MIB,
         flops=18 * ROWS * D * FF,
         moved=8 * MIB,
-        spaces=(pl.ANY,) * 4,
+        spaces=(None,) + (pl.ANY,) * 3,
         out_spaces=(pl.ANY,) * 8,
     )(
         recv,

time: 131 us -> 131 us (level)
  the two profiles are of different devices: /device:TPU:7 before, /device:TPU:2 now
where the time goes in v5:
time: 131 us; the launch traced here: 130 us
  starting transfers between devices  68.7 us (52%)
  waiting for transfers between devices  45.6 us (35%)
  Pallas kernels  13.8 us (11%)
    ppermute x12, starting transfers between devices, shift_x(): return lax.ppermute(v, 'dp', pairs)  39.1 us
    all_to_all x2, waiting for transfers between devices, swap_z(): lax.all_to_all(v, 'dp', split_axis=0, concat_axis=0, tiled=True, axis_ind...  22.2 us
    ppermute x12, waiting for transfers between devices, shift_x(): return lax.ppermute(v, 'dp', pairs)  17.1 us
    all_to_all x2, starting transfers between devices, swap_z(): lax.all_to_all(v, 'dp', split_axis=0, concat_axis=0, tiled=True, axis_ind...  14 us
    all_to_all x2, starting transfers between devices, exchange(): lax.all_to_all(v, 'expert', split_axis=0, concat_axis=0, tiled=True, axis...  11.7 us
    pallas_call x1, Pallas kernels, on_device(): call(expert_kernel, [((ROWS, 2 * D), BF), whole] + [part] * 6, scratch=[t...  5.19 us
    ppermute x2, waiting for transfers between devices, swap_core(): return lax.ppermute(v, 'expert', [(i, i ^ 1) for i in range(FLIGHT)])  3.96 us
    ppermute x2, starting transfers between devices, swap_core(): return lax.ppermute(v, 'expert', [(i, i ^ 1) for i in range(FLIGHT)])  3.83 us
  transfers between devices with their start and end apart: 18, of which 12 were waited for; matrix products, arithmetic and copies ran while one was open for 0% of the time, Pallas kernels for 4%

profile of v5, /device:TPU:2, one launch (start us, length us, event | category | flops | bytes accessed | tf_op | source)
XLA Modules:
  0.0 130.1 jit_solution(7044905526740008416)
XLA Ops:
  0.6 1.6 %shard_map.120 = bf16[8,48,768]{2,1,0:T(8,128)(2,1)} custom-call(bf16[32,384]{1,0:T(8,128)(2,1)} %bitcast.21, bf16[32,384]{1,0:T(8,128)(2,1)} %bitcast.22, bf16[12,1024]{1,0:T(8,128)(2,1)} %bitcast.20), custom_call_target="tpu_custom_call" | custom-call | bytes 1048576 | tf_op jit(solution)/shard_map/pallas_call | solution.py:298
  2.3 10.3 %all-to-all-start.1 = ((bf16[8,48,768]{2,1,0:T(8,128)(2,1)}), bf16[8,48,768]{2,1,0:T(8,128)(2,1)S(1)}, u32[]{:S(2)}, u32[]{:S(2)}) async-start(bf16[8,48,768]{2,1,0:T(8,128)(2,1)} %shard_map.120), calls=%async_computation.1 | async-start | bytes 1179648 | tf_op jit(solution)/shard_map/all_to_all | solution.py:272
  12.6 2.6 %shard_map.118 = (bf16[128,2048]{1,0:T(8,128)(2,1)}, bf16[128,2048]{1,0:T(8,128)(2,1)}) custom-call(s32[8,128]{1,0:T(8,128)} %bitcast.16, f32[8,128]{1,0:T(8,128)} %bitcast.18, bf16[128,1024]{1,0:T(8,128)(2,1)} %tokens_ref.1, bf16[128,1024]{1,0:T(8,128)(2,1)} %upstream_ref.3), custom_call_target="tpu_custom_call" | custom-call | flops 134217728 | bytes 1048576 | tf_op jit(solution)/shard_map/pallas_call | solution.py:300
  15.2 1.9 %collective-permute-start = (bf16[128,2048]{1,0:T(8,128)(2,1)}, bf16[128,2048]{1,0:T(8,128)(2,1)S(1)}, u32[]{:S(2)}, u32[]{:S(2)}) collective-permute-start(bf16[128,2048]{1,0:T(8,128)(2,1)} %get-tuple-element.25), channel_id=1, source_target_pairs={{0,1},{1,0},{2,3},{3,2},{4,5},{5,4},{6,7},{7,6},{8,9},{9,8},{10,11... | collective-permute-start | bytes 1572872 | tf_op jit(solution)/shard_map/ppermute | solution.py:287
  17.1 2.1 %collective-permute-done = bf16[128,2048]{1,0:T(8,128)(2,1)S(1)} collective-permute-done((bf16[128,2048]{1,0:T(8,128)(2,1)}, bf16[128,2048]{1,0:T(8,128)(2,1)S(1)}, u32[]{:S(2)}, u32[]{:S(2)}) %collective-permute-start) | collective-permute-done | bytes 524320 | tf_op jit(solution)/shard_map/ppermute | solution.py:287
  21.3 10.2 %all-to-all-done.1 = bf16[8,48,768]{2,1,0:T(8,128)(2,1)S(1)} async-done(((bf16[8,48,768]{2,1,0:T(8,128)(2,1)}), bf16[8,48,768]{2,1,0:T(8,128)(2,1)S(1)}, u32[]{:S(2)}, u32[]{:S(2)}) %all-to-all-start.1) | async-done | bytes 589856 | tf_op jit(solution)/shard_map/all_to_all | solution.py:272
  31.5 7.1 %all-to-all-start = ((bf16[8,2,16,2048]{3,2,1,0:T(8,128)(2,1)}), bf16[8,2,16,2048]{3,2,1,0:T(8,128)(2,1)S(1)}, u32[]{:S(2)}, u32[]{:S(2)}) async-start(bf16[8,2,16,2048]{3,2,1,0:T(8,128)(2,1)} %shard_map.119), calls=%async_computation | async-start | bytes 2097152 | tf_op jit(solution)/shard_map/all_to_all | solution.py:291
  38.6 2.4 %collective-permute-start.2 = (bf16[5,48,768]{2,1,0:T(8,128)(2,1)S(1)}, bf16[5,48,768]{2,1,0:T(8,128)(2,1)S(1)}, u32[]{:S(2)}, u32[]{:S(2)}) collective-permute-start(bf16[5,48,768]{2,1,0:T(8,128)(2,1)S(1)} %slice.9), channel_id=1, source_target_pairs={{0,48},{16,0},{32,16},{48,32},{64,112},{80,64},{96,80},{112,96},{1... | collective-permute-start | bytes 1105928 | tf_op jit(solution)/shard_map/ppermute | solution.py:279
  41.1 3.4 %collective-permute-start.1 = (bf16[3,48,768]{2,1,0:T(8,128)(2,1)S(1)}, bf16[3,48,768]{2,1,0:T(8,128)(2,1)S(1)}, u32[]{:S(2)}, u32[]{:S(2)}) collective-permute-start(bf16[3,48,768]{2,1,0:T(8,128)(2,1)S(1)} %slice.8), channel_id=1, source_target_pairs={{0,16},{16,32},{32,48},{48,0},{64,80},{80,96},{96,112},{112,64},{1... | collective-permute-start | bytes 663560 | tf_op jit(solution)/shard_map/ppermute | solution.py:279
  44.5 3.4 %collective-permute-start.3 = (bf16[5,48,768]{2,1,0:T(8,128)(2,1)S(1)}, bf16[5,48,768]{2,1,0:T(8,128)(2,1)S(1)}, u32[]{:S(2)}, u32[]{:S(2)}) collective-permute-start(bf16[5,48,768]{2,1,0:T(8,128)(2,1)S(1)} %slice.9), channel_id=1, source_target_pairs={{0,16},{16,32},{32,48},{48,0},{64,80},{80,96},{96,112},{112,64},{1... | collective-permute-start | bytes 1105928 | tf_op jit(solution)/shard_map/ppermute | solution.py:279
  47.9 2.4 %collective-permute-start.4 = (bf16[3,48,768]{2,1,0:T(8,128)(2,1)S(1)}, bf16[3,48,768]{2,1,0:T(8,128)(2,1)S(1)}, u32[]{:S(2)}, u32[]{:S(2)}) collective-permute-start(bf16[3,48,768]{2,1,0:T(8,128)(2,1)S(1)} %slice.8), channel_id=1, source_target_pairs={{0,48},{16,0},{32,16},{48,32},{64,112},{80,64},{96,80},{112,96},{1... | collective-permute-start | bytes 663560 | tf_op jit(solution)/shard_map/ppermute | solution.py:279
  50.4 1.7 %collective-permute-done.1 = bf16[3,48,768]{2,1,0:T(8,128)(2,1)S(1)} collective-permute-done((bf16[3,48,768]{2,1,0:T(8,128)(2,1)S(1)}, bf16[3,48,768]{2,1,0:T(8,128)(2,1)S(1)}, u32[]{:S(2)}, u32[]{:S(2)}) %collective-permute-start.1) | collective-permute-done | bytes 221216 | tf_op jit(solution)/shard_map/ppermute | solution.py:279
  52.1 2.7 %collective-permute-start.5 = (bf16[3,48,768]{2,1,0:T(8,128)(2,1)S(1)}, bf16[3,48,768]{2,1,0:T(8,128)(2,1)S(1)}, u32[]{:S(2)}, u32[]{:S(2)}) collective-permute-start(bf16[3,48,768]{2,1,0:T(8,128)(2,1)S(1)} %collective-permute-done.1), channel_id=1, source_target_pairs={{0,16},{16,32},{32,48},{48,0},{64,80},{80,96},{96,112},{112,64},{1... | collective-permute-start | bytes 663560 | tf_op jit(solution)/shard_map/ppermute | solution.py:279
  54.8 4.4 %collective-permute-start.6 = (bf16[5,48,768]{2,1,0:T(8,128)(2,1)S(1)}, bf16[5,48,768]{2,1,0:T(8,128)(2,1)S(1)}, u32[]{:S(2)}, u32[]{:S(2)}) collective-permute-start(bf16[5,48,768]{2,1,0:T(8,128)(2,1)S(1)} %collective-permute-done.2), channel_id=1, source_target_pairs={{0,48},{16,0},{32,16},{48,32},{64,112},{80,64},{96,80},{112,96},{1... | collective-permute-start | bytes 1105928 | tf_op jit(solution)/shard_map/ppermute | solution.py:279
  60.0 3.4 %collective-permute-done.5.refs_2_ = bf16[3,48,768]{2,1,0:T(8,128)(2,1)S(1)} collective-permute-done((bf16[3,48,768]{2,1,0:T(8,128)(2,1)S(1)}, bf16[3,48,768]{2,1,0:T(8,128)(2,1)S(1)}, u32[]{:S(2)}, u32[]{:S(2)}) %collective-permute-start.5) | collective-permute-done | bytes 221216 | tf_op jit(solution)/shard_map/ppermute | solution.py:279
  63.5 1.8 %collective-permute-done.6.refs_3_ = bf16[5,48,768]{2,1,0:T(8,128)(2,1)S(1)} collective-permute-done((bf16[5,48,768]{2,1,0:T(8,128)(2,1)S(1)}, bf16[5,48,768]{2,1,0:T(8,128)(2,1)S(1)}, u32[]{:S(2)}, u32[]{:S(2)}) %collective-permute-start.6) | collective-permute-done | bytes 368672 | tf_op jit(solution)/shard_map/ppermute | solution.py:279
  65.2 2.3 %all-to-all-done = bf16[8,2,16,2048]{3,2,1,0:T(8,128)(2,1)S(1)} async-done(((bf16[8,2,16,2048]{3,2,1,0:T(8,128)(2,1)}), bf16[8,2,16,2048]{3,2,1,0:T(8,128)(2,1)S(1)}, u32[]{:S(2)}, u32[]{:S(2)}) %all-to-all-start) | async-done | bytes 1048608 | tf_op jit(solution)/shard_map/all_to_all | solution.py:291
  67.6 5.2 %shard_map.121 = (bf16[256,2048]{1,0:T(8,128)(2,1)}, bf16[8,48,768]{2,1,0:T(8,128)(2,1)S(1)}, bf16[4,48,768]{2,1,0:T(8,128)(2,1)S(1)}, bf16[4,48,768]{2,1,0:T(8,...) custom-call(bf16[256,2048]{1,0:T(8,128)(2,1)S(1)} %bitcast.13, ...), custom_call_target="tpu_custom_call" | custom-call | flops 1811939328 | bytes 8388608 | tf_op jit(solution)/shard_map/pallas_call | solution.py:320
  72.8 4.6 %all-to-all-start.2 = ((bf16[8,2,16,2048]{3,2,1,0:T(8,128)(2,1)}), bf16[8,2,16,2048]{3,2,1,0:T(8,128)(2,1)S(1)}, u32[]{:S(2)}, u32[]{:S(2)}) async-start(bf16[8,2,16,2048]{3,2,1,0:T(8,128)(2,1)} %bitcast.8), calls=%async_computation.2 | async-start | bytes 2097152 | tf_op jit(solution)/shard_map/all_to_all | solution.py:291
  77.4 4.2 %collective-permute-start.7 = (bf16[4,48,768]{2,1,0:T(8,128)(2,1)}, bf16[4,48,768]{2,1,0:T(8,128)(2,1)S(1)}, u32[]{:S(2)}, u32[]{:S(2)}) collective-permute-start(bf16[4,48,768]{2,1,0:T(8,128)(2,1)} %get-tuple-element.30), channel_id=1, source_target_pairs={{0,16},{16,32},{32,48},{48,0},{64,80},{80,96},{96,112},{112,64},{1... | collective-permute-start | bytes 884744 | tf_op jit(solution)/shard_map/ppermute | solution.py:279
  81.6 2.1 %collective-permute-start.8 = (bf16[4,48,768]{2,1,0:T(8,128)(2,1)}, bf16[4,48,768]{2,1,0:T(8,128)(2,1)S(1)}, u32[]{:S(2)}, u32[]{:S(2)}) collective-permute-start(bf16[4,48,768]{2,1,0:T(8,128)(2,1)} %get-tuple-element.31), channel_id=1, source_target_pairs={{0,48},{16,0},{32,16},{48,32},{64,112},{80,64},{96,80},{112,96},{1... | collective-permute-start | bytes 884744 | tf_op jit(solution)/shard_map/ppermute | solution.py:279
  83.7 5.0 %collective-permute-start.10 = (bf16[4,48,768]{2,1,0:T(8,128)(2,1)S(1)}, bf16[4,48,768]{2,1,0:T(8,128)(2,1)S(1)}, u32[]{:S(2)}, u32[]{:S(2)}) collective-permute-start(bf16[4,48,768]{2,1,0:T(8,128)(2,1)S(1)} %get-tuple-element.33), channel_id=1, source_target_pairs={{0,16},{16,32},{32,48},{48,0},{64,80},{80,96},{96,112},{112,64},{1... | collective-permute-start | bytes 884744 | tf_op jit(solution)/shard_map/ppermute | solution.py:279
  88.7 2.5 %collective-permute-start.11 = (bf16[4,48,768]{2,1,0:T(8,128)(2,1)S(1)}, bf16[4,48,768]{2,1,0:T(8,128)(2,1)S(1)}, u32[]{:S(2)}, u32[]{:S(2)}) collective-permute-start(bf16[4,48,768]{2,1,0:T(8,128)(2,1)S(1)} %get-tuple-element.34), channel_id=1, source_target_pairs={{0,48},{16,0},{32,16},{48,32},{64,112},{80,64},{96,80},{112,96},{1... | collective-permute-start | bytes 884744 | tf_op jit(solution)/shard_map/ppermute | solution.py:279
  91.2 2.8 %collective-permute-done.8.high_ref = bf16[4,48,768]{2,1,0:T(8,128)(2,1)S(1)} collective-permute-done((bf16[4,48,768]{2,1,0:T(8,128)(2,1)}, bf16[4,48,768]{2,1,0:T(8,128)(2,1)S(1)}, u32[]{:S(2)}, u32[]{:S(2)}) %collective-permute-start.8) | collective-permute-done | bytes 294944 | tf_op jit(solution)/shard_map/ppermute | solution.py:279
  94.2 4.6 %collective-permute-start.9 = (bf16[4,48,768]{2,1,0:T(8,128)(2,1)S(1)}, bf16[4,48,768]{2,1,0:T(8,128)(2,1)S(1)}, u32[]{:S(2)}, u32[]{:S(2)}) collective-permute-start(bf16[4,48,768]{2,1,0:T(8,128)(2,1)S(1)} %get-tuple-element.32), channel_id=1, source_target_pairs={{0,16},{16,32},{32,48},{48,0},{64,80},{80,96},{96,112},{112,64},{1... | collective-permute-start | bytes 884744 | tf_op jit(solution)/shard_map/ppermute | solution.py:279
  98.8 1.9 %collective-permute-start.12 = (bf16[4,48,768]{2,1,0:T(8,128)(2,1)S(1)}, bf16[4,48,768]{2,1,0:T(8,128)(2,1)S(1)}, u32[]{:S(2)}, u32[]{:S(2)}) collective-permute-start(bf16[4,48,768]{2,1,0:T(8,128)(2,1)S(1)} %get-tuple-element.35), channel_id=1, source_target_pairs={{0,48},{16,0},{32,16},{48,32},{64,112},{80,64},{96,80},{112,96},{1... | collective-permute-start | bytes 884744 | tf_op jit(solution)/shard_map/ppermute | solution.py:279
  100.8 2.3 %collective-permute-done.9.left_lo = bf16[4,48,768]{2,1,0:T(8,128)(2,1)S(1)} collective-permute-done((bf16[4,48,768]{2,1,0:T(8,128)(2,1)S(1)}, bf16[4,48,768]{2,1,0:T(8,128)(2,1)S(1)}, u32[]{:S(2)}, u32[]{:S(2)}) %collective-permute-start.9) | collective-permute-done | bytes 294944 | tf_op jit(solution)/shard_map/ppermute | solution.py:279
  103.1 4.4 %collective-permute-done.12.right_hi = bf16[4,48,768]{2,1,0:T(8,128)(2,1)S(1)} collective-permute-done((bf16[4,48,768]{2,1,0:T(8,128)(2,1)S(1)}, bf16[4,48,768]{2,1,0:T(8,128)(2,1)S(1)}, u32[]{:S(2)}, u32[]{:S(2)}) %collective-permute-start.12) | collective-permute-done | bytes 294944 | tf_op jit(solution)/shard_map/ppermute | solution.py:279
  108.5 3.7 %all-to-all-start.3 = ((bf16[8,48,768]{2,1,0:T(8,128)(2,1)}), bf16[8,48,768]{2,1,0:T(8,128)(2,1)S(1)}, u32[]{:S(2)}, u32[]{:S(2)}) async-start(bf16[8,48,768]{2,1,0:T(8,128)(2,1)} %shard_map.123.after_ref), calls=%async_computation.3 | async-start | bytes 1179648 | tf_op jit(solution)/shard_map/all_to_all | solution.py:272
  112.2 1.9 %collective-permute-start.13 = (bf16[8,16,2048]{2,1,0:T(8,128)(2,1)S(1)}, bf16[8,16,2048]{2,1,0:T(8,128)(2,1)S(1)}, u32[]{:S(2)}, u32[]{:S(2)}) collective-permute-start(bf16[8,16,2048]{2,1,0:T(8,128)(2,1)S(1)} %shard_map.124), channel_id=1, source_target_pairs={{0,1},{1,0},{2,3},{3,2},{4,5},{5,4},{6,7},{7,6},{8,9},{9,8},{10,11... | collective-permute-start | bytes 1572872 | tf_op jit(solution)/shard_map/ppermute | solution.py:287
  114.2 1.9 %collective-permute-done.13.got_ref = bf16[8,16,2048]{2,1,0:T(8,128)(2,1)S(1)} collective-permute-done((bf16[8,16,2048]{2,1,0:T(8,128)(2,1)S(1)}, bf16[8,16,2048]{2,1,0:T(8,128)(2,1)S(1)}, u32[]{:S(2)}, u32[]{:S(2)}) %collective-permute-start.13) | collective-permute-done | bytes 524320 | tf_op jit(solution)/shard_map/ppermute | solution.py:287
  117.5 12.0 %all-to-all-done.3.parts_ref = bf16[8,48,768]{2,1,0:T(8,128)(2,1)S(1)} async-done(((bf16[8,48,768]{2,1,0:T(8,128)(2,1)}), bf16[8,48,768]{2,1,0:T(8,128)(2,1)S(1)}, u32[]{:S(2)}, u32[]{:S(2)}) %all-to-all-start.3) | async-done | bytes 589856 | tf_op jit(solution)/shard_map/all_to_all | solution.py:272
  (30 shorter events, 6.3 us)
Async XLA Ops:
  2.3 29.2 %all-to-all-start.1 = ((bf16[8,48,768]{2,1,0:T(8,128)(2,1)}), bf16[8,48,768]{2,1,0:T(8,128)(2,1)S(1)}, u32[]{:S(2)}, u32[]{:S(2)}) async-start(bf16[8,48,768]{2,1,0:T(8,128)(2,1)} %shard_map.120), calls=%async_computation.1 | async-start | bytes 1179648 | tf_op jit(solution)/shard_map/all_to_all | solution.py:272
  15.2 4.0 %collective-permute-start = (bf16[128,2048]{1,0:T(8,128)(2,1)}, bf16[128,2048]{1,0:T(8,128)(2,1)S(1)}, u32[]{:S(2)}, u32[]{:S(2)}) collective-permute-start(bf16[128,2048]{1,0:T(8,128)(2,1)} %get-tuple-element.25), channel_id=1, source_target_pairs={{0,1},{1,0},{2,3},{3,2},{4,5},{5,4},{6,7},{7,6},{8,9},{9,8},{10,11... | collective-permute-start | bytes 1572872 | tf_op jit(solution)/shard_map/ppermute | solution.py:287
  19.2 1.0 copy-start.1
  31.5 36.1 %all-to-all-start = ((bf16[8,2,16,2048]{3,2,1,0:T(8,128)(2,1)}), bf16[8,2,16,2048]{3,2,1,0:T(8,128)(2,1)S(1)}, u32[]{:S(2)}, u32[]{:S(2)}) async-start(bf16[8,2,16,2048]{3,2,1,0:T(8,128)(2,1)} %shard_map.119), calls=%async_computation | async-start | bytes 2097152 | tf_op jit(solution)/shard_map/all_to_all | solution.py:291
  38.6 16.1 %collective-permute-start.2 = (bf16[5,48,768]{2,1,0:T(8,128)(2,1)S(1)}, bf16[5,48,768]{2,1,0:T(8,128)(2,1)S(1)}, u32[]{:S(2)}, u32[]{:S(2)}) collective-permute-start(bf16[5,48,768]{2,1,0:T(8,128)(2,1)S(1)} %slice.9), channel_id=1, source_target_pairs={{0,48},{16,0},{32,16},{48,32},{64,112},{80,64},{96,80},{112,96},{1... | collective-permute-start | bytes 1105928 | tf_op jit(solution)/shard_map/ppermute | solution.py:279
  41.1 11.0 %collective-permute-start.1 = (bf16[3,48,768]{2,1,0:T(8,128)(2,1)S(1)}, bf16[3,48,768]{2,1,0:T(8,128)(2,1)S(1)}, u32[]{:S(2)}, u32[]{:S(2)}) collective-permute-start(bf16[3,48,768]{2,1,0:T(8,128)(2,1)S(1)} %slice.8), channel_id=1, source_target_pairs={{0,16},{16,32},{32,48},{48,0},{64,80},{80,96},{96,112},{112,64},{1... | collective-permute-start | bytes 663560 | tf_op jit(solution)/shard_map/ppermute | solution.py:279
  44.5 15.5 %collective-permute-start.3 = (bf16[5,48,768]{2,1,0:T(8,128)(2,1)S(1)}, bf16[5,48,768]{2,1,0:T(8,128)(2,1)S(1)}, u32[]{:S(2)}, u32[]{:S(2)}) collective-permute-start(bf16[5,48,768]{2,1,0:T(8,128)(2,1)S(1)} %slice.9), channel_id=1, source_target_pairs={{0,16},{16,32},{32,48},{48,0},{64,80},{80,96},{96,112},{112,64},{1... | collective-permute-start | bytes 1105928 | tf_op jit(solution)/shard_map/ppermute | solution.py:279
  47.9 12.1 %collective-permute-start.4 = (bf16[3,48,768]{2,1,0:T(8,128)(2,1)S(1)}, bf16[3,48,768]{2,1,0:T(8,128)(2,1)S(1)}, u32[]{:S(2)}, u32[]{:S(2)}) collective-permute-start(bf16[3,48,768]{2,1,0:T(8,128)(2,1)S(1)} %slice.8), channel_id=1, source_target_pairs={{0,48},{16,0},{32,16},{48,32},{64,112},{80,64},{96,80},{112,96},{1... | collective-permute-start | bytes 663560 | tf_op jit(solution)/shard_map/ppermute | solution.py:279
  52.1 11.4 %collective-permute-start.5 = (bf16[3,48,768]{2,1,0:T(8,128)(2,1)S(1)}, bf16[3,48,768]{2,1,0:T(8,128)(2,1)S(1)}, u32[]{:S(2)}, u32[]{:S(2)}) collective-permute-start(bf16[3,48,768]{2,1,0:T(8,128)(2,1)S(1)} %collective-permute-done.1), channel_id=1, source_target_pairs={{0,16},{16,32},{32,48},{48,0},{64,80},{80,96},{96,112},{112,64},{1... | collective-permute-start | bytes 663560 | tf_op jit(solution)/shard_map/ppermute | solution.py:279
  54.8 10.5 %collective-permute-start.6 = (bf16[5,48,768]{2,1,0:T(8,128)(2,1)S(1)}, bf16[5,48,768]{2,1,0:T(8,128)(2,1)S(1)}, u32[]{:S(2)}, u32[]{:S(2)}) collective-permute-start(bf16[5,48,768]{2,1,0:T(8,128)(2,1)S(1)} %collective-permute-done.2), channel_id=1, source_target_pairs={{0,48},{16,0},{32,16},{48,32},{64,112},{80,64},{96,80},{112,96},{1... | collective-permute-start | bytes 1105928 | tf_op jit(solution)/shard_map/ppermute | solution.py:279
  60.0 3.4 %copy-start.4 = (bf16[24,48,768]{2,1,0:T(8,128)(2,1)}, bf16[24,48,768]{2,1,0:T(8,128)(2,1)S(1)}, u32[]{:S(2)}) copy-start(bf16[24,48,768]{2,1,0:T(8,128)(2,1)S(1)} %constant_dynamic-update-slice_fusion.refs_1_) | copy-start | bytes 5308420
  72.8 34.7 %all-to-all-start.2 = ((bf16[8,2,16,2048]{3,2,1,0:T(8,128)(2,1)}), bf16[8,2,16,2048]{3,2,1,0:T(8,128)(2,1)S(1)}, u32[]{:S(2)}, u32[]{:S(2)}) async-start(bf16[8,2,16,2048]{3,2,1,0:T(8,128)(2,1)} %bitcast.8), calls=%async_computation.2 | async-start | bytes 2097152 | tf_op jit(solution)/shard_map/all_to_all | solution.py:291
  77.4 13.8 %collective-permute-start.7 = (bf16[4,48,768]{2,1,0:T(8,128)(2,1)}, bf16[4,48,768]{2,1,0:T(8,128)(2,1)S(1)}, u32[]{:S(2)}, u32[]{:S(2)}) collective-permute-start(bf16[4,48,768]{2,1,0:T(8,128)(2,1)} %get-tuple-element.30), channel_id=1, source_target_pairs={{0,16},{16,32},{32,48},{48,0},{64,80},{80,96},{96,112},{112,64},{1... | collective-permute-start | bytes 884744 | tf_op jit(solution)/shard_map/ppermute | solution.py:279
  81.6 12.4 %collective-permute-start.8 = (bf16[4,48,768]{2,1,0:T(8,128)(2,1)}, bf16[4,48,768]{2,1,0:T(8,128)(2,1)S(1)}, u32[]{:S(2)}, u32[]{:S(2)}) collective-permute-start(bf16[4,48,768]{2,1,0:T(8,128)(2,1)} %get-tuple-element.31), channel_id=1, source_target_pairs={{0,48},{16,0},{32,16},{48,32},{64,112},{80,64},{96,80},{112,96},{1... | collective-permute-start | bytes 884744 | tf_op jit(solution)/shard_map/ppermute | solution.py:279
  83.7 17.1 %collective-permute-start.10 = (bf16[4,48,768]{2,1,0:T(8,128)(2,1)S(1)}, bf16[4,48,768]{2,1,0:T(8,128)(2,1)S(1)}, u32[]{:S(2)}, u32[]{:S(2)}) collective-permute-start(bf16[4,48,768]{2,1,0:T(8,128)(2,1)S(1)} %get-tuple-element.33), channel_id=1, source_target_pairs={{0,16},{16,32},{32,48},{48,0},{64,80},{80,96},{96,112},{112,64},{1... | collective-permute-start | bytes 884744 | tf_op jit(solution)/shard_map/ppermute | solution.py:279
  88.7 12.1 %collective-permute-start.11 = (bf16[4,48,768]{2,1,0:T(8,128)(2,1)S(1)}, bf16[4,48,768]{2,1,0:T(8,128)(2,1)S(1)}, u32[]{:S(2)}, u32[]{:S(2)}) collective-permute-start(bf16[4,48,768]{2,1,0:T(8,128)(2,1)S(1)} %get-tuple-element.34), channel_id=1, source_target_pairs={{0,48},{16,0},{32,16},{48,32},{64,112},{80,64},{96,80},{112,96},{1... | collective-permute-start | bytes 884744 | tf_op jit(solution)/shard_map/ppermute | solution.py:279
  94.2 8.9 %collective-permute-start.9 = (bf16[4,48,768]{2,1,0:T(8,128)(2,1)S(1)}, bf16[4,48,768]{2,1,0:T(8,128)(2,1)S(1)}, u32[]{:S(2)}, u32[]{:S(2)}) collective-permute-start(bf16[4,48,768]{2,1,0:T(8,128)(2,1)S(1)} %get-tuple-element.32), channel_id=1, source_target_pairs={{0,16},{16,32},{32,48},{48,0},{64,80},{80,96},{96,112},{112,64},{1... | collective-permute-start | bytes 884744 | tf_op jit(solution)/shard_map/ppermute | solution.py:279
  98.8 8.6 %collective-permute-start.12 = (bf16[4,48,768]{2,1,0:T(8,128)(2,1)S(1)}, bf16[4,48,768]{2,1,0:T(8,128)(2,1)S(1)}, u32[]{:S(2)}, u32[]{:S(2)}) collective-permute-start(bf16[4,48,768]{2,1,0:T(8,128)(2,1)S(1)} %get-tuple-element.35), channel_id=1, source_target_pairs={{0,48},{16,0},{32,16},{48,32},{64,112},{80,64},{96,80},{112,96},{1... | collective-permute-start | bytes 884744 | tf_op jit(solution)/shard_map/ppermute | solution.py:279
  108.5 7.6 %copy-start = (bf16[128,1024]{1,0:T(8,128)(2,1)S(1)}, bf16[128,1024]{1,0:T(8,128)(2,1)}, u32[]{:S(2)}) copy-start(bf16[128,1024]{1,0:T(8,128)(2,1)} %upstream_ref.3) | copy-start | bytes 786436
  108.5 7.6 %copy-start.2 = (s32[128,8]{0,1:T(8,128)S(1)}, s32[128,8]{0,1:T(8,128)}, u32[]{:S(2)}) copy-start(s32[128,8]{0,1:T(8,128)} %param.8) | copy-start | bytes 12292
  108.5 7.6 %copy-start.3 = (f32[128,8]{0,1:T(8,128)S(1)}, f32[128,8]{0,1:T(8,128)}, u32[]{:S(2)}) copy-start(f32[128,8]{0,1:T(8,128)} %param.9) | copy-start | bytes 12292
  108.5 20.9 %all-to-all-start.3 = ((bf16[8,48,768]{2,1,0:T(8,128)(2,1)}), bf16[8,48,768]{2,1,0:T(8,128)(2,1)S(1)}, u32[]{:S(2)}, u32[]{:S(2)}) async-start(bf16[8,48,768]{2,1,0:T(8,128)(2,1)} %shard_map.123.after_ref), calls=%async_computation.3 | async-start | bytes 1179648 | tf_op jit(solution)/shard_map/all_to_all | solution.py:272
  112.2 3.8 %collective-permute-start.13 = (bf16[8,16,2048]{2,1,0:T(8,128)(2,1)S(1)}, bf16[8,16,2048]{2,1,0:T(8,128)(2,1)S(1)}, u32[]{:S(2)}, u32[]{:S(2)}) collective-permute-start(bf16[8,16,2048]{2,1,0:T(8,128)(2,1)S(1)} %shard_map.124), channel_id=1, source_target_pairs={{0,1},{1,0},{2,3},{3,2},{4,5},{5,4},{6,7},{7,6},{8,9},{9,8},{10,11... | collective-permute-start | bytes 1572872 | tf_op jit(solution)/shard_map/ppermute | solution.py:287

commit v6 on v5

--- a/solution.py
+++ b/solution.py
@@ -203,13 +203,17 @@
     to_left_ref[...] = (left_ref[...].astype(F32) + high_ref[...].astype(F32)).astype(BF)
 
 
-def sum_x_kernel(own_ref, left_lo, left_hi, right_lo, right_hi, after_ref, out_ref):
+def sum_x_kernel(own_ref, left_lo, left_hi, right_lo, right_hi, after_ref, out_ref, total, sems):
     del after_ref
-    h = NZ // 2
-    low = left_lo[...].astype(F32) + right_lo[...].astype(F32)
-    out_ref[:h] = (own_ref[:h].astype(F32) + low).astype(BF)
-    high = left_hi[...].astype(F32) + right_hi[...].astype(F32)
-    out_ref[h:] = (own_ref[h:].astype(F32) + high).astype(BF)
+    half, copies = NZ // 2, []
+    for z in range(NZ):
+        left, right = (left_lo, right_lo) if z < half else (left_hi, right_hi)
+        met = left[z % half].astype(F32) + right[z % half].astype(F32)
+        total[z] = (own_ref[z].astype(F32) + met).astype(BF)
+        copies.append(pltpu.make_async_copy(total.at[z], out_ref.at[z], sems.at[z]))
+        copies[-1].start()
+    for copy in copies:
+        copy.wait()
 
 
 def sum_z_kernel(parts_ref, gate_ref, up_ref, down_ref):
@@ -345,7 +349,14 @@
         q_right_lo, q_left_hi, add_lo, add_hi
     )
     from_left_lo, from_right_hi = shift_x(to_right, 1), shift_x(to_left, NX - 1)
-    total = call(sum_x_kernel, [whole], moved=3 * MIB, spaces=(None,) * 5 + (pl.ANY,))(
+    total = call(
+        sum_x_kernel,
+        [whole],
+        scratch=[pltpu.VMEM(whole[0], BF), pltpu.SemaphoreType.DMA((NZ,))],
+        moved=3 * MIB,
+        spaces=(None,) * 5 + (pl.ANY,),
+        out_spaces=(pl.ANY,),
+    )(
         q_own, from_left_lo, from_left_hi, from_right_lo, from_right_hi, home
     )
     got = swap_core(

time: 131 us -> 131 us (level)
  no operation moved by 1% of the time
where the time goes in v6:
time: 131 us; the launch traced here: 130 us
  starting transfers between devices  68.7 us (52%)
  waiting for transfers between devices  45.6 us (35%)
  Pallas kernels  13.7 us (10%)
    ppermute x12, starting transfers between devices, shift_x(): return lax.ppermute(v, 'dp', pairs)  39.1 us
    all_to_all x2, waiting for transfers between devices, swap_z(): lax.all_to_all(v, 'dp', split_axis=0, concat_axis=0, tiled=True, axis_ind...  22.2 us
    ppermute x12, waiting for transfers between devices, shift_x(): return lax.ppermute(v, 'dp', pairs)  17.1 us
    all_to_all x2, starting transfers between devices, swap_z(): lax.all_to_all(v, 'dp', split_axis=0, concat_axis=0, tiled=True, axis_ind...  14 us
    all_to_all x2, starting transfers between devices, exchange(): lax.all_to_all(v, 'expert', split_axis=0, concat_axis=0, tiled=True, axis...  11.7 us
    pallas_call x1, Pallas kernels, on_device(): call(expert_kernel, [((ROWS, 2 * D), BF), whole] + [part] * 6, scratch=[t...  5.19 us
    ppermute x2, waiting for transfers between devices, swap_core(): return lax.ppermute(v, 'expert', [(i, i ^ 1) for i in range(FLIGHT)])  3.96 us
    ppermute x2, starting transfers between devices, swap_core(): return lax.ppermute(v, 'expert', [(i, i ^ 1) for i in range(FLIGHT)])  3.83 us
  transfers between devices with their start and end apart: 18, of which 12 were waited for; matrix products, arithmetic and copies ran while one was open for 0% of the time, Pallas kernels for 4%

profile of v6, /device:TPU:2, one launch (start us, length us, event | category | flops | bytes accessed | tf_op | source)
XLA Modules:
  0.0 130.1 jit_solution(2140147490728501916)
XLA Ops:
  0.6 1.6 %shard_map.120 = bf16[8,48,768]{2,1,0:T(8,128)(2,1)} custom-call(bf16[32,384]{1,0:T(8,128)(2,1)} %bitcast.21, bf16[32,384]{1,0:T(8,128)(2,1)} %bitcast.22, bf16[12,1024]{1,0:T(8,128)(2,1)} %bitcast.20), custom_call_target="tpu_custom_call" | custom-call | bytes 1048576 | tf_op jit(solution)/shard_map/pallas_call | solution.py:302
  2.3 10.3 %all-to-all-start.1 = ((bf16[8,48,768]{2,1,0:T(8,128)(2,1)}), bf16[8,48,768]{2,1,0:T(8,128)(2,1)S(1)}, u32[]{:S(2)}, u32[]{:S(2)}) async-start(bf16[8,48,768]{2,1,0:T(8,128)(2,1)} %shard_map.120), calls=%async_computation.1 | async-start | bytes 1179648 | tf_op jit(solution)/shard_map/all_to_all | solution.py:276
  12.6 2.6 %shard_map.118 = (bf16[128,2048]{1,0:T(8,128)(2,1)}, bf16[128,2048]{1,0:T(8,128)(2,1)}) custom-call(s32[8,128]{1,0:T(8,128)} %bitcast.16, f32[8,128]{1,0:T(8,128)} %bitcast.18, bf16[128,1024]{1,0:T(8,128)(2,1)} %tokens_ref.1, bf16[128,1024]{1,0:T(8,128)(2,1)} %upstream_ref.3), custom_call_target="tpu_custom_call" | custom-call | flops 134217728 | bytes 1048576 | tf_op jit(solution)/shard_map/pallas_call | solution.py:304
  15.2 1.9 %collective-permute-start = (bf16[128,2048]{1,0:T(8,128)(2,1)}, bf16[128,2048]{1,0:T(8,128)(2,1)S(1)}, u32[]{:S(2)}, u32[]{:S(2)}) collective-permute-start(bf16[128,2048]{1,0:T(8,128)(2,1)} %get-tuple-element.25), channel_id=1, source_target_pairs={{0,1},{1,0},{2,3},{3,2},{4,5},{5,4},{6,7},{7,6},{8,9},{9,8},{10,11... | collective-permute-start | bytes 1572872 | tf_op jit(solution)/shard_map/ppermute | solution.py:291
  17.1 2.1 %collective-permute-done = bf16[128,2048]{1,0:T(8,128)(2,1)S(1)} collective-permute-done((bf16[128,2048]{1,0:T(8,128)(2,1)}, bf16[128,2048]{1,0:T(8,128)(2,1)S(1)}, u32[]{:S(2)}, u32[]{:S(2)}) %collective-permute-start) | collective-permute-done | bytes 524320 | tf_op jit(solution)/shard_map/ppermute | solution.py:291
  21.3 10.2 %all-to-all-done.1 = bf16[8,48,768]{2,1,0:T(8,128)(2,1)S(1)} async-done(((bf16[8,48,768]{2,1,0:T(8,128)(2,1)}), bf16[8,48,768]{2,1,0:T(8,128)(2,1)S(1)}, u32[]{:S(2)}, u32[]{:S(2)}) %all-to-all-start.1) | async-done | bytes 589856 | tf_op jit(solution)/shard_map/all_to_all | solution.py:276
  31.5 7.1 %all-to-all-start = ((bf16[8,2,16,2048]{3,2,1,0:T(8,128)(2,1)}), bf16[8,2,16,2048]{3,2,1,0:T(8,128)(2,1)S(1)}, u32[]{:S(2)}, u32[]{:S(2)}) async-start(bf16[8,2,16,2048]{3,2,1,0:T(8,128)(2,1)} %shard_map.119), calls=%async_computation | async-start | bytes 2097152 | tf_op jit(solution)/shard_map/all_to_all | solution.py:295
  38.6 2.4 %collective-permute-start.2 = (bf16[5,48,768]{2,1,0:T(8,128)(2,1)S(1)}, bf16[5,48,768]{2,1,0:T(8,128)(2,1)S(1)}, u32[]{:S(2)}, u32[]{:S(2)}) collective-permute-start(bf16[5,48,768]{2,1,0:T(8,128)(2,1)S(1)} %slice.9), channel_id=1, source_target_pairs={{0,48},{16,0},{32,16},{48,32},{64,112},{80,64},{96,80},{112,96},{1... | collective-permute-start | bytes 1105928 | tf_op jit(solution)/shard_map/ppermute | solution.py:283
  41.1 3.4 %collective-permute-start.1 = (bf16[3,48,768]{2,1,0:T(8,128)(2,1)S(1)}, bf16[3,48,768]{2,1,0:T(8,128)(2,1)S(1)}, u32[]{:S(2)}, u32[]{:S(2)}) collective-permute-start(bf16[3,48,768]{2,1,0:T(8,128)(2,1)S(1)} %slice.8), channel_id=1, source_target_pairs={{0,16},{16,32},{32,48},{48,0},{64,80},{80,96},{96,112},{112,64},{1... | collective-permute-start | bytes 663560 | tf_op jit(solution)/shard_map/ppermute | solution.py:283
  44.5 3.4 %collective-permute-start.3 = (bf16[5,48,768]{2,1,0:T(8,128)(2,1)S(1)}, bf16[5,48,768]{2,1,0:T(8,128)(2,1)S(1)}, u32[]{:S(2)}, u32[]{:S(2)}) collective-permute-start(bf16[5,48,768]{2,1,0:T(8,128)(2,1)S(1)} %slice.9), channel_id=1, source_target_pairs={{0,16},{16,32},{32,48},{48,0},{64,80},{80,96},{96,112},{112,64},{1... | collective-permute-start | bytes 1105928 | tf_op jit(solution)/shard_map/ppermute | solution.py:283
  47.9 2.4 %collective-permute-start.4 = (bf16[3,48,768]{2,1,0:T(8,128)(2,1)S(1)}, bf16[3,48,768]{2,1,0:T(8,128)(2,1)S(1)}, u32[]{:S(2)}, u32[]{:S(2)}) collective-permute-start(bf16[3,48,768]{2,1,0:T(8,128)(2,1)S(1)} %slice.8), channel_id=1, source_target_pairs={{0,48},{16,0},{32,16},{48,32},{64,112},{80,64},{96,80},{112,96},{1... | collective-permute-start | bytes 663560 | tf_op jit(solution)/shard_map/ppermute | solution.py:283
  50.4 1.7 %collective-permute-done.1 = bf16[3,48,768]{2,1,0:T(8,128)(2,1)S(1)} collective-permute-done((bf16[3,48,768]{2,1,0:T(8,128)(2,1)S(1)}, bf16[3,48,768]{2,1,0:T(8,128)(2,1)S(1)}, u32[]{:S(2)}, u32[]{:S(2)}) %collective-permute-start.1) | collective-permute-done | bytes 221216 | tf_op jit(solution)/shard_map/ppermute | solution.py:283
  52.1 2.7 %collective-permute-start.5 = (bf16[3,48,768]{2,1,0:T(8,128)(2,1)S(1)}, bf16[3,48,768]{2,1,0:T(8,128)(2,1)S(1)}, u32[]{:S(2)}, u32[]{:S(2)}) collective-permute-start(bf16[3,48,768]{2,1,0:T(8,128)(2,1)S(1)} %collective-permute-done.1), channel_id=1, source_target_pairs={{0,16},{16,32},{32,48},{48,0},{64,80},{80,96},{96,112},{112,64},{1... | collective-permute-start | bytes 663560 | tf_op jit(solution)/shard_map/ppermute | solution.py:283
  54.8 4.4 %collective-permute-start.6 = (bf16[5,48,768]{2,1,0:T(8,128)(2,1)S(1)}, bf16[5,48,768]{2,1,0:T(8,128)(2,1)S(1)}, u32[]{:S(2)}, u32[]{:S(2)}) collective-permute-start(bf16[5,48,768]{2,1,0:T(8,128)(2,1)S(1)} %collective-permute-done.2), channel_id=1, source_target_pairs={{0,48},{16,0},{32,16},{48,32},{64,112},{80,64},{96,80},{112,96},{1... | collective-permute-start | bytes 1105928 | tf_op jit(solution)/shard_map/ppermute | solution.py:283
  60.0 3.4 %collective-permute-done.5.refs_2_ = bf16[3,48,768]{2,1,0:T(8,128)(2,1)S(1)} collective-permute-done((bf16[3,48,768]{2,1,0:T(8,128)(2,1)S(1)}, bf16[3,48,768]{2,1,0:T(8,128)(2,1)S(1)}, u32[]{:S(2)}, u32[]{:S(2)}) %collective-permute-start.5) | collective-permute-done | bytes 221216 | tf_op jit(solution)/shard_map/ppermute | solution.py:283
  63.5 1.8 %collective-permute-done.6.refs_3_ = bf16[5,48,768]{2,1,0:T(8,128)(2,1)S(1)} collective-permute-done((bf16[5,48,768]{2,1,0:T(8,128)(2,1)S(1)}, bf16[5,48,768]{2,1,0:T(8,128)(2,1)S(1)}, u32[]{:S(2)}, u32[]{:S(2)}) %collective-permute-start.6) | collective-permute-done | bytes 368672 | tf_op jit(solution)/shard_map/ppermute | solution.py:283
  65.2 2.3 %all-to-all-done = bf16[8,2,16,2048]{3,2,1,0:T(8,128)(2,1)S(1)} async-done(((bf16[8,2,16,2048]{3,2,1,0:T(8,128)(2,1)}), bf16[8,2,16,2048]{3,2,1,0:T(8,128)(2,1)S(1)}, u32[]{:S(2)}, u32[]{:S(2)}) %all-to-all-start) | async-done | bytes 1048608 | tf_op jit(solution)/shard_map/all_to_all | solution.py:295
  67.6 5.2 %shard_map.121 = (bf16[256,2048]{1,0:T(8,128)(2,1)}, bf16[8,48,768]{2,1,0:T(8,128)(2,1)S(1)}, bf16[4,48,768]{2,1,0:T(8,128)(2,1)S(1)}, bf16[4,48,768]{2,1,0:T(8,...) custom-call(bf16[256,2048]{1,0:T(8,128)(2,1)S(1)} %bitcast.13, ...), custom_call_target="tpu_custom_call" | custom-call | flops 1811939328 | bytes 8388608 | tf_op jit(solution)/shard_map/pallas_call | solution.py:324
  72.8 4.6 %all-to-all-start.2 = ((bf16[8,2,16,2048]{3,2,1,0:T(8,128)(2,1)}), bf16[8,2,16,2048]{3,2,1,0:T(8,128)(2,1)S(1)}, u32[]{:S(2)}, u32[]{:S(2)}) async-start(bf16[8,2,16,2048]{3,2,1,0:T(8,128)(2,1)} %bitcast.8), calls=%async_computation.2 | async-start | bytes 2097152 | tf_op jit(solution)/shard_map/all_to_all | solution.py:295
  77.4 4.2 %collective-permute-start.7 = (bf16[4,48,768]{2,1,0:T(8,128)(2,1)}, bf16[4,48,768]{2,1,0:T(8,128)(2,1)S(1)}, u32[]{:S(2)}, u32[]{:S(2)}) collective-permute-start(bf16[4,48,768]{2,1,0:T(8,128)(2,1)} %get-tuple-element.30), channel_id=1, source_target_pairs={{0,16},{16,32},{32,48},{48,0},{64,80},{80,96},{96,112},{112,64},{1... | collective-permute-start | bytes 884744 | tf_op jit(solution)/shard_map/ppermute | solution.py:283
  81.6 2.1 %collective-permute-start.8 = (bf16[4,48,768]{2,1,0:T(8,128)(2,1)}, bf16[4,48,768]{2,1,0:T(8,128)(2,1)S(1)}, u32[]{:S(2)}, u32[]{:S(2)}) collective-permute-start(bf16[4,48,768]{2,1,0:T(8,128)(2,1)} %get-tuple-element.31), channel_id=1, source_target_pairs={{0,48},{16,0},{32,16},{48,32},{64,112},{80,64},{96,80},{112,96},{1... | collective-permute-start | bytes 884744 | tf_op jit(solution)/shard_map/ppermute | solution.py:283
  83.7 5.0 %collective-permute-start.10 = (bf16[4,48,768]{2,1,0:T(8,128)(2,1)S(1)}, bf16[4,48,768]{2,1,0:T(8,128)(2,1)S(1)}, u32[]{:S(2)}, u32[]{:S(2)}) collective-permute-start(bf16[4,48,768]{2,1,0:T(8,128)(2,1)S(1)} %get-tuple-element.33), channel_id=1, source_target_pairs={{0,16},{16,32},{32,48},{48,0},{64,80},{80,96},{96,112},{112,64},{1... | collective-permute-start | bytes 884744 | tf_op jit(solution)/shard_map/ppermute | solution.py:283
  88.7 2.5 %collective-permute-start.11 = (bf16[4,48,768]{2,1,0:T(8,128)(2,1)S(1)}, bf16[4,48,768]{2,1,0:T(8,128)(2,1)S(1)}, u32[]{:S(2)}, u32[]{:S(2)}) collective-permute-start(bf16[4,48,768]{2,1,0:T(8,128)(2,1)S(1)} %get-tuple-element.34), channel_id=1, source_target_pairs={{0,48},{16,0},{32,16},{48,32},{64,112},{80,64},{96,80},{112,96},{1... | collective-permute-start | bytes 884744 | tf_op jit(solution)/shard_map/ppermute | solution.py:283
  91.2 2.8 %collective-permute-done.8.high_ref = bf16[4,48,768]{2,1,0:T(8,128)(2,1)S(1)} collective-permute-done((bf16[4,48,768]{2,1,0:T(8,128)(2,1)}, bf16[4,48,768]{2,1,0:T(8,128)(2,1)S(1)}, u32[]{:S(2)}, u32[]{:S(2)}) %collective-permute-start.8) | collective-permute-done | bytes 294944 | tf_op jit(solution)/shard_map/ppermute | solution.py:283
  94.2 4.6 %collective-permute-start.9 = (bf16[4,48,768]{2,1,0:T(8,128)(2,1)S(1)}, bf16[4,48,768]{2,1,0:T(8,128)(2,1)S(1)}, u32[]{:S(2)}, u32[]{:S(2)}) collective-permute-start(bf16[4,48,768]{2,1,0:T(8,128)(2,1)S(1)} %get-tuple-element.32), channel_id=1, source_target_pairs={{0,16},{16,32},{32,48},{48,0},{64,80},{80,96},{96,112},{112,64},{1... | collective-permute-start | bytes 884744 | tf_op jit(solution)/shard_map/ppermute | solution.py:283
  98.8 1.9 %collective-permute-start.12 = (bf16[4,48,768]{2,1,0:T(8,128)(2,1)S(1)}, bf16[4,48,768]{2,1,0:T(8,128)(2,1)S(1)}, u32[]{:S(2)}, u32[]{:S(2)}) collective-permute-start(bf16[4,48,768]{2,1,0:T(8,128)(2,1)S(1)} %get-tuple-element.35), channel_id=1, source_target_pairs={{0,48},{16,0},{32,16},{48,32},{64,112},{80,64},{96,80},{112,96},{1... | collective-permute-start | bytes 884744 | tf_op jit(solution)/shard_map/ppermute | solution.py:283
  100.8 2.3 %collective-permute-done.9.left_lo = bf16[4,48,768]{2,1,0:T(8,128)(2,1)S(1)} collective-permute-done((bf16[4,48,768]{2,1,0:T(8,128)(2,1)S(1)}, bf16[4,48,768]{2,1,0:T(8,128)(2,1)S(1)}, u32[]{:S(2)}, u32[]{:S(2)}) %collective-permute-start.9) | collective-permute-done | bytes 294944 | tf_op jit(solution)/shard_map/ppermute | solution.py:283
  103.1 4.4 %collective-permute-done.12.right_hi = bf16[4,48,768]{2,1,0:T(8,128)(2,1)S(1)} collective-permute-done((bf16[4,48,768]{2,1,0:T(8,128)(2,1)S(1)}, bf16[4,48,768]{2,1,0:T(8,128)(2,1)S(1)}, u32[]{:S(2)}, u32[]{:S(2)}) %collective-permute-start.12) | collective-permute-done | bytes 294944 | tf_op jit(solution)/shard_map/ppermute | solution.py:283
  108.4 3.7 %all-to-all-start.3 = ((bf16[8,48,768]{2,1,0:T(8,128)(2,1)}), bf16[8,48,768]{2,1,0:T(8,128)(2,1)S(1)}, u32[]{:S(2)}, u32[]{:S(2)}) async-start(bf16[8,48,768]{2,1,0:T(8,128)(2,1)} %shard_map.123.after_ref), calls=%async_computation.3 | async-start | bytes 1179648 | tf_op jit(solution)/shard_map/all_to_all | solution.py:276
  112.2 1.9 %collective-permute-start.13 = (bf16[8,16,2048]{2,1,0:T(8,128)(2,1)S(1)}, bf16[8,16,2048]{2,1,0:T(8,128)(2,1)S(1)}, u32[]{:S(2)}, u32[]{:S(2)}) collective-permute-start(bf16[8,16,2048]{2,1,0:T(8,128)(2,1)S(1)} %shard_map.124), channel_id=1, source_target_pairs={{0,1},{1,0},{2,3},{3,2},{4,5},{5,4},{6,7},{7,6},{8,9},{9,8},{10,11... | collective-permute-start | bytes 1572872 | tf_op jit(solution)/shard_map/ppermute | solution.py:291
  114.1 1.9 %collective-permute-done.13.got_ref = bf16[8,16,2048]{2,1,0:T(8,128)(2,1)S(1)} collective-permute-done((bf16[8,16,2048]{2,1,0:T(8,128)(2,1)S(1)}, bf16[8,16,2048]{2,1,0:T(8,128)(2,1)S(1)}, u32[]{:S(2)}, u32[]{:S(2)}) %collective-permute-start.13) | collective-permute-done | bytes 524320 | tf_op jit(solution)/shard_map/ppermute | solution.py:291
  117.4 12.0 %all-to-all-done.3.parts_ref = bf16[8,48,768]{2,1,0:T(8,128)(2,1)S(1)} async-done(((bf16[8,48,768]{2,1,0:T(8,128)(2,1)}), bf16[8,48,768]{2,1,0:T(8,128)(2,1)S(1)}, u32[]{:S(2)}, u32[]{:S(2)}) %all-to-all-start.3) | async-done | bytes 589856 | tf_op jit(solution)/shard_map/all_to_all | solution.py:276
  (30 shorter events, 6.2 us)
Async XLA Ops:
  2.3 29.2 %all-to-all-start.1 = ((bf16[8,48,768]{2,1,0:T(8,128)(2,1)}), bf16[8,48,768]{2,1,0:T(8,128)(2,1)S(1)}, u32[]{:S(2)}, u32[]{:S(2)}) async-start(bf16[8,48,768]{2,1,0:T(8,128)(2,1)} %shard_map.120), calls=%async_computation.1 | async-start | bytes 1179648 | tf_op jit(solution)/shard_map/all_to_all | solution.py:276
  15.2 4.0 %collective-permute-start = (bf16[128,2048]{1,0:T(8,128)(2,1)}, bf16[128,2048]{1,0:T(8,128)(2,1)S(1)}, u32[]{:S(2)}, u32[]{:S(2)}) collective-permute-start(bf16[128,2048]{1,0:T(8,128)(2,1)} %get-tuple-element.25), channel_id=1, source_target_pairs={{0,1},{1,0},{2,3},{3,2},{4,5},{5,4},{6,7},{7,6},{8,9},{9,8},{10,11... | collective-permute-start | bytes 1572872 | tf_op jit(solution)/shard_map/ppermute | solution.py:291
  19.2 1.0 copy-start.1
  31.5 36.1 %all-to-all-start = ((bf16[8,2,16,2048]{3,2,1,0:T(8,128)(2,1)}), bf16[8,2,16,2048]{3,2,1,0:T(8,128)(2,1)S(1)}, u32[]{:S(2)}, u32[]{:S(2)}) async-start(bf16[8,2,16,2048]{3,2,1,0:T(8,128)(2,1)} %shard_map.119), calls=%async_computation | async-start | bytes 2097152 | tf_op jit(solution)/shard_map/all_to_all | solution.py:295
  38.6 16.1 %collective-permute-start.2 = (bf16[5,48,768]{2,1,0:T(8,128)(2,1)S(1)}, bf16[5,48,768]{2,1,0:T(8,128)(2,1)S(1)}, u32[]{:S(2)}, u32[]{:S(2)}) collective-permute-start(bf16[5,48,768]{2,1,0:T(8,128)(2,1)S(1)} %slice.9), channel_id=1, source_target_pairs={{0,48},{16,0},{32,16},{48,32},{64,112},{80,64},{96,80},{112,96},{1... | collective-permute-start | bytes 1105928 | tf_op jit(solution)/shard_map/ppermute | solution.py:283
  41.1 11.0 %collective-permute-start.1 = (bf16[3,48,768]{2,1,0:T(8,128)(2,1)S(1)}, bf16[3,48,768]{2,1,0:T(8,128)(2,1)S(1)}, u32[]{:S(2)}, u32[]{:S(2)}) collective-permute-start(bf16[3,48,768]{2,1,0:T(8,128)(2,1)S(1)} %slice.8), channel_id=1, source_target_pairs={{0,16},{16,32},{32,48},{48,0},{64,80},{80,96},{96,112},{112,64},{1... | collective-permute-start | bytes 663560 | tf_op jit(solution)/shard_map/ppermute | solution.py:283
  44.5 15.5 %collective-permute-start.3 = (bf16[5,48,768]{2,1,0:T(8,128)(2,1)S(1)}, bf16[5,48,768]{2,1,0:T(8,128)(2,1)S(1)}, u32[]{:S(2)}, u32[]{:S(2)}) collective-permute-start(bf16[5,48,768]{2,1,0:T(8,128)(2,1)S(1)} %slice.9), channel_id=1, source_target_pairs={{0,16},{16,32},{32,48},{48,0},{64,80},{80,96},{96,112},{112,64},{1... | collective-permute-start | bytes 1105928 | tf_op jit(solution)/shard_map/ppermute | solution.py:283
  47.9 12.1 %collective-permute-start.4 = (bf16[3,48,768]{2,1,0:T(8,128)(2,1)S(1)}, bf16[3,48,768]{2,1,0:T(8,128)(2,1)S(1)}, u32[]{:S(2)}, u32[]{:S(2)}) collective-permute-start(bf16[3,48,768]{2,1,0:T(8,128)(2,1)S(1)} %slice.8), channel_id=1, source_target_pairs={{0,48},{16,0},{32,16},{48,32},{64,112},{80,64},{96,80},{112,96},{1... | collective-permute-start | bytes 663560 | tf_op jit(solution)/shard_map/ppermute | solution.py:283
  52.1 11.4 %collective-permute-start.5 = (bf16[3,48,768]{2,1,0:T(8,128)(2,1)S(1)}, bf16[3,48,768]{2,1,0:T(8,128)(2,1)S(1)}, u32[]{:S(2)}, u32[]{:S(2)}) collective-permute-start(bf16[3,48,768]{2,1,0:T(8,128)(2,1)S(1)} %collective-permute-done.1), channel_id=1, source_target_pairs={{0,16},{16,32},{32,48},{48,0},{64,80},{80,96},{96,112},{112,64},{1... | collective-permute-start | bytes 663560 | tf_op jit(solution)/shard_map/ppermute | solution.py:283
  54.8 10.5 %collective-permute-start.6 = (bf16[5,48,768]{2,1,0:T(8,128)(2,1)S(1)}, bf16[5,48,768]{2,1,0:T(8,128)(2,1)S(1)}, u32[]{:S(2)}, u32[]{:S(2)}) collective-permute-start(bf16[5,48,768]{2,1,0:T(8,128)(2,1)S(1)} %collective-permute-done.2), channel_id=1, source_target_pairs={{0,48},{16,0},{32,16},{48,32},{64,112},{80,64},{96,80},{112,96},{1... | collective-permute-start | bytes 1105928 | tf_op jit(solution)/shard_map/ppermute | solution.py:283
  60.0 3.4 %copy-start.4 = (bf16[24,48,768]{2,1,0:T(8,128)(2,1)}, bf16[24,48,768]{2,1,0:T(8,128)(2,1)S(1)}, u32[]{:S(2)}) copy-start(bf16[24,48,768]{2,1,0:T(8,128)(2,1)S(1)} %constant_dynamic-update-slice_fusion.refs_1_) | copy-start | bytes 5308420
  72.8 34.7 %all-to-all-start.2 = ((bf16[8,2,16,2048]{3,2,1,0:T(8,128)(2,1)}), bf16[8,2,16,2048]{3,2,1,0:T(8,128)(2,1)S(1)}, u32[]{:S(2)}, u32[]{:S(2)}) async-start(bf16[8,2,16,2048]{3,2,1,0:T(8,128)(2,1)} %bitcast.8), calls=%async_computation.2 | async-start | bytes 2097152 | tf_op jit(solution)/shard_map/all_to_all | solution.py:295
  77.4 13.8 %collective-permute-start.7 = (bf16[4,48,768]{2,1,0:T(8,128)(2,1)}, bf16[4,48,768]{2,1,0:T(8,128)(2,1)S(1)}, u32[]{:S(2)}, u32[]{:S(2)}) collective-permute-start(bf16[4,48,768]{2,1,0:T(8,128)(2,1)} %get-tuple-element.30), channel_id=1, source_target_pairs={{0,16},{16,32},{32,48},{48,0},{64,80},{80,96},{96,112},{112,64},{1... | collective-permute-start | bytes 884744 | tf_op jit(solution)/shard_map/ppermute | solution.py:283
  81.6 12.4 %collective-permute-start.8 = (bf16[4,48,768]{2,1,0:T(8,128)(2,1)}, bf16[4,48,768]{2,1,0:T(8,128)(2,1)S(1)}, u32[]{:S(2)}, u32[]{:S(2)}) collective-permute-start(bf16[4,48,768]{2,1,0:T(8,128)(2,1)} %get-tuple-element.31), channel_id=1, source_target_pairs={{0,48},{16,0},{32,16},{48,32},{64,112},{80,64},{96,80},{112,96},{1... | collective-permute-start | bytes 884744 | tf_op jit(solution)/shard_map/ppermute | solution.py:283
  83.7 17.1 %collective-permute-start.10 = (bf16[4,48,768]{2,1,0:T(8,128)(2,1)S(1)}, bf16[4,48,768]{2,1,0:T(8,128)(2,1)S(1)}, u32[]{:S(2)}, u32[]{:S(2)}) collective-permute-start(bf16[4,48,768]{2,1,0:T(8,128)(2,1)S(1)} %get-tuple-element.33), channel_id=1, source_target_pairs={{0,16},{16,32},{32,48},{48,0},{64,80},{80,96},{96,112},{112,64},{1... | collective-permute-start | bytes 884744 | tf_op jit(solution)/shard_map/ppermute | solution.py:283
  88.7 12.1 %collective-permute-start.11 = (bf16[4,48,768]{2,1,0:T(8,128)(2,1)S(1)}, bf16[4,48,768]{2,1,0:T(8,128)(2,1)S(1)}, u32[]{:S(2)}, u32[]{:S(2)}) collective-permute-start(bf16[4,48,768]{2,1,0:T(8,128)(2,1)S(1)} %get-tuple-element.34), channel_id=1, source_target_pairs={{0,48},{16,0},{32,16},{48,32},{64,112},{80,64},{96,80},{112,96},{1... | collective-permute-start | bytes 884744 | tf_op jit(solution)/shard_map/ppermute | solution.py:283
  94.2 8.9 %collective-permute-start.9 = (bf16[4,48,768]{2,1,0:T(8,128)(2,1)S(1)}, bf16[4,48,768]{2,1,0:T(8,128)(2,1)S(1)}, u32[]{:S(2)}, u32[]{:S(2)}) collective-permute-start(bf16[4,48,768]{2,1,0:T(8,128)(2,1)S(1)} %get-tuple-element.32), channel_id=1, source_target_pairs={{0,16},{16,32},{32,48},{48,0},{64,80},{80,96},{96,112},{112,64},{1... | collective-permute-start | bytes 884744 | tf_op jit(solution)/shard_map/ppermute | solution.py:283
  98.8 8.6 %collective-permute-start.12 = (bf16[4,48,768]{2,1,0:T(8,128)(2,1)S(1)}, bf16[4,48,768]{2,1,0:T(8,128)(2,1)S(1)}, u32[]{:S(2)}, u32[]{:S(2)}) collective-permute-start(bf16[4,48,768]{2,1,0:T(8,128)(2,1)S(1)} %get-tuple-element.35), channel_id=1, source_target_pairs={{0,48},{16,0},{32,16},{48,32},{64,112},{80,64},{96,80},{112,96},{1... | collective-permute-start | bytes 884744 | tf_op jit(solution)/shard_map/ppermute | solution.py:283
  108.4 7.6 %copy-start = (bf16[128,1024]{1,0:T(8,128)(2,1)S(1)}, bf16[128,1024]{1,0:T(8,128)(2,1)}, u32[]{:S(2)}) copy-start(bf16[128,1024]{1,0:T(8,128)(2,1)} %upstream_ref.3) | copy-start | bytes 786436
  108.4 7.6 %copy-start.2 = (s32[128,8]{0,1:T(8,128)S(1)}, s32[128,8]{0,1:T(8,128)}, u32[]{:S(2)}) copy-start(s32[128,8]{0,1:T(8,128)} %param.8) | copy-start | bytes 12292
  108.4 7.6 %copy-start.3 = (f32[128,8]{0,1:T(8,128)S(1)}, f32[128,8]{0,1:T(8,128)}, u32[]{:S(2)}) copy-start(f32[128,8]{0,1:T(8,128)} %param.9) | copy-start | bytes 12292
  108.4 20.9 %all-to-all-start.3 = ((bf16[8,48,768]{2,1,0:T(8,128)(2,1)}), bf16[8,48,768]{2,1,0:T(8,128)(2,1)S(1)}, u32[]{:S(2)}, u32[]{:S(2)}) async-start(bf16[8,48,768]{2,1,0:T(8,128)(2,1)} %shard_map.123.after_ref), calls=%async_computation.3 | async-start | bytes 1179648 | tf_op jit(solution)/shard_map/all_to_all | solution.py:276
  112.2 3.8 %collective-permute-start.13 = (bf16[8,16,2048]{2,1,0:T(8,128)(2,1)S(1)}, bf16[8,16,2048]{2,1,0:T(8,128)(2,1)S(1)}, u32[]{:S(2)}, u32[]{:S(2)}) collective-permute-start(bf16[8,16,2048]{2,1,0:T(8,128)(2,1)S(1)} %shard_map.124), channel_id=1, source_target_pairs={{0,1},{1,0},{2,3},{3,2},{4,5},{5,4},{6,7},{7,6},{8,9},{9,8},{10,11... | collective-permute-start | bytes 1572872 | tf_op jit(solution)/shard_map/ppermute | solution.py:291
